TPU v7x, 1024 devices: a whole 4x4x32 slice. The times are simulated.
1024 devices in a mesh: node: 16 (over y_lo, x, core), expert: 64 (over y_hi, z).
Axes of the slice: x: 4, y: 4 (y_hi: 2, y_lo: 2; y = y_hi * 2 + y_lo), z: 32, core: 2. Of those that a mesh axis runs over, the one named last changes fastest.
Arguments:
- tokens: bfloat16 [4096, 4096], P(('node', 'expert')), may hold values from -6 to 6
- expert_ids: int32 [4096, 8], P(('node', 'expert')), may hold values from 0 to 127, as said below
- gate_units: int32 [4096, 8], P(('node', 'expert')), may hold values from 1 to 16
- slot_ids: int32 [4096, 8], P(('node', 'expert')), may hold values from 0 to 39, as said below
- grad_out: bfloat16 [4096, 4096], P(('node', 'expert')), may hold values from -6 to 6
- gate_weight: bfloat16 [64, 4096, 1536], P('expert', None, 'node'), may hold values from -0.09375 to 0.09375
- up_weight: bfloat16 [64, 4096, 1536], P('expert', None, 'node'), may hold values from -0.09375 to 0.09375
- down_weight: bfloat16 [64, 1536, 4096], P('expert', 'node'), may hold values from -0.21875 to 0.21875
Outputs:
- mixed: bfloat16 [4096, 4096], P(('node', 'expert'))
- grad_tokens: bfloat16 [4096, 4096], P(('node', 'expert'))
- grad_down: bfloat16 [64, 1536, 4096], P('expert', 'node')
Inputs may be any that keep to these rules, and one draw needn't show every extreme that they name: `expert_ids`: each token names 8 experts whose indices e // 2 differ; the tokens of one device name each such index at most 1 times; the 256 tokens of one node group name each index exactly 4 * 8 times, and one expert at most 20 times, a bound reached by some expert of each parity in every group. slot_ids[t, k] = (e % 2) * 20 + r with e = expert_ids[t, k] and r below 20; within one node group the choices of one expert have distinct r from 0 upward.
All inputs are finite; a program needn't handle non-finite values.
Results may differ from a plain program's by a relative error of at most 0.012.
Values may be sent and summed in bfloat16 or wider, within the bound.
No kernel may reach another device: no remote copies, remote signals or barrier semaphores. Data moves between devices by JAX's collectives and lax.ppermute only.
A program may use at most 64 MiB of HBM per device.

v0:
```python
import jax
import jax.numpy as jnp
from jax import lax
from jax.sharding import PartitionSpec as P

EXP_COL = 2


def per_device(
    tokens, expert_ids, gate_units, slot_ids, grad_out, gate_weight, up_weight, down_weight
):
    tok_count, model_width = tokens.shape
    top_count = expert_ids.shape[1]
    columns = lax.axis_size("expert")
    node_count = lax.axis_size("node")
    holders = node_count // EXP_COL
    capacity = 5 * tok_count * top_count // 8
    choice_count = tok_count * top_count
    per_lane = max(1, choice_count // columns)
    shares = gate_units.astype(jnp.float32)
    shares = shares / jnp.sum(shares, axis=1, keepdims=True)
    target = (expert_ids // EXP_COL).reshape(-1)
    lanes = jnp.arange(columns, dtype=jnp.int32)
    onehot = (target[:, None] == lanes[None, :]).astype(jnp.int32)
    earlier = jnp.cumsum(onehot, axis=0) - onehot
    rank_in_lane = jnp.sum(earlier * onehot, axis=1)
    dest = target * per_lane + rank_in_lane
    send_rows = jnp.arange(columns * per_lane, dtype=jnp.int32)
    routing = dest[None, :] == send_rows[:, None]
    route_tok = jnp.sum(
        routing.reshape(columns * per_lane, tok_count, top_count).astype(jnp.float32), axis=2
    ).astype(jnp.bfloat16)
    scaled = (shares[:, :, None] * grad_out[:, None, :].astype(jnp.float32)).astype(jnp.bfloat16)
    scaled = scaled.reshape(choice_count, model_width)
    send_x = jnp.dot(route_tok, tokens, preferred_element_type=jnp.float32).astype(jnp.bfloat16)
    send_dy = jnp.dot(
        routing.astype(jnp.bfloat16), scaled, preferred_element_type=jnp.float32
    ).astype(jnp.bfloat16)
    send_slot = jnp.sum(jnp.where(routing, slot_ids.reshape(-1)[None, :] + 1, 0), axis=1) - 1
    got_x, got_dy, got_slot = (
        lax.all_to_all(send_x, "expert", split_axis=0, concat_axis=0, tiled=True),
        lax.all_to_all(send_dy, "expert", split_axis=0, concat_axis=0, tiled=True),
        lax.all_to_all(send_slot, "expert", split_axis=0, concat_axis=0, tiled=True),
    )
    positions = jnp.arange(EXP_COL * capacity, dtype=jnp.int32)
    placer = (got_slot[None, :] == positions[:, None]).astype(jnp.bfloat16)
    packed_x = jnp.dot(placer, got_x, preferred_element_type=jnp.float32).astype(jnp.bfloat16)
    packed_dy = jnp.dot(placer, got_dy, preferred_element_type=jnp.float32).astype(jnp.bfloat16)
    packed_x = packed_x.reshape(EXP_COL, capacity, model_width)
    packed_dy = packed_dy.reshape(EXP_COL, capacity, model_width)
    my_half = lax.axis_index("node") // holders
    every_x, every_dy = (
        lax.all_gather(packed_x, "node", axis=0, tiled=True),
        lax.all_gather(packed_dy, "node", axis=0, tiled=True),
    )
    every_x = every_x.reshape(node_count, EXP_COL, capacity, model_width)
    every_dy = every_dy.reshape(node_count, EXP_COL, capacity, model_width)
    mine_x = lax.dynamic_index_in_dim(every_x, my_half, axis=1, keepdims=False)
    mine_dy = lax.dynamic_index_in_dim(every_dy, my_half, axis=1, keepdims=False)
    row_x = mine_x.reshape(node_count * capacity, model_width)
    row_dy = mine_dy.reshape(node_count * capacity, model_width)
    w_gate = gate_weight[0]
    w_up = up_weight[0]
    w_down = down_weight[0]
    gate_pre = jnp.dot(row_x, w_gate, preferred_element_type=jnp.float32)
    up_pre = jnp.dot(row_x, w_up, preferred_element_type=jnp.float32)
    sigma_gate = jax.nn.sigmoid(gate_pre)
    activ = gate_pre * sigma_gate
    hidden = (activ * up_pre).astype(jnp.bfloat16)
    out_part = jnp.dot(hidden, w_down, preferred_element_type=jnp.float32).astype(jnp.bfloat16)
    grad_hidden = jnp.dot(row_dy, w_down.T, preferred_element_type=jnp.float32)
    grad_down = jnp.dot(hidden.T, row_dy, preferred_element_type=jnp.float32).astype(jnp.bfloat16)
    grad_gpre = (grad_hidden * up_pre * sigma_gate * (1.0 + gate_pre * (1.0 - sigma_gate))).astype(
        jnp.bfloat16
    )
    grad_upre = (grad_hidden * activ).astype(jnp.bfloat16)
    back_part = (
        jnp.dot(grad_gpre, w_gate.T, preferred_element_type=jnp.float32)
        + jnp.dot(grad_upre, w_up.T, preferred_element_type=jnp.float32)
    ).astype(jnp.bfloat16)
    out_part = out_part.reshape(node_count, capacity, model_width)
    back_part = back_part.reshape(node_count, capacity, model_width)
    got_out, got_back = (
        lax.all_to_all(out_part, "node", split_axis=0, concat_axis=0, tiled=True),
        lax.all_to_all(back_part, "node", split_axis=0, concat_axis=0, tiled=True),
    )
    summed_out = jnp.sum(
        got_out.reshape(EXP_COL, holders, capacity, model_width).astype(jnp.float32), axis=1
    )
    summed_back = jnp.sum(
        got_back.reshape(EXP_COL, holders, capacity, model_width).astype(jnp.float32), axis=1
    )
    summed_out = summed_out.astype(jnp.bfloat16).reshape(EXP_COL * capacity, model_width)
    summed_back = summed_back.astype(jnp.bfloat16).reshape(EXP_COL * capacity, model_width)
    ret_out = jnp.dot(placer.T, summed_out, preferred_element_type=jnp.float32).astype(jnp.bfloat16)
    ret_back = jnp.dot(placer.T, summed_back, preferred_element_type=jnp.float32).astype(
        jnp.bfloat16
    )
    home_out, home_back = (
        lax.all_to_all(ret_out, "expert", split_axis=0, concat_axis=0, tiled=True),
        lax.all_to_all(ret_back, "expert", split_axis=0, concat_axis=0, tiled=True),
    )
    dest_tok = dest.reshape(tok_count, top_count)
    mixing = jnp.sum(
        jnp.where(
            dest_tok[:, :, None] == send_rows[None, None, :], shares[:, :, None], jnp.float32(0.0)
        ),
        axis=1,
    )
    mixed = jnp.dot(mixing, home_out.astype(jnp.float32), precision=lax.Precision.HIGHEST).astype(
        jnp.bfloat16
    )
    grad_tokens = jnp.dot(route_tok.T, home_back, preferred_element_type=jnp.float32).astype(
        jnp.bfloat16
    )
    return (mixed, grad_tokens, grad_down[None])


def solution(mesh):
    placed = (
        P(("node", "expert"), None),
        P(("node", "expert"), None),
        P(("node", "expert"), None),
        P(("node", "expert"), None),
        P(("node", "expert"), None),
        P("expert", None, "node"),
        P("expert", None, "node"),
        P("expert", "node", None),
    )
    return jax.shard_map(
        per_device,
        mesh=mesh,
        in_specs=placed,
        out_specs=(
            P(("node", "expert"), None),
            P(("node", "expert"), None),
            P("expert", "node", None),
        ),
        check_vma=False,
    )
```

profile of v0, /device:TPU:98, one launch (start us, length us, event | category | flops | bytes accessed | tf_op | source)
XLA Modules:
  0.0 544.7 jit_solution(9569667803304064679)
XLA Ops:
  9.9 30.7 %all-to-all-start = ((s32[64,1,1]{2,1,0:T(1,128)}), s32[64,1,1]{2,1,0:T(1,128)S(1)}, u32[]{:S(2)}, u32[]{:S(2)}) async-start(s32[64,1,1]{2,1,0:T(1,128)} %copy.27), calls=%async_computation | async-start | bytes 65536 | tf_op jit(solution)/shard_map/all_to_all | solution.py:43
  46.2 16.7 %all-to-all-done = s32[64,1,1]{2,1,0:T(1,128)S(1)} async-done(((s32[64,1,1]{2,1,0:T(1,128)}), s32[64,1,1]{2,1,0:T(1,128)S(1)}, u32[]{:S(2)}, u32[]{:S(2)}) %all-to-all-start) | async-done | bytes 288 | tf_op jit(solution)/shard_map/all_to_all | solution.py:43
  63.0 8.1 %all-to-all-start.4 = ((bf16[64,2,2048]{2,1,0:T(2,128)(2,1)}), bf16[64,2,2048]{2,1,0:T(2,128)(2,1)S(1)}, u32[]{:S(2)}, u32[]{:S(2)}) async-start(bf16[64,2,2048]{2,1,0:T(2,128)(2,1)} %reshape.122), calls=%async_computation.4 | async-start | bytes 1048576 | tf_op jit(solution)/shard_map/all_to_all | solution.py:42
  72.3 61.5 %all-to-all-done.4 = bf16[64,2,2048]{2,1,0:T(2,128)(2,1)S(1)} async-done(((bf16[64,2,2048]{2,1,0:T(2,128)(2,1)}), bf16[64,2,2048]{2,1,0:T(2,128)(2,1)S(1)}, u32[]{:S(2)}, u32[]{:S(2)}) %all-to-all-start.4) | async-done | bytes 524320 | tf_op jit(solution)/shard_map/all_to_all | solution.py:42
  137.9 69.9 %all_to_all.64 = bf16[64,2,2048]{2,1,0:T(2,128)(2,1)S(1)} all-to-all(bf16[64,2,2048]{2,1,0:T(2,128)(2,1)S(1)} %reshape.118), channel_id=1, replica_groups=mesh['node'=16,'expert'=64] {'expert'}, dimensions={0} | all-to-all | bytes 1048576 | tf_op jit(solution)/shard_map/all_to_all | solution.py:41
  210.0 42.9 %all-gather.3.cloned.1.call-done = bf16[32,20,4096]{2,1,0:T(8,128)(2,1)} async-done(((bf16[2,20,4096]{2,1,0:T(8,128)(2,1)}), bf16[32,20,4096]{2,1,0:T(8,128)(2,1)}) %all-gather.3.cloned.1.call-update) | async-done | bytes 5242896 | tf_op jit(solution)/shard_map/all_gather | solution.py:53
  252.9 6.4 %dynamic-slice_bitcast_fusion = (bf16[16,1,20,4096]{3,2,0,1:T(8,128)(2,1)}, bf16[16,1,20,4096]{3,2,0,1:T(8,128)(2,1)}) fusion(bf16[16,2,20,4096]{3,2,1,0:T(8,128)(2,1)} %bitcast.72, s32[]{:T(128)S(6)} %select_n.27, bf16[16,2,20,4096]{3,2,1,0:T(8,128)(2,1)} %bitcast.73), kind=kLoop, calls=%fused_computation.19 | loop fusion | bytes 10485764
  259.3 2.8 reshape.113
  262.1 4.3 reshape.107
  266.4 2.2 fusion.6
  271.5 2.4 fusion
  273.9 4.3 reshape.114
  278.2 5.5 %all-to-all-start.5 = ((bf16[16,20,4096]{2,1,0:T(8,128)(2,1)}), bf16[16,20,4096]{2,1,0:T(8,128)(2,1)}, u32[]{:S(2)}, u32[]{:S(2)}) async-start(bf16[16,20,4096]{2,1,0:T(8,128)(2,1)} %reshape.114), calls=%async_computation.5 | async-start | bytes 6291456 | tf_op jit(solution)/shard_map/all_to_all | solution.py:85
  283.7 3.5 convolution_convert_fusion
  287.2 4.3 reshape.108
  291.5 35.3 %all-to-all-done.5 = bf16[16,20,4096]{2,1,0:T(8,128)(2,1)} async-done(((bf16[16,20,4096]{2,1,0:T(8,128)(2,1)}), bf16[16,20,4096]{2,1,0:T(8,128)(2,1)}, u32[]{:S(2)}, u32[]{:S(2)}) %all-to-all-start.5) | async-done | bytes 2621472 | tf_op jit(solution)/shard_map/all_to_all | solution.py:85
  326.7 4.4 all-to-all-start.2
  331.1 3.3 bitcast_reduce_fusion
  336.2 2.1 fusion.5
  338.3 2.7 reduce.6
  341.0 2.2 reshape.124
  343.3 30.3 %all-to-all-done.2 = bf16[16,20,4096]{2,1,0:T(8,128)(2,1)} async-done(((bf16[16,20,4096]{2,1,0:T(8,128)(2,1)}), bf16[16,20,4096]{2,1,0:T(8,128)(2,1)}, u32[]{:S(2)}, u32[]{:S(2)}) %all-to-all-start.2) | async-done | bytes 2621472 | tf_op jit(solution)/shard_map/all_to_all | solution.py:84
  373.6 25.7 %all-to-all-start.6 = ((bf16[64,2,2048]{2,1,0:T(2,128)(2,1)}), bf16[64,2,2048]{2,1,0:T(2,128)(2,1)}, u32[]{:S(2)}, u32[]{:S(2)}) async-start(bf16[64,2,2048]{2,1,0:T(2,128)(2,1)} %reshape.124), calls=%async_computation.6 | async-start | bytes 1048576 | tf_op jit(solution)/shard_map/all_to_all | solution.py:101
  399.3 3.3 bitcast_reduce_fusion.1
  404.3 2.1 fusion.4
  406.5 2.7 reduce.5
  409.2 2.2 reshape.120
  411.4 51.1 %all-to-all-done.6 = bf16[64,2,2048]{2,1,0:T(2,128)(2,1)} async-done(((bf16[64,2,2048]{2,1,0:T(2,128)(2,1)}), bf16[64,2,2048]{2,1,0:T(2,128)(2,1)}, u32[]{:S(2)}, u32[]{:S(2)}) %all-to-all-start.6) | async-done | bytes 524320 | tf_op jit(solution)/shard_map/all_to_all | solution.py:101
  462.6 7.2 %all-to-all-start.3 = ((bf16[64,2,2048]{2,1,0:T(2,128)(2,1)}), bf16[64,2,2048]{2,1,0:T(2,128)(2,1)}, u32[]{:S(2)}, u32[]{:S(2)}) async-start(bf16[64,2,2048]{2,1,0:T(2,128)(2,1)} %reshape.120), calls=%async_computation.3 | async-start | bytes 1048576 | tf_op jit(solution)/shard_map/all_to_all | solution.py:100
  471.5 3.6 reshape.125
  476.4 56.5 %all-to-all-done.3 = bf16[64,2,2048]{2,1,0:T(2,128)(2,1)} async-done(((bf16[64,2,2048]{2,1,0:T(2,128)(2,1)}), bf16[64,2,2048]{2,1,0:T(2,128)(2,1)}, u32[]{:S(2)}, u32[]{:S(2)}) %all-to-all-start.3) | async-done | bytes 524320 | tf_op jit(solution)/shard_map/all_to_all | solution.py:100
  532.8 3.6 reshape.121
  (56 shorter events, 26.5 us)
Async XLA Ops:
  7.2 262.5 %copy-start = (bf16[1,4096,96]{1,2,0:T(8,128)(2,1)S(1)}, bf16[1,4096,96]{1,2,0:T(8,128)(2,1)}, u32[]{:S(2)}) copy-start(bf16[1,4096,96]{1,2,0:T(8,128)(2,1)} %param.14) | copy-start | bytes 2359300
  9.9 53.0 %all-to-all-start = ((s32[64,1,1]{2,1,0:T(1,128)}), s32[64,1,1]{2,1,0:T(1,128)S(1)}, u32[]{:S(2)}, u32[]{:S(2)}) async-start(s32[64,1,1]{2,1,0:T(1,128)} %copy.27), calls=%async_computation | async-start | bytes 65536 | tf_op jit(solution)/shard_map/all_to_all | solution.py:43
  44.0 92.0 %copy-start.4 = (s32[4,8]{1,0:T(4,128)S(1)}, s32[4,8]{1,0:T(4,128)}, u32[]{:S(2)}) copy-start(s32[4,8]{1,0:T(4,128)} %param.9) | copy-start | bytes 388
  44.0 92.1 %copy-start.3 = (bf16[4,4096]{1,0:T(4,128)(2,1)S(1)}, bf16[4,4096]{1,0:T(4,128)(2,1)}, u32[]{:S(2)}) copy-start(bf16[4,4096]{1,0:T(4,128)(2,1)} %param.8) | copy-start | bytes 98308
  63.0 70.9 %all-to-all-start.4 = ((bf16[64,2,2048]{2,1,0:T(2,128)(2,1)}), bf16[64,2,2048]{2,1,0:T(2,128)(2,1)S(1)}, u32[]{:S(2)}, u32[]{:S(2)}) async-start(bf16[64,2,2048]{2,1,0:T(2,128)(2,1)} %reshape.122), calls=%async_computation.4 | async-start | bytes 1048576 | tf_op jit(solution)/shard_map/all_to_all | solution.py:42
  71.0 139.0 %all-gather.5.cloned.1.call-start = ((), (), s32[]{:S(2)}) async-start(), calls=%async_computation.8 | async-start | bytes 6684672 | tf_op jit(solution)/shard_map/all_gather | solution.py:54
  135.9 116.9 %all-gather.3.cloned.1.call-start = ((), (), s32[]{:S(2)}) async-start(), calls=%async_computation.7 | async-start | bytes 6684672 | tf_op jit(solution)/shard_map/all_gather | solution.py:53
  266.4 2.3 copy-start.1
  266.4 2.3 copy-start.2
  278.2 48.5 %all-to-all-start.5 = ((bf16[16,20,4096]{2,1,0:T(8,128)(2,1)}), bf16[16,20,4096]{2,1,0:T(8,128)(2,1)}, u32[]{:S(2)}, u32[]{:S(2)}) async-start(bf16[16,20,4096]{2,1,0:T(8,128)(2,1)} %reshape.114), calls=%async_computation.5 | async-start | bytes 6291456 | tf_op jit(solution)/shard_map/all_to_all | solution.py:85
  326.7 46.8 %all-to-all-start.2 = ((bf16[16,20,4096]{2,1,0:T(8,128)(2,1)}), bf16[16,20,4096]{2,1,0:T(8,128)(2,1)}, u32[]{:S(2)}, u32[]{:S(2)}) async-start(bf16[16,20,4096]{2,1,0:T(8,128)(2,1)} %reshape.108), calls=%async_computation.2 | async-start | bytes 6291456 | tf_op jit(solution)/shard_map/all_to_all | solution.py:84
  373.6 89.0 %all-to-all-start.6 = ((bf16[64,2,2048]{2,1,0:T(2,128)(2,1)}), bf16[64,2,2048]{2,1,0:T(2,128)(2,1)}, u32[]{:S(2)}, u32[]{:S(2)}) async-start(bf16[64,2,2048]{2,1,0:T(2,128)(2,1)} %reshape.124), calls=%async_computation.6 | async-start | bytes 1048576 | tf_op jit(solution)/shard_map/all_to_all | solution.py:101
  462.6 70.3 %all-to-all-start.3 = ((bf16[64,2,2048]{2,1,0:T(2,128)(2,1)}), bf16[64,2,2048]{2,1,0:T(2,128)(2,1)}, u32[]{:S(2)}, u32[]{:S(2)}) async-start(bf16[64,2,2048]{2,1,0:T(2,128)(2,1)} %reshape.120), calls=%async_computation.3 | async-start | bytes 1048576 | tf_op jit(solution)/shard_map/all_to_all | solution.py:100
Sparse Core Ops, SparseCore 0:
  136.0 45.1 all-gather.4
  210.1 42.7 all-gather.2
where the time goes:
time: 546 us; the launch traced here: 545 us
  waiting for transfers between devices  294 us (54%)
  starting transfers between devices  81.7 us (15%)
  blocking collectives  69.9 us (13%)
  local copies, waits for them, and re-layouts  43.3 us (8%)
  matrix products  21.7 us (4%)
  other arithmetic  19.6 us (4%)
  between operations  14.3 us (3%)
    all_to_all x1, blocking collectives, per_device(): lax.all_to_all(send_x, 'expert', split_axis=0, concat_axis=0, tiled=True)  69.9 us
    all_to_all x1, waiting for transfers between devices, per_device(): lax.all_to_all(send_dy, 'expert', split_axis=0, concat_axis=0, tiled=True)  61.5 us
    all_to_all x1, waiting for transfers between devices, per_device(): lax.all_to_all(ret_out, 'expert', split_axis=0, concat_axis=0, tiled=True)  56.5 us
    all_to_all x1, waiting for transfers between devices, per_device(): lax.all_to_all(ret_back, 'expert', split_axis=0, concat_axis=0, tiled=True)  51.1 us
    all_gather x1, waiting for transfers between devices, per_device(): lax.all_gather(packed_x, 'node', axis=0, tiled=True)  42.9 us
    all_to_all x1, waiting for transfers between devices, per_device(): lax.all_to_all(back_part, 'node', split_axis=0, concat_axis=0, tiled=True)  35.3 us
    all_to_all x1, starting transfers between devices, per_device(): lax.all_to_all(send_slot, 'expert', split_axis=0, concat_axis=0, tiled=True)  30.7 us
    all_to_all x1, waiting for transfers between devices, per_device(): lax.all_to_all(out_part, 'node', split_axis=0, concat_axis=0, tiled=True)  30.3 us
  transfers between devices with their start and end apart: 8, of which 7 were waited for; matrix products, arithmetic and copies ran while one was open for 9% of the time, Pallas kernels for 0%

commit v1 on v0

v1 whole, which is shorter than its diff:
```python
import jax
import jax.numpy as jnp
from jax import lax
from jax.sharding import Mesh
from jax.sharding import PartitionSpec as P

EXP_COL = 2
BLOCK = ("yh", "zd")
CHIPS = ("yl", "x")
LANES = 128


def per_device(
    tokens, expert_ids, gate_units, slot_ids, grad_out, gate_weight, up_weight, down_weight
):
    bf16, f32 = jnp.bfloat16, jnp.float32
    tok_count, width = tokens.shape
    top_count = expert_ids.shape[1]
    za, zd, yh = lax.axis_size("za"), lax.axis_size("zd"), lax.axis_size("yh")
    yl, xs = lax.axis_size("yl"), lax.axis_size("x")
    capacity = 5 * tok_count * top_count // 8
    dests = yh * zd
    chips = yl * xs
    kinds = jnp.eye(2, dtype=f32)

    with jax.named_scope("spread"):
        meta = jnp.concatenate([expert_ids, slot_ids, gate_units], axis=1).astype(bf16)
        meta = jnp.pad(meta, ((0, tok_count), (0, LANES - 3 * top_count)))
        block = jnp.concatenate([tokens, grad_out], axis=0)
        spread = lax.all_gather(jnp.concatenate([block, meta], axis=1), "za", axis=0, tiled=True)

    with jax.named_scope("relay"):
        info = spread[:, width : width + 3 * top_count].reshape(za, 2, tok_count, -1)[:, 0]
        info = info.astype(jnp.int32)
        ids, slots, units = (
            info[..., :top_count],
            info[..., top_count : 2 * top_count],
            info[..., 2 * top_count :].astype(f32),
        )
        shares = units / jnp.sum(units, axis=-1, keepdims=True)
        lane = jnp.arange(dests, dtype=jnp.int32)
        column = (lane // zd) * (za * zd) + lax.axis_index("za") * zd + lane % zd
        match = (ids // EXP_COL)[None] == column[:, None, None, None]
        picks = jnp.sum(match.astype(f32), axis=-1)
        pick_share = jnp.sum(jnp.where(match, shares[None], f32(0.0)), axis=-1)
        row_share = jnp.sum(pick_share, axis=-1)
        row_slot = jnp.sum(jnp.where(match, slots[None] + 1, 0), axis=(-1, -2)) - 1
        sources = jnp.eye(za, dtype=f32)
        route = (
            picks[:, None, :, None, None, :]
            * sources[None, None, :, :, None, None]
            * kinds[None, :, None, None, :, None]
        ).reshape(dests * 2 * za, za * 2 * tok_count)
        scale = jnp.stack([jnp.ones_like(row_share), row_share], axis=1).reshape(-1, 1)
        rows = jnp.dot(route.astype(bf16), spread[:, :width], preferred_element_type=f32)
        rows = (rows * scale).astype(bf16)
        slot_rows = jnp.broadcast_to(row_slot[:, None, :, None], (dests, 2, za, LANES))
        slot_rows = slot_rows.reshape(-1, LANES).astype(bf16)
        sending = jnp.concatenate([rows, slot_rows], axis=1).reshape(dests, 2 * za, -1)
        got = lax.all_to_all(sending, BLOCK, split_axis=0, concat_axis=0, tiled=True)

    with jax.named_scope("dispatch"):
        got_slot = got[:, :za, width].astype(jnp.int32)
        position = jnp.arange(EXP_COL * capacity, dtype=jnp.int32).reshape(EXP_COL, capacity)
        placer = (got_slot[None, None] == position[:, :, None, None]).astype(f32)
        place = (
            placer[:, None, :, :, None, :] * kinds[None, :, None, None, :, None]
        ).reshape(EXP_COL, 2 * capacity, dests * 2 * za)
        packed = jnp.dot(
            place.reshape(EXP_COL * 2 * capacity, -1).astype(bf16),
            got[:, :, :width].reshape(dests * 2 * za, width),
            preferred_element_type=f32,
        ).astype(bf16)
        packed = packed.reshape(EXP_COL, 1, 2 * capacity, width)
        packed = jnp.broadcast_to(packed, (EXP_COL, xs, 2 * capacity, width))
        mine = lax.all_to_all(
            packed.reshape(chips, 2 * capacity, width), CHIPS, split_axis=0, concat_axis=0, tiled=True
        )
        swap = [(0, 1), (1, 0)]
        other = lax.ppermute(mine, "co", swap)

    with jax.named_scope("expert"):
        weights = jnp.concatenate([down_weight[0], gate_weight[0].T, up_weight[0].T], axis=0)
        hid = down_weight.shape[1]

        def half(rows_in):
            pre = lax.dot_general(
                rows_in, weights, (((1,), (1,)), ((), ())), preferred_element_type=f32
            ).reshape(chips, 2, capacity, 3 * hid)
            gate_pre = pre[:, 0, :, hid : 2 * hid]
            up_pre = pre[:, 0, :, 2 * hid :]
            grad_hidden = pre[:, 1, :, :hid]
            sigma = jax.nn.sigmoid(gate_pre)
            activ = gate_pre * sigma
            hidden = (activ * up_pre).astype(bf16)
            dgate = (grad_hidden * up_pre * sigma * (1.0 + gate_pre * (1.0 - sigma))).astype(bf16)
            dup = (grad_hidden * activ).astype(bf16)
            zero = jnp.zeros_like(hidden)
            mixer = jnp.stack(
                [
                    jnp.concatenate([hidden, zero, zero], axis=-1),
                    jnp.concatenate([zero, dgate, dup], axis=-1),
                ],
                axis=1,
            ).reshape(chips * 2 * capacity, 3 * hid)
            held = jnp.stack([zero, hidden], axis=1).reshape(chips * 2 * capacity, hid)
            return mixer, held

        flat_mine = mine.reshape(chips * 2 * capacity, width)
        flat_other = other.reshape(chips * 2 * capacity, width)
        mixer_mine, held_mine = half(flat_mine)
        mixer_other, held_other = half(flat_other)
        part_other = jnp.dot(mixer_other, weights, preferred_element_type=f32).astype(bf16)
        part_got = lax.ppermute(part_other, "co", swap)
        part_mine = jnp.dot(mixer_mine, weights, preferred_element_type=f32)
        grad_down = lax.dot_general(
            held_mine, flat_mine, (((0,), (0,)), ((), ())), preferred_element_type=f32
        ) + lax.dot_general(
            held_other, flat_other, (((0,), (0,)), ((), ())), preferred_element_type=f32
        )
        part = (part_mine + part_got.astype(f32)).astype(bf16)

    with jax.named_scope("combine"):
        parts = lax.all_to_all(
            part.reshape(chips, 2 * capacity, width), CHIPS, split_axis=0, concat_axis=0, tiled=True
        )
        gather = jnp.broadcast_to(
            place[:, None], (EXP_COL, xs, 2 * capacity, dests * 2 * za)
        ).reshape(chips * 2 * capacity, -1)
        back_rows = lax.dot_general(
            gather.astype(bf16),
            parts.reshape(chips * 2 * capacity, width),
            (((0,), (0,)), ((), ())),
            preferred_element_type=f32,
        ).astype(bf16)
        home = lax.all_to_all(
            back_rows.reshape(dests, 2 * za, width), BLOCK, split_axis=0, concat_axis=0, tiled=True
        ).reshape(dests * 2 * za, width)

    with jax.named_scope("sum"):
        weigh = jnp.stack([pick_share, picks], axis=1)
        weigh = (
            weigh.transpose(2, 1, 3, 0)[:, :, :, :, None, None]
            * sources[:, None, None, None, None, :]
            * kinds[None, :, None, None, :, None]
        ).reshape(za * 2 * tok_count, dests * 2 * za)
        high = lax.reduce_precision(weigh, 8, 7)
        rest = weigh - high
        middle = lax.reduce_precision(rest, 8, 7)
        low = rest - middle
        split = jnp.concatenate([high, middle, low], axis=0).astype(bf16)
        sums = jnp.dot(split, home, preferred_element_type=f32).reshape(3, -1, width)
        sums = (sums[0] + (sums[1] + sums[2])).astype(bf16)
        blocks = lax.all_to_all(
            sums.reshape(za, 2 * tok_count, width), "za", split_axis=0, concat_axis=0, tiled=True
        )
        total = jnp.sum(blocks.astype(f32), axis=0).astype(bf16)
    return total[:tok_count], total[tok_count:], grad_down.astype(bf16)[None]


def solution(mesh):
    columns = mesh.shape["expert"]
    zd = min(4, columns // 4)
    za = columns // (2 * zd)
    names = ("yl", "x", "co", "yh", "za", "zd")
    chips = mesh.shape["node"] // 4
    fine = Mesh(mesh.devices.reshape(2, chips, 2, 2, za, zd), names)
    node, expert = names[:3], names[3:]
    rows = P(names, None)
    return jax.shard_map(
        per_device,
        mesh=fine,
        in_specs=(rows,) * 5 + (P(expert, None, node),) * 2 + (P(expert, node, None),),
        out_specs=(rows, rows, P(expert, node, None)),
        check_vma=False,
    )
```

time: 546 us -> 307 us (0.56)
  the two profiles are of different devices: /device:TPU:98 before, /device:TPU:95 now
where the time goes in v1:
time: 307 us; the launch traced here: 306 us
  waiting for transfers between devices  143 us (47%)
  blocking collectives  83 us (27%)
  starting transfers between devices  36.9 us (12%)
  matrix products  22.7 us (7%)
  other arithmetic  10.1 us (3%)
  local copies, waits for them, and re-layouts  9.1 us (3%)
    all_to_all x1, waiting for transfers between devices, per_device(): lax.all_to_all(sums.reshape(za, 2 * tok_count, width), 'za', split_axis=0...  51.1 us
    all_gather x1, blocking collectives, per_device(): lax.all_gather(jnp.concatenate([block, meta], axis=1), 'za', axis=0, tile...  49.1 us
    all_to_all x1, waiting for transfers between devices, per_device(): lax.all_to_all(part.reshape(chips, 2 * capacity, width), CHIPS, split_axi...  37.5 us
    all_to_all x1, blocking collectives, per_device(): lax.all_to_all(packed.reshape(chips, 2 * capacity, width), CHIPS, split_a...  33.9 us
    all_to_all x1, waiting for transfers between devices, per_device(): lax.all_to_all(sending, BLOCK, split_axis=0, concat_axis=0, tiled=True)  24.4 us
    all_to_all x1, waiting for transfers between devices, per_device(): lax.all_to_all(back_rows.reshape(dests, 2 * za, width), BLOCK, split_axis...  22.8 us
    all_to_all x1, starting transfers between devices, per_device(): lax.all_to_all(sums.reshape(za, 2 * tok_count, width), 'za', split_axis=0...  9.35 us
    all_to_all x1, starting transfers between devices, per_device(): lax.all_to_all(sending, BLOCK, split_axis=0, concat_axis=0, tiled=True)  8.41 us
  transfers between devices with their start and end apart: 6, of which 6 were waited for; matrix products, arithmetic and copies ran while one was open for 4% of the time, Pallas kernels for 0%

profile of v1, /device:TPU:95, one launch (start us, length us, event | category | flops | bytes accessed | tf_op | source)
XLA Modules:
  0.0 306.2 jit_solution(3357786590364927915)
XLA Ops:
  0.6 0.7 convert.21
  1.3 0.7 convert.22
  2.8 0.8 pad_maximum_fusion.4
  3.6 49.1 %all_gather.3 = bf16[64,4224]{1,0:T(8,128)(2,1)S(1)} all-gather(bf16[8,4224]{1,0:T(8,128)(2,1)S(1)} %pad_maximum_fusion.4), channel_id=1, replica_groups=mesh['yl'=2,'x'=4,'co'=2,'yh'=2,'za'=8,'zd'=4] {'za'}, dimensions={0}, use_global_device_ids=true | all-gather | bytes 608256 | tf_op jit(solution)/shard_map/spread/all_gather | solution.py:30
  55.4 1.1 pad_maximum_fusion.1
  56.4 8.4 %all-to-all-start = ((bf16[8,16,4224]{2,1,0:T(8,128)(2,1)}), bf16[8,16,4224]{2,1,0:T(8,128)(2,1)S(1)}, u32[]{:S(2)}, u32[]{:S(2)}) async-start(bf16[8,16,4224]{2,1,0:T(8,128)(2,1)} %bitcast.7), calls=%async_computation | async-start | bytes 2162688 | tf_op jit(solution)/shard_map/relay/all_to_all | solution.py:60
  64.9 24.4 %all-to-all-done = bf16[8,16,4224]{2,1,0:T(8,128)(2,1)S(1)} async-done(((bf16[8,16,4224]{2,1,0:T(8,128)(2,1)}), bf16[8,16,4224]{2,1,0:T(8,128)(2,1)S(1)}, u32[]{:S(2)}, u32[]{:S(2)}) %all-to-all-start) | async-done | bytes 1081376 | tf_op jit(solution)/shard_map/relay/all_to_all | solution.py:60
  90.7 33.9 %all_to_all.25 = bf16[8,40,4096]{2,1,0:T(8,128)(2,1)S(1)} all-to-all(bf16[8,40,4096]{2,1,0:T(8,128)(2,1)S(1)} %bitcast.157), channel_id=1, replica_groups=mesh['yl'=2,'x'=4,'co'=2,'yh'=2,'za'=8,'zd'=4] {'yl','x'}, dimensions={0} | all-to-all | bytes 5242880 | tf_op jit(solution)/shard_map/dispatch/all_to_all | solution.py:76
  124.5 1.4 copy.110
  126.0 4.1 %collective-permute-start = (bf16[8,40,4096]{2,0,1:T(8,128)(2,1)S(1)}, bf16[8,40,4096]{2,0,1:T(8,128)(2,1)S(1)}, u32[]{:S(2)}, u32[]{:S(2)}) collective-permute-start(bf16[8,40,4096]{2,0,1:T(8,128)(2,1)S(1)} %copy.110), channel_id=1, source_target_pairs={{0,64},{64,0},{1,65},{65,1},{2,66},{66,2},{3,67},{67,3},{4,68},{68... | collective-permute-start | bytes 7864328 | tf_op jit(solution)/shard_map/dispatch/ppermute | solution.py:80
  130.1 1.5 fusion.5
  131.8 2.8 collective-permute-done
  134.6 1.5 fusion.3
  137.1 4.6 %convolution_convert_fusion = bf16[320,4096]{1,0:T(8,128)(2,1)} fusion(bf16[320,288]{1,0:T(8,128)(2,1)S(1)} %reshape.214, bf16[96,4096]{1,0:T(8,128)(2,1)} %bitcast.169, bf16[96,4096]{1,0:T(8,128)(2,1)} %bitcast.173, bf16[96,4096]{1,0:T(8,128)(2,1)} %bitcast.177), kind=kOutput, calls=%fused_computation | convolution fusion | flops 763363328 | bytes 5165056 | tf_op jit(solution)/shard_map/expert/dot_general | solution.py:113
  141.7 2.3 collective-permute-start.1
  144.2 4.7 %collective-permute-done.1 = bf16[320,4096]{1,0:T(8,128)(2,1)} collective-permute-done((bf16[320,4096]{1,0:T(8,128)(2,1)}, bf16[320,4096]{1,0:T(8,128)(2,1)}, u32[]{:S(2)}, u32[]{:S(2)}) %collective-permute-start.1) | collective-permute-done | bytes 2621472 | tf_op jit(solution)/shard_map/expert/ppermute | solution.py:114
  148.8 5.5 %add_convert_fusion = bf16[320,4096]{1,0:T(8,128)(2,1)} fusion(bf16[320,4096]{1,0:T(8,128)(2,1)} %collective-permute-done.1, bf16[320,288]{1,0:T(8,128)(2,1)S(1)} %reshape.213, bf16[96,4096]{1,0:T(8,128)(2,1)} %bitcast.170, bf16[96,4096]{1,0:T(8,128)(2,1)} %bitcast.174, bf16[96,4096]{1,0:T(8,128)(2,1)} %bitcast.178), kind=kOutput, calls=%fused_computation.1 | convolution fusion | flops 765984768 | bytes 7786496 | tf_op jit(solution)/shard_map/expert/dot_general | solution.py:115
  154.3 6.7 %all-to-all-start.2 = ((bf16[8,40,4096]{2,1,0:T(8,128)(2,1)}), bf16[8,40,4096]{2,1,0:T(8,128)(2,1)}, u32[]{:S(2)}, u32[]{:S(2)}) async-start(bf16[8,40,4096]{2,1,0:T(8,128)(2,1)} %bitcast.161), calls=%async_computation.2 | async-start | bytes 5242880 | tf_op jit(solution)/shard_map/combine/all_to_all | solution.py:124
  161.8 37.5 %all-to-all-done.2 = bf16[8,40,4096]{2,1,0:T(8,128)(2,1)} async-done(((bf16[8,40,4096]{2,1,0:T(8,128)(2,1)}), bf16[8,40,4096]{2,1,0:T(8,128)(2,1)}, u32[]{:S(2)}, u32[]{:S(2)}) %all-to-all-start.2) | async-done | bytes 2621472 | tf_op jit(solution)/shard_map/combine/all_to_all | solution.py:124
  199.3 3.5 %convolution_convert_fusion.1 = bf16[128,4096]{1,0:T(8,128)(2,1)} fusion(bf16[320,128]{1,0:T(8,128)(2,1)S(1)} %bitcast.164, bf16[320,4096]{1,0:T(8,128)(2,1)} %bitcast.34), kind=kOutput, calls=%fused_computation.4 | convolution fusion | flops 336068608 | bytes 3751936 | tf_op jit(solution)/shard_map/combine/dot_general | solution.py:130
  202.8 6.0 %all-to-all-start.3 = ((bf16[8,16,4096]{2,1,0:T(8,128)(2,1)}), bf16[8,16,4096]{2,1,0:T(8,128)(2,1)}, u32[]{:S(2)}, u32[]{:S(2)}) async-start(bf16[8,16,4096]{2,1,0:T(8,128)(2,1)} %bitcast.158), calls=%async_computation.3 | async-start | bytes 2097152 | tf_op jit(solution)/shard_map/combine/all_to_all | solution.py:136
  209.6 0.7 mul.185
  210.3 22.8 %all-to-all-done.3 = bf16[8,16,4096]{2,1,0:T(8,128)(2,1)} async-done(((bf16[8,16,4096]{2,1,0:T(8,128)(2,1)}), bf16[8,16,4096]{2,1,0:T(8,128)(2,1)}, u32[]{:S(2)}, u32[]{:S(2)}) %all-to-all-start.3) | async-done | bytes 1048608 | tf_op jit(solution)/shard_map/combine/all_to_all | solution.py:136
  233.1 1.8 fusion.32
  234.9 0.9 fusion.9
  235.9 9.4 %all-to-all-start.4 = ((bf16[8,8,4096]{2,1,0:T(8,128)(2,1)}), bf16[8,8,4096]{2,1,0:T(8,128)(2,1)S(1)}, u32[]{:S(2)}, u32[]{:S(2)}) async-start(bf16[8,8,4096]{2,1,0:T(8,128)(2,1)} %fusion.9), calls=%async_computation.4 | async-start | bytes 1048576 | tf_op jit(solution)/shard_map/sum/all_to_all | solution.py:154
  245.2 1.1 multiply_convert_fusion.3
  246.4 1.9 fusion.62
  248.3 1.1 multiply_convert_fusion.2
  249.5 3.3 %copy.116 = bf16[8,40,4096]{2,1,0:T(8,128)(2,1)S(1)} copy(bf16[8,40,4096]{2,0,1:T(8,128)(2,1)} %copy-done.1) | data formatting | bytes 5242880 | tf_op jit(solution)/shard_map/dispatch/ppermute | solution.py:80
  252.8 1.6 fusion.2
  254.4 51.1 %all-to-all-done.4 = bf16[8,8,4096]{2,1,0:T(8,128)(2,1)S(1)} async-done(((bf16[8,8,4096]{2,1,0:T(8,128)(2,1)}), bf16[8,8,4096]{2,1,0:T(8,128)(2,1)S(1)}, u32[]{:S(2)}, u32[]{:S(2)}) %all-to-all-start.4) | async-done | bytes 524320 | tf_op jit(solution)/shard_map/sum/all_to_all | solution.py:154
  (81 shorter events, 8.1 us)
Async XLA Ops:
  56.4 32.8 %all-to-all-start = ((bf16[8,16,4224]{2,1,0:T(8,128)(2,1)}), bf16[8,16,4224]{2,1,0:T(8,128)(2,1)S(1)}, u32[]{:S(2)}, u32[]{:S(2)}) async-start(bf16[8,16,4224]{2,1,0:T(8,128)(2,1)} %bitcast.7), calls=%async_computation | async-start | bytes 2162688 | tf_op jit(solution)/shard_map/relay/all_to_all | solution.py:60
  124.5 5.6 %copy-start.4 = (bf16[1,4096,96]{1,2,0:T(8,128)(2,1)S(1)}, bf16[1,4096,96]{1,2,0:T(8,128)(2,1)}, u32[]{:S(2)}) copy-start(bf16[1,4096,96]{1,2,0:T(8,128)(2,1)} %param.14) | copy-start | bytes 2359300
  124.5 5.6 %copy-start.5 = (bf16[1,4096,96]{1,2,0:T(8,128)(2,1)S(1)}, bf16[1,4096,96]{1,2,0:T(8,128)(2,1)}, u32[]{:S(2)}) copy-start(bf16[1,4096,96]{1,2,0:T(8,128)(2,1)} %param.13) | copy-start | bytes 2359300
  124.5 5.6 %copy-start.6 = (bf16[1,96,4096]{2,1,0:T(8,128)(2,1)S(1)}, bf16[1,96,4096]{2,1,0:T(8,128)(2,1)}, u32[]{:S(2)}) copy-start(bf16[1,96,4096]{2,1,0:T(8,128)(2,1)} %param.15) | copy-start | bytes 2359300
  126.0 8.6 %collective-permute-start = (bf16[8,40,4096]{2,0,1:T(8,128)(2,1)S(1)}, bf16[8,40,4096]{2,0,1:T(8,128)(2,1)S(1)}, u32[]{:S(2)}, u32[]{:S(2)}) collective-permute-start(bf16[8,40,4096]{2,0,1:T(8,128)(2,1)S(1)} %copy.110), channel_id=1, source_target_pairs={{0,64},{64,0},{1,65},{65,1},{2,66},{66,2},{3,67},{67,3},{4,68},{68... | collective-permute-start | bytes 7864328 | tf_op jit(solution)/shard_map/dispatch/ppermute | solution.py:80
  131.6 4.5 %copy-start.3 = (f32[8,2,20,288]{3,0,2,1:T(8,128)}, f32[8,2,20,288]{3,0,2,1:T(8,128)S(1)}, u32[]{:S(2)}) copy-start(f32[8,2,20,288]{3,0,2,1:T(8,128)S(1)} %fusion.5) | copy-start | bytes 1105924
  134.6 1.5 copy-start.1
  136.1 0.8 copy-start.2
  141.7 7.1 %collective-permute-start.1 = (bf16[320,4096]{1,0:T(8,128)(2,1)}, bf16[320,4096]{1,0:T(8,128)(2,1)}, u32[]{:S(2)}, u32[]{:S(2)}) collective-permute-start(bf16[320,4096]{1,0:T(8,128)(2,1)} %convolution_convert_fusion), channel_id=1, source_target_pairs={{0,64},{64,0},{1,65},{65,1},{2,66},{66,2},{3,67},{67,3},{4,68},{68... | collective-permute-start | bytes 7864328 | tf_op jit(solution)/shard_map/expert/ppermute | solution.py:114
  154.3 45.0 %all-to-all-start.2 = ((bf16[8,40,4096]{2,1,0:T(8,128)(2,1)}), bf16[8,40,4096]{2,1,0:T(8,128)(2,1)}, u32[]{:S(2)}, u32[]{:S(2)}) async-start(bf16[8,40,4096]{2,1,0:T(8,128)(2,1)} %bitcast.161), calls=%async_computation.2 | async-start | bytes 5242880 | tf_op jit(solution)/shard_map/combine/all_to_all | solution.py:124
  202.8 30.3 %all-to-all-start.3 = ((bf16[8,16,4096]{2,1,0:T(8,128)(2,1)}), bf16[8,16,4096]{2,1,0:T(8,128)(2,1)}, u32[]{:S(2)}, u32[]{:S(2)}) async-start(bf16[8,16,4096]{2,1,0:T(8,128)(2,1)} %bitcast.158), calls=%async_computation.3 | async-start | bytes 2097152 | tf_op jit(solution)/shard_map/combine/all_to_all | solution.py:136
  235.9 69.6 %all-to-all-start.4 = ((bf16[8,8,4096]{2,1,0:T(8,128)(2,1)}), bf16[8,8,4096]{2,1,0:T(8,128)(2,1)S(1)}, u32[]{:S(2)}, u32[]{:S(2)}) async-start(bf16[8,8,4096]{2,1,0:T(8,128)(2,1)} %fusion.9), calls=%async_computation.4 | async-start | bytes 1048576 | tf_op jit(solution)/shard_map/sum/all_to_all | solution.py:154
  249.4 3.3 %copy-start = (f32[96,4096]{1,0:T(8,128)S(1)}, f32[96,4096]{1,0:T(8,128)}, u32[]{:S(2)}) copy-start(f32[96,4096]{1,0:T(8,128)} %fusion.62) | copy-start | bytes 4718596

commit v2 on v1

--- a/solution.py
+++ b/solution.py
@@ -5,9 +5,20 @@
 from jax.sharding import PartitionSpec as P
 
 EXP_COL = 2
-BLOCK = ("yh", "zd")
+NAMES = ("yl", "x", "co", "yh", "za", "zd")
 CHIPS = ("yl", "x")
 LANES = 128
+
+
+def block_groups(yl, xs, yh, za, zd):
+    depth, shift = za * zd, zd // 2
+    groups = []
+    for chip in range(yl * xs):
+        for core in range(2):
+            for first in range(0, depth, zd):
+                zs = [(first + core * shift + step) % depth for step in range(zd)]
+                groups.append([((chip * 2 + core) * yh + hi) * depth + z for hi in range(yh) for z in zs])
+    return groups
 
 
 def per_device(
@@ -22,9 +33,16 @@
     dests = yh * zd
     chips = yl * xs
     kinds = jnp.eye(2, dtype=f32)
+    groups = block_groups(yl, xs, yh, za, zd)
+
+    def exchange(rows_out):
+        return lax.all_to_all(
+            rows_out, NAMES, split_axis=0, concat_axis=0, axis_index_groups=groups, tiled=True
+        )
 
     with jax.named_scope("spread"):
-        meta = jnp.concatenate([expert_ids, slot_ids, gate_units], axis=1).astype(bf16)
+        meta = jnp.concatenate([expert_ids, slot_ids, gate_units], axis=1)
+        meta = lax.optimization_barrier(meta).astype(bf16)
         meta = jnp.pad(meta, ((0, tok_count), (0, LANES - 3 * top_count)))
         block = jnp.concatenate([tokens, grad_out], axis=0)
         spread = lax.all_gather(jnp.concatenate([block, meta], axis=1), "za", axis=0, tiled=True)
@@ -39,7 +57,9 @@
         )
         shares = units / jnp.sum(units, axis=-1, keepdims=True)
         lane = jnp.arange(dests, dtype=jnp.int32)
-        column = (lane // zd) * (za * zd) + lax.axis_index("za") * zd + lane % zd
+        depth, shift = za * zd, lax.axis_index("co") * (zd // 2)
+        own = (lax.axis_index("za") * zd + lax.axis_index("zd") + depth - shift) % depth
+        column = (lane // zd) * depth + (own // zd * zd + shift + lane % zd) % depth
         match = (ids // EXP_COL)[None] == column[:, None, None, None]
         picks = jnp.sum(match.astype(f32), axis=-1)
         pick_share = jnp.sum(jnp.where(match, shares[None], f32(0.0)), axis=-1)
@@ -57,7 +77,8 @@
         slot_rows = jnp.broadcast_to(row_slot[:, None, :, None], (dests, 2, za, LANES))
         slot_rows = slot_rows.reshape(-1, LANES).astype(bf16)
         sending = jnp.concatenate([rows, slot_rows], axis=1).reshape(dests, 2 * za, -1)
-        got = lax.all_to_all(sending, BLOCK, split_axis=0, concat_axis=0, tiled=True)
+        weights = jnp.concatenate([down_weight[0], gate_weight[0].T, up_weight[0].T], axis=0)
+        got, weights = lax.optimization_barrier((exchange(sending), weights))
 
     with jax.named_scope("dispatch"):
         got_slot = got[:, :za, width].astype(jnp.int32)
@@ -80,13 +101,13 @@
         other = lax.ppermute(mine, "co", swap)
 
     with jax.named_scope("expert"):
-        weights = jnp.concatenate([down_weight[0], gate_weight[0].T, up_weight[0].T], axis=0)
         hid = down_weight.shape[1]
 
         def half(rows_in):
             pre = lax.dot_general(
                 rows_in, weights, (((1,), (1,)), ((), ())), preferred_element_type=f32
-            ).reshape(chips, 2, capacity, 3 * hid)
+            )
+            pre = lax.optimization_barrier(pre).reshape(chips, 2, capacity, 3 * hid)
             gate_pre = pre[:, 0, :, hid : 2 * hid]
             up_pre = pre[:, 0, :, 2 * hid :]
             grad_hidden = pre[:, 1, :, :hid]
@@ -110,15 +131,18 @@
         flat_other = other.reshape(chips * 2 * capacity, width)
         mixer_mine, held_mine = half(flat_mine)
         mixer_other, held_other = half(flat_other)
-        part_other = jnp.dot(mixer_other, weights, preferred_element_type=f32).astype(bf16)
-        part_got = lax.ppermute(part_other, "co", swap)
-        part_mine = jnp.dot(mixer_mine, weights, preferred_element_type=f32)
+        pieces, wide = [], width // 2
+        for cut in (slice(0, wide), slice(wide, width)):
+            part_other = jnp.dot(mixer_other, weights[:, cut], preferred_element_type=f32)
+            part_got = lax.ppermute(part_other.astype(bf16), "co", swap)
+            part_mine = jnp.dot(mixer_mine, weights[:, cut], preferred_element_type=f32)
+            pieces.append((part_mine + part_got.astype(f32)).astype(bf16))
         grad_down = lax.dot_general(
             held_mine, flat_mine, (((0,), (0,)), ((), ())), preferred_element_type=f32
         ) + lax.dot_general(
             held_other, flat_other, (((0,), (0,)), ((), ())), preferred_element_type=f32
         )
-        part = (part_mine + part_got.astype(f32)).astype(bf16)
+        part = jnp.concatenate(pieces, axis=1)
 
     with jax.named_scope("combine"):
         parts = lax.all_to_all(
@@ -127,15 +151,14 @@
         gather = jnp.broadcast_to(
             place[:, None], (EXP_COL, xs, 2 * capacity, dests * 2 * za)
         ).reshape(chips * 2 * capacity, -1)
+        gather = lax.optimization_barrier(gather.T.astype(bf16))
         back_rows = lax.dot_general(
-            gather.astype(bf16),
+            gather,
             parts.reshape(chips * 2 * capacity, width),
-            (((0,), (0,)), ((), ())),
+            (((1,), (0,)), ((), ())),
             preferred_element_type=f32,
         ).astype(bf16)
-        home = lax.all_to_all(
-            back_rows.reshape(dests, 2 * za, width), BLOCK, split_axis=0, concat_axis=0, tiled=True
-        ).reshape(dests * 2 * za, width)
+        home = exchange(back_rows.reshape(dests, 2 * za, width)).reshape(dests * 2 * za, width)
 
     with jax.named_scope("sum"):
         weigh = jnp.stack([pick_share, picks], axis=1)
@@ -162,7 +185,7 @@
     columns = mesh.shape["expert"]
     zd = min(4, columns // 4)
     za = columns // (2 * zd)
-    names = ("yl", "x", "co", "yh", "za", "zd")
+    names = NAMES
     chips = mesh.shape["node"] // 4
     fine = Mesh(mesh.devices.reshape(2, chips, 2, 2, za, zd), names)
     node, expert = names[:3], names[3:]

time: 307 us -> 315 us (1.026)
  the two profiles are of different devices: /device:TPU:95 before, /device:TPU:79 now
where the time goes in v2:
time: 315 us; the launch traced here: 314 us
  waiting for transfers between devices  132 us (42%)
  blocking collectives  83.2 us (26%)
  starting transfers between devices  36.8 us (12%)
  matrix products  28.9 us (9%)
  local copies, waits for them, and re-layouts  17.7 us (6%)
  other arithmetic  13.6 us (4%)
    all_gather x1, blocking collectives, per_device(): lax.all_gather(jnp.concatenate([block, meta], axis=1), 'za', axis=0, tile...  49.1 us
    all_to_all x1, waiting for transfers between devices, per_device(): lax.all_to_all(sums.reshape(za, 2 * tok_count, width), 'za', split_axis=0...  48.7 us
    all_to_all x2, waiting for transfers between devices, exchange(): lax.all_to_all(rows_out, NAMES, split_axis=0, concat_axis=0, axis_index_g...  44.2 us
    all_to_all x1, waiting for transfers between devices, per_device(): lax.all_to_all(part.reshape(chips, 2 * capacity, width), CHIPS, split_axi...  38 us
    all_to_all x1, blocking collectives, per_device(): lax.all_to_all(packed.reshape(chips, 2 * capacity, width), CHIPS, split_a...  34.1 us
    all_to_all x1, starting transfers between devices, per_device(): lax.all_to_all(sums.reshape(za, 2 * tok_count, width), 'za', split_axis=0...  11.4 us
    all_to_all x2, starting transfers between devices, exchange(): lax.all_to_all(rows_out, NAMES, split_axis=0, concat_axis=0, axis_index_g...  10.2 us
    optimization_barrier x1, local copies, waits for them, and re-layouts, per_device(): got, weights = lax.optimization_barrier((exchange(sending), weights))  7.4 us
  transfers between devices with their start and end apart: 7, of which 6 were waited for; matrix products, arithmetic and copies ran while one was open for 7% of the time, Pallas kernels for 0%

profile of v2, /device:TPU:79, one launch (start us, length us, event | category | flops | bytes accessed | tf_op | source)
XLA Modules:
  0.0 313.5 jit_solution(6268246855246584927)
XLA Ops:
  2.3 49.1 %all_gather.3 = bf16[64,4224]{1,0:T(8,128)(2,1)S(1)} all-gather(bf16[8,4224]{1,0:T(8,128)(2,1)S(1)} %fusion.47), channel_id=1, replica_groups=mesh['yl'=2,'x'=4,'co'=2,'yh'=2,'za'=8,'zd'=4] {'za'}, dimensions={0}, use_global_device_ids=true | all-gather | bytes 608256 | tf_op jit(solution)/shard_map/spread/all_gather | solution.py:48
  54.1 1.1 pad_maximum_fusion.2
  55.2 5.8 %all-to-all-start = ((bf16[8,16,4224]{2,1,0:T(8,128)(2,1)}), bf16[8,16,4224]{2,1,0:T(8,128)(2,1)S(1)}, u32[]{:S(2)}, u32[]{:S(2)}) async-start(bf16[8,16,4224]{2,1,0:T(8,128)(2,1)} %bitcast.7), calls=%async_computation | async-start | bytes 2162688 | tf_op jit(solution)/shard_map/relay/all_to_all | solution.py:39
  61.0 1.6 pad_maximum_fusion.1
  62.7 21.8 %all-to-all-done = bf16[8,16,4224]{2,1,0:T(8,128)(2,1)S(1)} async-done(((bf16[8,16,4224]{2,1,0:T(8,128)(2,1)}), bf16[8,16,4224]{2,1,0:T(8,128)(2,1)S(1)}, u32[]{:S(2)}, u32[]{:S(2)}) %all-to-all-start) | async-done | bytes 1081376 | tf_op jit(solution)/shard_map/relay/all_to_all | solution.py:39
  84.5 7.4 %copy.103 = bf16[8,16,4224]{1,0,2:T(8,128)(2,1)} copy(bf16[8,16,4224]{2,1,0:T(8,128)(2,1)S(1)} %all-to-all-done) | data formatting | bytes 2162688 | tf_op jit(solution)/shard_map/relay/optimization_barrier | solution.py:81
  94.4 34.1 %all_to_all.25 = bf16[8,40,4096]{2,1,0:T(8,128)(2,1)S(1)} all-to-all(bf16[8,40,4096]{2,1,0:T(8,128)(2,1)S(1)} %bitcast.209), channel_id=1, replica_groups=mesh['yl'=2,'x'=4,'co'=2,'yh'=2,'za'=8,'zd'=4] {'yl','x'}, dimensions={0} | all-to-all | bytes 5242880 | tf_op jit(solution)/shard_map/dispatch/all_to_all | solution.py:97
  128.4 4.0 %collective-permute-start = (bf16[8,40,4096]{2,1,0:T(8,128)(2,1)S(1)}, bf16[8,40,4096]{2,1,0:T(8,128)(2,1)}, u32[]{:S(2)}, u32[]{:S(2)}) collective-permute-start(bf16[8,40,4096]{2,1,0:T(8,128)(2,1)S(1)} %all_to_all.25), channel_id=1, source_target_pairs={{0,64},{64,0},{1,65},{65,1},{2,66},{66,2},{3,67},{67,3},{4,68},{68... | collective-permute-start | bytes 7864328 | tf_op jit(solution)/shard_map/dispatch/ppermute | solution.py:101
  132.5 1.4 fusion.72
  134.9 1.1 reshape.225
  137.1 4.6 %fusion.73 = f32[320,288]{0,1:T(8,128)} fusion(bf16[320,4096]{1,0:T(8,128)(2,1)} %bitcast.25, bf16[288,4096]{1,0:T(8,128)(2,1)} %pad_maximum_fusion.1), kind=kOutput, calls=%fused_computation.145 | convolution fusion | flops 754974720 | bytes 5349376 | tf_op jit(solution)/shard_map/expert/dot_general | solution.py:107
  141.7 2.0 copy.110
  143.7 1.1 reshape.228
  146.7 3.5 %convolution_convert_fusion.3 = bf16[320,2048]{1,0:T(8,128)(2,1)} fusion(bf16[320,288]{1,0:T(8,128)(2,1)} %reshape.229, bf16[288,4096]{1,0:T(8,128)(2,1)} %pad_maximum_fusion.1), kind=kOutput, calls=%fused_computation.8 | convolution fusion | flops 378142720 | bytes 2736128 | tf_op jit(solution)/shard_map/expert/dot_general | solution.py:136
  150.2 2.3 collective-permute-start.1
  152.5 2.9 convolution_convert_fusion.2
  155.3 2.0 collective-permute-start.2
  157.6 2.7 add_convert_fusion.1
  160.6 2.2 add_convert_fusion
  162.8 1.8 pad_maximum_fusion
  164.6 6.9 %all-to-all-start.2 = ((bf16[8,40,4096]{2,1,0:T(8,128)(2,1)}), bf16[8,40,4096]{2,1,0:T(8,128)(2,1)}, u32[]{:S(2)}, u32[]{:S(2)}) async-start(bf16[8,40,4096]{2,1,0:T(8,128)(2,1)} %bitcast.208), calls=%async_computation.2 | async-start | bytes 5242880 | tf_op jit(solution)/shard_map/combine/all_to_all | solution.py:148
  172.2 38.0 %all-to-all-done.2 = bf16[8,40,4096]{2,1,0:T(8,128)(2,1)} async-done(((bf16[8,40,4096]{2,1,0:T(8,128)(2,1)}), bf16[8,40,4096]{2,1,0:T(8,128)(2,1)}, u32[]{:S(2)}, u32[]{:S(2)}) %all-to-all-start.2) | async-done | bytes 2621472 | tf_op jit(solution)/shard_map/combine/all_to_all | solution.py:148
  210.2 3.5 %convolution_convert_fusion = bf16[128,4096]{1,0:T(8,128)(2,1)} fusion(bf16[128,320]{0,1:T(8,128)(2,1)S(1)} %bitcast.216, bf16[320,4096]{1,0:T(8,128)(2,1)} %bitcast.32), kind=kOutput, calls=%fused_computation.2 | convolution fusion | flops 336068608 | bytes 3751936 | tf_op jit(solution)/shard_map/combine/dot_general | solution.py:155
  213.7 4.4 %all-to-all-start.3 = ((bf16[8,16,4096]{2,1,0:T(8,128)(2,1)}), bf16[8,16,4096]{2,1,0:T(8,128)(2,1)}, u32[]{:S(2)}, u32[]{:S(2)}) async-start(bf16[8,16,4096]{2,1,0:T(8,128)(2,1)} %bitcast.210), calls=%async_computation.3 | async-start | bytes 2097152 | tf_op jit(solution)/shard_map/combine/all_to_all | solution.py:39
  219.5 22.4 %all-to-all-done.3 = bf16[8,16,4096]{2,1,0:T(8,128)(2,1)} async-done(((bf16[8,16,4096]{2,1,0:T(8,128)(2,1)}), bf16[8,16,4096]{2,1,0:T(8,128)(2,1)}, u32[]{:S(2)}, u32[]{:S(2)}) %all-to-all-start.3) | async-done | bytes 1048608 | tf_op jit(solution)/shard_map/combine/all_to_all | solution.py:39
  241.9 1.8 fusion.48
  244.7 11.4 %all-to-all-start.4 = ((bf16[8,8,4096]{2,1,0:T(8,128)(2,1)}), bf16[8,8,4096]{2,1,0:T(8,128)(2,1)S(1)}, u32[]{:S(2)}, u32[]{:S(2)}) async-start(bf16[8,8,4096]{2,1,0:T(8,128)(2,1)} %fusion.15), calls=%async_computation.4 | async-start | bytes 1048576 | tf_op jit(solution)/shard_map/sum/all_to_all | solution.py:177
  256.0 1.1 fusion.54
  257.3 1.9 fusion.74
  259.1 1.1 fusion.55
  260.3 3.8 %fusion.2 = bf16[1,96,4096]{2,1,0:T(8,128)(2,1)} fusion(f32[96,4096]{1,0:T(8,128)} %fusion.74, bf16[320,96]{1,0:T(8,128)(2,1)S(1)} %reshape.235, bf16[320,4096]{1,0:T(8,128)(2,1)} %bitcast.25), kind=kOutput, calls=%fused_computation.6 | convolution fusion | flops 252444672 | bytes 5042176 | tf_op jit(solution)/shard_map/expert/dot_general | solution.py:142
  264.1 48.7 %all-to-all-done.4 = bf16[8,8,4096]{2,1,0:T(8,128)(2,1)S(1)} async-done(((bf16[8,8,4096]{2,1,0:T(8,128)(2,1)}), bf16[8,8,4096]{2,1,0:T(8,128)(2,1)S(1)}, u32[]{:S(2)}, u32[]{:S(2)}) %all-to-all-start.4) | async-done | bytes 524320 | tf_op jit(solution)/shard_map/sum/all_to_all | solution.py:177
  (94 shorter events, 15.0 us)
Async XLA Ops:
  54.0 7.0 %copy-start.5 = (bf16[1,4096,96]{1,2,0:T(8,128)(2,1)S(1)}, bf16[1,4096,96]{1,2,0:T(8,128)(2,1)}, u32[]{:S(2)}) copy-start(bf16[1,4096,96]{1,2,0:T(8,128)(2,1)} %param.14) | copy-start | bytes 2359300
  54.0 7.0 %copy-start.6 = (bf16[1,4096,96]{1,2,0:T(8,128)(2,1)S(1)}, bf16[1,4096,96]{1,2,0:T(8,128)(2,1)}, u32[]{:S(2)}) copy-start(bf16[1,4096,96]{1,2,0:T(8,128)(2,1)} %param.13) | copy-start | bytes 2359300
  54.0 7.0 %copy-start.7 = (bf16[1,96,4096]{2,1,0:T(8,128)(2,1)S(1)}, bf16[1,96,4096]{2,1,0:T(8,128)(2,1)}, u32[]{:S(2)}) copy-start(bf16[1,96,4096]{2,1,0:T(8,128)(2,1)} %param.15) | copy-start | bytes 2359300
  55.2 29.3 %all-to-all-start = ((bf16[8,16,4224]{2,1,0:T(8,128)(2,1)}), bf16[8,16,4224]{2,1,0:T(8,128)(2,1)S(1)}, u32[]{:S(2)}, u32[]{:S(2)}) async-start(bf16[8,16,4224]{2,1,0:T(8,128)(2,1)} %bitcast.7), calls=%async_computation | async-start | bytes 2162688 | tf_op jit(solution)/shard_map/relay/all_to_all | solution.py:39
  92.8 0.6 copy-start.8
  94.4 38.1 %copy-start = (bf16[288,4096]{1,0:T(8,128)(2,1)S(1)}, bf16[288,4096]{1,0:T(8,128)(2,1)}, u32[]{:S(2)}) copy-start(bf16[288,4096]{1,0:T(8,128)(2,1)} %pad_maximum_fusion.1) | copy-start | bytes 7077892
  128.4 8.6 %collective-permute-start = (bf16[8,40,4096]{2,1,0:T(8,128)(2,1)S(1)}, bf16[8,40,4096]{2,1,0:T(8,128)(2,1)}, u32[]{:S(2)}, u32[]{:S(2)}) collective-permute-start(bf16[8,40,4096]{2,1,0:T(8,128)(2,1)S(1)} %all_to_all.25), channel_id=1, source_target_pairs={{0,64},{64,0},{1,65},{65,1},{2,66},{66,2},{3,67},{67,3},{4,68},{68... | collective-permute-start | bytes 7864328 | tf_op jit(solution)/shard_map/dispatch/ppermute | solution.py:101
  135.9 5.8 %copy-start.3 = (f32[8,2,20,288]{3,2,1,0:T(8,128)}, f32[8,2,20,288]{3,2,1,0:T(8,128)S(1)}, u32[]{:S(2)}) copy-start(f32[8,2,20,288]{3,2,1,0:T(8,128)S(1)} %reshape.225) | copy-start | bytes 1105924
  144.8 5.4 %copy-start.4 = (f32[8,2,20,288]{3,2,1,0:T(8,128)}, f32[8,2,20,288]{3,2,1,0:T(8,128)S(1)}, u32[]{:S(2)}) copy-start(f32[8,2,20,288]{3,2,1,0:T(8,128)S(1)} %reshape.228) | copy-start | bytes 1105924
  146.7 5.8 %copy-start.1 = (bf16[288,4096]{1,0:T(8,128)(2,1)S(1)}, bf16[288,4096]{1,0:T(8,128)(2,1)}, u32[]{:S(2)}) copy-start(bf16[288,4096]{1,0:T(8,128)(2,1)} %pad_maximum_fusion.1) | copy-start | bytes 7077892
  146.7 10.7 %copy-start.10 = (bf16[8,1,20,288]{3,2,0,1:T(8,128)(2,1)S(1)}, bf16[8,1,20,288]{3,2,0,1:T(8,128)(2,1)}, u32[]{:S(2)}) copy-start(bf16[8,1,20,288]{3,2,0,1:T(8,128)(2,1)} %get-tuple-element.23) | copy-start | bytes 276484
  146.7 10.7 %copy-start.11 = (bf16[8,1,20,288]{3,2,0,1:T(8,128)(2,1)S(1)}, bf16[8,1,20,288]{3,2,0,1:T(8,128)(2,1)}, u32[]{:S(2)}) copy-start(bf16[8,1,20,288]{3,2,0,1:T(8,128)(2,1)} %get-tuple-element.25) | copy-start | bytes 276484
  150.2 7.4 %collective-permute-start.1 = (bf16[320,2048]{1,0:T(8,128)(2,1)}, bf16[320,2048]{1,0:T(8,128)(2,1)}, u32[]{:S(2)}, u32[]{:S(2)}) collective-permute-start(bf16[320,2048]{1,0:T(8,128)(2,1)} %convolution_convert_fusion.3), channel_id=1, source_target_pairs={{0,64},{64,0},{1,65},{65,1},{2,66},{66,2},{3,67},{67,3},{4,68},{68... | collective-permute-start | bytes 3932168 | tf_op jit(solution)/shard_map/expert/ppermute | solution.py:137
  155.3 5.3 %collective-permute-start.2 = (bf16[320,2048]{1,0:T(8,128)(2,1)}, bf16[320,2048]{1,0:T(8,128)(2,1)}, u32[]{:S(2)}, u32[]{:S(2)}) collective-permute-start(bf16[320,2048]{1,0:T(8,128)(2,1)} %convolution_convert_fusion.2), channel_id=1, source_target_pairs={{0,64},{64,0},{1,65},{65,1},{2,66},{66,2},{3,67},{67,3},{4,68},{68... | collective-permute-start | bytes 3932168 | tf_op jit(solution)/shard_map/expert/ppermute | solution.py:137
  157.6 3.0 copy-start.2
  164.6 7.1 %copy-start.9 = (f32[2,20,8,8]{1,0,3,2:T(2,128)S(1)}, f32[2,20,8,8]{1,0,3,2:T(2,128)}, u32[]{:S(2)}) copy-start(f32[2,20,8,8]{1,0,3,2:T(2,128)} %copy-done.8) | copy-start | bytes 30724
  164.6 45.6 %all-to-all-start.2 = ((bf16[8,40,4096]{2,1,0:T(8,128)(2,1)}), bf16[8,40,4096]{2,1,0:T(8,128)(2,1)}, u32[]{:S(2)}, u32[]{:S(2)}) async-start(bf16[8,40,4096]{2,1,0:T(8,128)(2,1)} %bitcast.208), calls=%async_computation.2 | async-start | bytes 5242880 | tf_op jit(solution)/shard_map/combine/all_to_all | solution.py:148
  213.7 28.3 %all-to-all-start.3 = ((bf16[8,16,4096]{2,1,0:T(8,128)(2,1)}), bf16[8,16,4096]{2,1,0:T(8,128)(2,1)}, u32[]{:S(2)}, u32[]{:S(2)}) async-start(bf16[8,16,4096]{2,1,0:T(8,128)(2,1)} %bitcast.210), calls=%async_computation.3 | async-start | bytes 2097152 | tf_op jit(solution)/shard_map/combine/all_to_all | solution.py:39
  244.7 68.1 %all-to-all-start.4 = ((bf16[8,8,4096]{2,1,0:T(8,128)(2,1)}), bf16[8,8,4096]{2,1,0:T(8,128)(2,1)S(1)}, u32[]{:S(2)}, u32[]{:S(2)}) async-start(bf16[8,8,4096]{2,1,0:T(8,128)(2,1)} %fusion.15), calls=%async_computation.4 | async-start | bytes 1048576 | tf_op jit(solution)/shard_map/sum/all_to_all | solution.py:177

commit v3 on v2

--- a/solution.py
+++ b/solution.py
@@ -1,6 +1,10 @@
+import functools
+
 import jax
 import jax.numpy as jnp
 from jax import lax
+from jax.experimental import pallas as pl
+from jax.experimental.pallas import tpu as pltpu
 from jax.sharding import Mesh
 from jax.sharding import PartitionSpec as P
 
@@ -19,6 +23,50 @@
                 zs = [(first + core * shift + step) % depth for step in range(zd)]
                 groups.append([((chip * 2 + core) * yh + hi) * depth + z for hi in range(yh) for z in zs])
     return groups
+
+
+def expert_kernel(capacity, rows_ref, weights_ref, out_ref, held_ref):
+    bf16, f32 = jnp.bfloat16, jnp.float32
+    count, width = rows_ref.shape
+    pre = lax.dot_general(
+        rows_ref[...], weights_ref[...], (((1,), (1,)), ((), ())), preferred_element_type=f32
+    )
+    gate_pre, up_pre = pre[:, LANES : 2 * LANES], pre[:, 2 * LANES :]
+    grad_hidden = pltpu.roll(pre[:, :LANES], count - capacity, 0)
+    row = lax.broadcasted_iota(jnp.int32, (count, LANES), 0)
+    first = lax.rem(row, 2 * capacity) < capacity
+    sigma = 1.0 / (1.0 + jnp.exp(-gate_pre))
+    activ = gate_pre * sigma
+    hidden = jnp.where(first, activ * up_pre, 0.0)
+    dgate = grad_hidden * up_pre * sigma * (1.0 + gate_pre * (1.0 - sigma))
+    dgate = pltpu.roll(jnp.where(first, dgate, 0.0), capacity, 0)
+    dup = pltpu.roll(jnp.where(first, grad_hidden * activ, 0.0), capacity, 0)
+    held_ref[...] = pltpu.roll(hidden, capacity, 0).astype(bf16)
+    mixer = jnp.concatenate([hidden.astype(bf16), dgate.astype(bf16), dup.astype(bf16)], axis=1)
+    step = min(width, 512)
+    for at in range(0, width, step):
+        out_ref[:, at : at + step] = jnp.dot(
+            mixer, weights_ref[:, at : at + step], preferred_element_type=f32
+        ).astype(bf16)
+
+
+def expert_half(rows, weights, capacity):
+    count, width = rows.shape
+    return pl.pallas_call(
+        functools.partial(expert_kernel, capacity),
+        out_shape=(
+            jax.ShapeDtypeStruct((count, width), jnp.bfloat16),
+            jax.ShapeDtypeStruct((count, LANES), jnp.bfloat16),
+        ),
+        in_specs=[pl.BlockSpec(memory_space=pltpu.VMEM)] * 2,
+        out_specs=(pl.BlockSpec(memory_space=pltpu.VMEM),) * 2,
+        compiler_params=pltpu.CompilerParams(vmem_limit_bytes=24 << 20),
+        cost_estimate=pl.CostEstimate(
+            flops=4 * count * width * 3 * LANES,
+            bytes_accessed=4 * count * width + 6 * LANES * width,
+            transcendentals=count * LANES,
+        ),
+    )(rows, weights)
 
 
 def per_device(
@@ -77,11 +125,16 @@
         slot_rows = jnp.broadcast_to(row_slot[:, None, :, None], (dests, 2, za, LANES))
         slot_rows = slot_rows.reshape(-1, LANES).astype(bf16)
         sending = jnp.concatenate([rows, slot_rows], axis=1).reshape(dests, 2 * za, -1)
-        weights = jnp.concatenate([down_weight[0], gate_weight[0].T, up_weight[0].T], axis=0)
-        got, weights = lax.optimization_barrier((exchange(sending), weights))
+        got = exchange(sending)
+        hid = down_weight.shape[1]
+        pad = ((0, LANES - hid), (0, 0))
+        weights = jnp.concatenate(
+            [jnp.pad(w, pad) for w in (down_weight[0], gate_weight[0].T, up_weight[0].T)], axis=0
+        )
+        slot_part, weights = lax.optimization_barrier((got[:, :za, width:], weights))
 
     with jax.named_scope("dispatch"):
-        got_slot = got[:, :za, width].astype(jnp.int32)
+        got_slot = slot_part[:, :, 0].astype(jnp.int32)
         position = jnp.arange(EXP_COL * capacity, dtype=jnp.int32).reshape(EXP_COL, capacity)
         placer = (got_slot[None, None] == position[:, :, None, None]).astype(f32)
         place = (
@@ -101,48 +154,18 @@
         other = lax.ppermute(mine, "co", swap)
 
     with jax.named_scope("expert"):
-        hid = down_weight.shape[1]
-
-        def half(rows_in):
-            pre = lax.dot_general(
-                rows_in, weights, (((1,), (1,)), ((), ())), preferred_element_type=f32
-            )
-            pre = lax.optimization_barrier(pre).reshape(chips, 2, capacity, 3 * hid)
-            gate_pre = pre[:, 0, :, hid : 2 * hid]
-            up_pre = pre[:, 0, :, 2 * hid :]
-            grad_hidden = pre[:, 1, :, :hid]
-            sigma = jax.nn.sigmoid(gate_pre)
-            activ = gate_pre * sigma
-            hidden = (activ * up_pre).astype(bf16)
-            dgate = (grad_hidden * up_pre * sigma * (1.0 + gate_pre * (1.0 - sigma))).astype(bf16)
-            dup = (grad_hidden * activ).astype(bf16)
-            zero = jnp.zeros_like(hidden)
-            mixer = jnp.stack(
-                [
-                    jnp.concatenate([hidden, zero, zero], axis=-1),
-                    jnp.concatenate([zero, dgate, dup], axis=-1),
-                ],
-                axis=1,
-            ).reshape(chips * 2 * capacity, 3 * hid)
-            held = jnp.stack([zero, hidden], axis=1).reshape(chips * 2 * capacity, hid)
-            return mixer, held
-
         flat_mine = mine.reshape(chips * 2 * capacity, width)
         flat_other = other.reshape(chips * 2 * capacity, width)
-        mixer_mine, held_mine = half(flat_mine)
-        mixer_other, held_other = half(flat_other)
-        pieces, wide = [], width // 2
-        for cut in (slice(0, wide), slice(wide, width)):
-            part_other = jnp.dot(mixer_other, weights[:, cut], preferred_element_type=f32)
-            part_got = lax.ppermute(part_other.astype(bf16), "co", swap)
-            part_mine = jnp.dot(mixer_mine, weights[:, cut], preferred_element_type=f32)
-            pieces.append((part_mine + part_got.astype(f32)).astype(bf16))
+        part_mine, held_mine = expert_half(flat_mine, weights, capacity)
+        part_other, held_other = expert_half(flat_other, weights, capacity)
+        part_got = lax.ppermute(part_other, "co", swap)
+        part = (part_mine.astype(f32) + part_got.astype(f32)).astype(bf16)
         grad_down = lax.dot_general(
             held_mine, flat_mine, (((0,), (0,)), ((), ())), preferred_element_type=f32
         ) + lax.dot_general(
             held_other, flat_other, (((0,), (0,)), ((), ())), preferred_element_type=f32
         )
-        part = jnp.concatenate(pieces, axis=1)
+        grad_down = grad_down[:hid]
 
     with jax.named_scope("combine"):
         parts = lax.all_to_all(

time: 315 us -> 289 us (0.917)
  the two profiles are of different devices: /device:TPU:79 before, /device:TPU:71 now
where the time goes in v3:
time: 289 us; the launch traced here: 288 us
  waiting for transfers between devices  139 us (48%)
  blocking collectives  82.8 us (29%)
  starting transfers between devices  35.4 us (12%)
  other arithmetic  11.6 us (4%)
  matrix products  7.58 us (3%)
  Pallas kernels  6.31 us (2%)
  local copies, waits for them, and re-layouts  4.58 us (2%)
    all_to_all x1, waiting for transfers between devices, per_device(): lax.all_to_all(sums.reshape(za, 2 * tok_count, width), 'za', split_axis=0...  50.2 us
    all_gather x1, blocking collectives, per_device(): lax.all_gather(jnp.concatenate([block, meta], axis=1), 'za', axis=0, tile...  49.1 us
    all_to_all x2, waiting for transfers between devices, exchange(): lax.all_to_all(rows_out, NAMES, split_axis=0, concat_axis=0, axis_index_g...  45.3 us
    all_to_all x1, waiting for transfers between devices, per_device(): lax.all_to_all(part.reshape(chips, 2 * capacity, width), CHIPS, split_axi...  37.5 us
    all_to_all x1, blocking collectives, per_device(): lax.all_to_all(packed.reshape(chips, 2 * capacity, width), CHIPS, split_a...  33.6 us
    all_to_all x1, starting transfers between devices, per_device(): lax.all_to_all(sums.reshape(za, 2 * tok_count, width), 'za', split_axis=0...  11.5 us
    all_to_all x2, starting transfers between devices, exchange(): lax.all_to_all(rows_out, NAMES, split_axis=0, concat_axis=0, axis_index_g...  11.2 us
    pallas_call x2, Pallas kernels, expert_half(): pl.pallas_call(functools.partial(expert_kernel, capacity), out_shape=(jax...  6.31 us
  transfers between devices with their start and end apart: 6, of which 6 were waited for; matrix products, arithmetic and copies ran while one was open for 2% of the time, Pallas kernels for 1%

profile of v3, /device:TPU:71, one launch (start us, length us, event | category | flops | bytes accessed | tf_op | source)
XLA Modules:
  0.0 288.2 jit_solution(3593295089816098344)
XLA Ops:
  0.7 0.8 pad_add_fusion
  1.5 0.8 fusion.19
  2.3 49.1 %all_gather.3 = bf16[64,4224]{1,0:T(8,128)(2,1)S(1)} all-gather(bf16[8,4224]{1,0:T(8,128)(2,1)S(1)} %fusion.19), channel_id=1, replica_groups=mesh['yl'=2,'x'=4,'co'=2,'yh'=2,'za'=8,'zd'=4] {'za'}, dimensions={0}, use_global_device_ids=true | all-gather | bytes 608256 | tf_op jit(solution)/shard_map/spread/all_gather | solution.py:96
  51.5 0.6 fusion.29
  53.6 0.5 fusion.4
  54.1 1.1 pad_maximum_fusion
  55.2 6.7 %all-to-all-start = ((bf16[8,16,4224]{2,1,0:T(8,128)(2,1)}), bf16[8,16,4224]{2,1,0:T(8,128)(2,1)S(1)}, u32[]{:S(2)}, u32[]{:S(2)}) async-start(bf16[8,16,4224]{2,1,0:T(8,128)(2,1)} %bitcast.7), calls=%async_computation | async-start | bytes 2162688 | tf_op jit(solution)/shard_map/relay/all_to_all | solution.py:87
  61.9 1.9 fusion.6.weights_ref
  63.9 21.5 %all-to-all-done = bf16[8,16,4224]{2,1,0:T(8,128)(2,1)S(1)} async-done(((bf16[8,16,4224]{2,1,0:T(8,128)(2,1)}), bf16[8,16,4224]{2,1,0:T(8,128)(2,1)S(1)}, u32[]{:S(2)}, u32[]{:S(2)}) %all-to-all-start) | async-done | bytes 1081376 | tf_op jit(solution)/shard_map/relay/all_to_all | solution.py:87
  86.8 33.6 %all_to_all.25 = bf16[8,40,4096]{2,1,0:T(8,128)(2,1)S(1)} all-to-all(bf16[8,40,4096]{2,1,0:T(8,128)(2,1)S(1)} %bitcast.62), channel_id=1, replica_groups=mesh['yl'=2,'x'=4,'co'=2,'yh'=2,'za'=8,'zd'=4] {'yl','x'}, dimensions={0} | all-to-all | bytes 5242880 | tf_op jit(solution)/shard_map/dispatch/all_to_all | solution.py:150
  120.4 4.3 %collective-permute-start = (bf16[8,40,4096]{2,1,0:T(8,128)(2,1)S(1)}, bf16[8,40,4096]{2,1,0:T(8,128)(2,1)S(1)}, u32[]{:S(2)}, u32[]{:S(2)}) collective-permute-start(bf16[8,40,4096]{2,1,0:T(8,128)(2,1)S(1)} %all_to_all.25), channel_id=1, source_target_pairs={{0,64},{64,0},{1,65},{65,1},{2,66},{66,2},{3,67},{67,3},{4,68},{68... | collective-permute-start | bytes 7864328 | tf_op jit(solution)/shard_map/dispatch/ppermute | solution.py:154
  124.7 4.5 %collective-permute-done = bf16[8,40,4096]{2,1,0:T(8,128)(2,1)S(1)} collective-permute-done((bf16[8,40,4096]{2,1,0:T(8,128)(2,1)S(1)}, bf16[8,40,4096]{2,1,0:T(8,128)(2,1)S(1)}, u32[]{:S(2)}, u32[]{:S(2)}) %collective-permute-start) | collective-permute-done | bytes 2621472 | tf_op jit(solution)/shard_map/dispatch/ppermute | solution.py:154
  129.3 3.2 %expert.3 = (bf16[320,4096]{1,0:T(8,128)(2,1)S(1)}, bf16[320,128]{1,0:T(8,128)(2,1)S(1)}) custom-call(bf16[320,4096]{1,0:T(8,128)(2,1)S(1)} %bitcast.60, bf16[384,4096]{1,0:T(8,128)(2,1)S(1)} %copy-done), custom_call_target="tpu_custom_call" | custom-call | flops 2013265920 | bytes 8388608 | tf_op jit(solution)/shard_map/expert/pallas_call | solution.py:55
  132.4 2.3 collective-permute-start.1
  134.7 3.2 %expert.2 = (bf16[320,4096]{1,0:T(8,128)(2,1)S(1)}, bf16[320,128]{1,0:T(8,128)(2,1)S(1)}) custom-call(bf16[320,4096]{1,0:T(8,128)(2,1)S(1)} %bitcast.58, bf16[384,4096]{1,0:T(8,128)(2,1)S(1)} %copy-done), custom_call_target="tpu_custom_call" | custom-call | flops 2013265920 | bytes 8388608 | tf_op jit(solution)/shard_map/expert/pallas_call | solution.py:55
  137.9 1.4 collective-permute-done.1
  139.2 2.7 add_convert_fusion
  141.9 6.1 %all-to-all-start.2 = ((bf16[8,40,4096]{2,1,0:T(8,128)(2,1)}), bf16[8,40,4096]{2,1,0:T(8,128)(2,1)}, u32[]{:S(2)}, u32[]{:S(2)}) async-start(bf16[8,40,4096]{2,1,0:T(8,128)(2,1)} %bitcast.63), calls=%async_computation.2 | async-start | bytes 5242880 | tf_op jit(solution)/shard_map/combine/all_to_all | solution.py:171
  148.8 37.5 %all-to-all-done.2 = bf16[8,40,4096]{2,1,0:T(8,128)(2,1)} async-done(((bf16[8,40,4096]{2,1,0:T(8,128)(2,1)}), bf16[8,40,4096]{2,1,0:T(8,128)(2,1)}, u32[]{:S(2)}, u32[]{:S(2)}) %all-to-all-start.2) | async-done | bytes 2621472 | tf_op jit(solution)/shard_map/combine/all_to_all | solution.py:171
  186.3 3.5 %convolution_convert_fusion = bf16[128,4096]{1,0:T(8,128)(2,1)} fusion(bf16[128,320]{0,1:T(8,128)(2,1)S(1)} %bitcast.70, bf16[320,4096]{1,0:T(8,128)(2,1)} %bitcast.22), kind=kOutput, calls=%fused_computation.11 | convolution fusion | flops 336068608 | bytes 3751936 | tf_op jit(solution)/shard_map/combine/dot_general | solution.py:178
  189.8 4.4 %all-to-all-start.3 = ((bf16[8,16,4096]{2,1,0:T(8,128)(2,1)}), bf16[8,16,4096]{2,1,0:T(8,128)(2,1)}, u32[]{:S(2)}, u32[]{:S(2)}) async-start(bf16[8,16,4096]{2,1,0:T(8,128)(2,1)} %bitcast.64), calls=%async_computation.3 | async-start | bytes 2097152 | tf_op jit(solution)/shard_map/combine/all_to_all | solution.py:87
  195.0 0.7 mul.139
  195.7 23.8 %all-to-all-done.3 = bf16[8,16,4096]{2,1,0:T(8,128)(2,1)} async-done(((bf16[8,16,4096]{2,1,0:T(8,128)(2,1)}), bf16[8,16,4096]{2,1,0:T(8,128)(2,1)}, u32[]{:S(2)}, u32[]{:S(2)}) %all-to-all-start.3) | async-done | bytes 1048608 | tf_op jit(solution)/shard_map/combine/all_to_all | solution.py:87
  219.5 1.8 fusion.20
  221.3 1.0 fusion.11
  222.2 11.5 %all-to-all-start.4 = ((bf16[8,8,4096]{2,1,0:T(8,128)(2,1)}), bf16[8,8,4096]{2,1,0:T(8,128)(2,1)S(1)}, u32[]{:S(2)}, u32[]{:S(2)}) async-start(bf16[8,8,4096]{2,1,0:T(8,128)(2,1)} %fusion.11), calls=%async_computation.4 | async-start | bytes 1048576 | tf_op jit(solution)/shard_map/sum/all_to_all | solution.py:200
  233.7 0.7 fusion.41
  234.5 1.0 copy-done.2
  235.5 0.7 fusion.42
  236.2 1.0 fusion.10
  237.2 50.2 %all-to-all-done.4 = bf16[8,8,4096]{2,1,0:T(8,128)(2,1)S(1)} async-done(((bf16[8,8,4096]{2,1,0:T(8,128)(2,1)}), bf16[8,8,4096]{2,1,0:T(8,128)(2,1)S(1)}, u32[]{:S(2)}, u32[]{:S(2)}) %all-to-all-start.4) | async-done | bytes 524320 | tf_op jit(solution)/shard_map/sum/all_to_all | solution.py:200
  287.6 0.7 fusion.40
  (56 shorter events, 4.4 us)
Async XLA Ops:
  53.5 8.4 %copy-start.3 = (bf16[1,4096,96]{1,2,0:T(8,128)(2,1)S(1)}, bf16[1,4096,96]{1,2,0:T(8,128)(2,1)}, u32[]{:S(2)}) copy-start(bf16[1,4096,96]{1,2,0:T(8,128)(2,1)} %param.14) | copy-start | bytes 2359300
  53.5 8.4 %copy-start.4 = (bf16[1,4096,96]{1,2,0:T(8,128)(2,1)S(1)}, bf16[1,4096,96]{1,2,0:T(8,128)(2,1)}, u32[]{:S(2)}) copy-start(bf16[1,4096,96]{1,2,0:T(8,128)(2,1)} %param.13) | copy-start | bytes 2359300
  53.6 8.4 %copy-start.5 = (bf16[1,96,4096]{2,1,0:T(8,128)(2,1)S(1)}, bf16[1,96,4096]{2,1,0:T(8,128)(2,1)}, u32[]{:S(2)}) copy-start(bf16[1,96,4096]{2,1,0:T(8,128)(2,1)} %param.15) | copy-start | bytes 2359300
  55.2 30.2 %all-to-all-start = ((bf16[8,16,4224]{2,1,0:T(8,128)(2,1)}), bf16[8,16,4224]{2,1,0:T(8,128)(2,1)S(1)}, u32[]{:S(2)}, u32[]{:S(2)}) async-start(bf16[8,16,4224]{2,1,0:T(8,128)(2,1)} %bitcast.7), calls=%async_computation | async-start | bytes 2162688 | tf_op jit(solution)/shard_map/relay/all_to_all | solution.py:87
  86.8 42.5 %copy-start = (bf16[384,4096]{1,0:T(8,128)(2,1)S(1)}, bf16[384,4096]{1,0:T(8,128)(2,1)}, u32[]{:S(2)}) copy-start(bf16[384,4096]{1,0:T(8,128)(2,1)} %fusion.6.weights_ref) | copy-start | bytes 9437188
  120.4 8.8 %collective-permute-start = (bf16[8,40,4096]{2,1,0:T(8,128)(2,1)S(1)}, bf16[8,40,4096]{2,1,0:T(8,128)(2,1)S(1)}, u32[]{:S(2)}, u32[]{:S(2)}) collective-permute-start(bf16[8,40,4096]{2,1,0:T(8,128)(2,1)S(1)} %all_to_all.25), channel_id=1, source_target_pairs={{0,64},{64,0},{1,65},{65,1},{2,66},{66,2},{3,67},{67,3},{4,68},{68... | collective-permute-start | bytes 7864328 | tf_op jit(solution)/shard_map/dispatch/ppermute | solution.py:154
  129.3 3.2 %copy-start.1 = (bf16[8,40,4096]{2,1,0:T(8,128)(2,1)}, bf16[8,40,4096]{2,1,0:T(8,128)(2,1)S(1)}, u32[]{:S(2)}) copy-start(bf16[8,40,4096]{2,1,0:T(8,128)(2,1)S(1)} %collective-permute-done) | copy-start | bytes 7864324
  132.4 6.8 %collective-permute-start.1 = (bf16[320,4096]{1,0:T(8,128)(2,1)S(1)}, bf16[320,4096]{1,0:T(8,128)(2,1)S(1)}, u32[]{:S(2)}, u32[]{:S(2)}) collective-permute-start(bf16[320,4096]{1,0:T(8,128)(2,1)S(1)} %get-tuple-element.12), channel_id=1, source_target_pairs={{0,64},{64,0},{1,65},{65,1},{2,66},{66,2},{3,67},{67,3},{4,68},{68... | collective-permute-start | bytes 7864328 | tf_op jit(solution)/shard_map/expert/ppermute | solution.py:161
  141.9 44.4 %all-to-all-start.2 = ((bf16[8,40,4096]{2,1,0:T(8,128)(2,1)}), bf16[8,40,4096]{2,1,0:T(8,128)(2,1)}, u32[]{:S(2)}, u32[]{:S(2)}) async-start(bf16[8,40,4096]{2,1,0:T(8,128)(2,1)} %bitcast.63), calls=%async_computation.2 | async-start | bytes 5242880 | tf_op jit(solution)/shard_map/combine/all_to_all | solution.py:171
  189.8 29.6 %all-to-all-start.3 = ((bf16[8,16,4096]{2,1,0:T(8,128)(2,1)}), bf16[8,16,4096]{2,1,0:T(8,128)(2,1)}, u32[]{:S(2)}, u32[]{:S(2)}) async-start(bf16[8,16,4096]{2,1,0:T(8,128)(2,1)} %bitcast.64), calls=%async_computation.3 | async-start | bytes 2097152 | tf_op jit(solution)/shard_map/combine/all_to_all | solution.py:87
  222.2 65.3 %all-to-all-start.4 = ((bf16[8,8,4096]{2,1,0:T(8,128)(2,1)}), bf16[8,8,4096]{2,1,0:T(8,128)(2,1)S(1)}, u32[]{:S(2)}, u32[]{:S(2)}) async-start(bf16[8,8,4096]{2,1,0:T(8,128)(2,1)} %fusion.11), calls=%async_computation.4 | async-start | bytes 1048576 | tf_op jit(solution)/shard_map/sum/all_to_all | solution.py:200
  233.7 1.7 copy-start.2

commit v4 on v3

--- a/solution.py
+++ b/solution.py
@@ -22,6 +22,21 @@
             for first in range(0, depth, zd):
                 zs = [(first + core * shift + step) % depth for step in range(zd)]
                 groups.append([((chip * 2 + core) * yh + hi) * depth + z for hi in range(yh) for z in zs])
+    return groups
+
+
+def spread_groups(yl, xs, yh, za, zd):
+    groups = []
+    for chip in range(yl * xs):
+        for core in range(2):
+            for hi in range(yh):
+                for kind in range(zd):
+                    group = []
+                    for step in range(za):
+                        b = (step + core * zd + kind) % za
+                        z = b * zd + (kind if b < za // 2 else kind ^ 1)
+                        group.append(((chip * 2 + core) * yh + hi) * za * zd + z)
+                    groups.append(group)
     return groups
 
 
@@ -82,6 +97,7 @@
     chips = yl * xs
     kinds = jnp.eye(2, dtype=f32)
     groups = block_groups(yl, xs, yh, za, zd)
+    far_groups = spread_groups(yl, xs, yh, za, zd)
 
     def exchange(rows_out):
         return lax.all_to_all(
@@ -93,7 +109,13 @@
         meta = lax.optimization_barrier(meta).astype(bf16)
         meta = jnp.pad(meta, ((0, tok_count), (0, LANES - 3 * top_count)))
         block = jnp.concatenate([tokens, grad_out], axis=0)
-        spread = lax.all_gather(jnp.concatenate([block, meta], axis=1), "za", axis=0, tiled=True)
+        spread = lax.all_gather(
+            jnp.concatenate([block, meta], axis=1),
+            NAMES,
+            axis=0,
+            axis_index_groups=far_groups,
+            tiled=True,
+        )
 
     with jax.named_scope("relay"):
         info = spread[:, width : width + 3 * top_count].reshape(za, 2, tok_count, -1)[:, 0]
@@ -198,7 +220,12 @@
         sums = jnp.dot(split, home, preferred_element_type=f32).reshape(3, -1, width)
         sums = (sums[0] + (sums[1] + sums[2])).astype(bf16)
         blocks = lax.all_to_all(
-            sums.reshape(za, 2 * tok_count, width), "za", split_axis=0, concat_axis=0, tiled=True
+            sums.reshape(za, 2 * tok_count, width),
+            NAMES,
+            split_axis=0,
+            concat_axis=0,
+            axis_index_groups=far_groups,
+            tiled=True,
         )
         total = jnp.sum(blocks.astype(f32), axis=0).astype(bf16)
     return total[:tok_count], total[tok_count:], grad_down.astype(bf16)[None]

time: 289 us -> 285 us (0.986)
  the two profiles are of different devices: /device:TPU:71 before, /device:TPU:14 now
where the time goes in v4:
time: 285 us
  waiting for transfers between devices  129 us (45%)
  blocking collectives  89.1 us (31%)
  starting transfers between devices  35.3 us (12%)
  other arithmetic  11.6 us (4%)
  matrix products  7.6 us (3%)
  Pallas kernels  6.3 us (2%)
  local copies, waits for them, and re-layouts  4.57 us (2%)
    all_gather x1, blocking collectives, per_device(): lax.all_gather(jnp.concatenate([block, meta], axis=1), NAMES, axis=0, axi...  58.8 us
    all_to_all x1, waiting for transfers between devices, per_device(): lax.all_to_all(sums.reshape(za, 2 * tok_count, width), NAMES, split_axis=...  47 us
    all_to_all x1, waiting for transfers between devices, per_device(): lax.all_to_all(part.reshape(chips, 2 * capacity, width), CHIPS, split_axi...  38.1 us
    all_to_all x2, waiting for transfers between devices, exchange(): lax.all_to_all(rows_out, NAMES, split_axis=0, concat_axis=0, axis_index_g...  37.4 us
    all_to_all x1, blocking collectives, per_device(): lax.all_to_all(packed.reshape(chips, 2 * capacity, width), CHIPS, split_a...  30.3 us
    all_to_all x1, starting transfers between devices, per_device(): lax.all_to_all(sums.reshape(za, 2 * tok_count, width), NAMES, split_axis=...  12.5 us
    all_to_all x2, starting transfers between devices, exchange(): lax.all_to_all(rows_out, NAMES, split_axis=0, concat_axis=0, axis_index_g...  12.1 us
    all_to_all x1, starting transfers between devices, per_device(): lax.all_to_all(part.reshape(chips, 2 * capacity, width), CHIPS, split_axi...  6.77 us
  transfers between devices with their start and end apart: 6, of which 6 were waited for; matrix products, arithmetic and copies ran while one was open for 2% of the time, Pallas kernels for 1%

profile of v4, /device:TPU:14, one launch (start us, length us, event | category | flops | bytes accessed | tf_op | source)
XLA Modules:
  0.0 284.6 jit_solution(16948722836164344117)
XLA Ops:
  0.7 0.8 pad_add_fusion
  1.5 0.8 fusion.19
  2.3 58.8 %all_gather.3 = bf16[64,4224]{1,0:T(8,128)(2,1)S(1)} all-gather(bf16[8,4224]{1,0:T(8,128)(2,1)S(1)} %fusion.19), channel_id=1, replica_groups={{0,4,8,12,17,21,25,29},{5,9,13,16,20,24,28,1},{10,14,19,23,27,31,2,6},{..., dimensions={0}, use_global_device_ids=true | all-gather | bytes 608256 | tf_op jit(solution)/shard_map/spread/all_gather | solution.py:112
  61.2 0.6 fusion.29
  63.2 0.5 fusion.4
  63.8 1.1 pad_maximum_fusion
  64.8 4.1 %all-to-all-start = ((bf16[8,16,4224]{2,1,0:T(8,128)(2,1)}), bf16[8,16,4224]{2,1,0:T(8,128)(2,1)S(1)}, u32[]{:S(2)}, u32[]{:S(2)}) async-start(bf16[8,16,4224]{2,1,0:T(8,128)(2,1)} %bitcast.7), calls=%async_computation | async-start | bytes 2162688 | tf_op jit(solution)/shard_map/relay/all_to_all | solution.py:103
  69.0 1.9 fusion.6.weights_ref
  70.9 18.2 %all-to-all-done = bf16[8,16,4224]{2,1,0:T(8,128)(2,1)S(1)} async-done(((bf16[8,16,4224]{2,1,0:T(8,128)(2,1)}), bf16[8,16,4224]{2,1,0:T(8,128)(2,1)S(1)}, u32[]{:S(2)}, u32[]{:S(2)}) %all-to-all-start) | async-done | bytes 1081376 | tf_op jit(solution)/shard_map/relay/all_to_all | solution.py:103
  90.6 30.3 %all_to_all.25 = bf16[8,40,4096]{2,1,0:T(8,128)(2,1)S(1)} all-to-all(bf16[8,40,4096]{2,1,0:T(8,128)(2,1)S(1)} %bitcast.62), channel_id=1, replica_groups=mesh['yl'=2,'x'=4,'co'=2,'yh'=2,'za'=8,'zd'=4] {'yl','x'}, dimensions={0} | all-to-all | bytes 5242880 | tf_op jit(solution)/shard_map/dispatch/all_to_all | solution.py:172
  120.9 1.9 collective-permute-start
  122.8 4.9 %collective-permute-done = bf16[8,40,4096]{2,1,0:T(8,128)(2,1)S(1)} collective-permute-done((bf16[8,40,4096]{2,1,0:T(8,128)(2,1)S(1)}, bf16[8,40,4096]{2,1,0:T(8,128)(2,1)S(1)}, u32[]{:S(2)}, u32[]{:S(2)}) %collective-permute-start) | collective-permute-done | bytes 2621472 | tf_op jit(solution)/shard_map/dispatch/ppermute | solution.py:176
  127.7 3.2 %expert.3 = (bf16[320,4096]{1,0:T(8,128)(2,1)S(1)}, bf16[320,128]{1,0:T(8,128)(2,1)S(1)}) custom-call(bf16[320,4096]{1,0:T(8,128)(2,1)S(1)} %bitcast.60, bf16[384,4096]{1,0:T(8,128)(2,1)S(1)} %copy-done), custom_call_target="tpu_custom_call" | custom-call | flops 2013265920 | bytes 8388608 | tf_op jit(solution)/shard_map/expert/pallas_call | solution.py:70
  130.8 2.0 collective-permute-start.1
  132.9 3.2 %expert.2 = (bf16[320,4096]{1,0:T(8,128)(2,1)S(1)}, bf16[320,128]{1,0:T(8,128)(2,1)S(1)}) custom-call(bf16[320,4096]{1,0:T(8,128)(2,1)S(1)} %bitcast.58, bf16[384,4096]{1,0:T(8,128)(2,1)S(1)} %copy-done), custom_call_target="tpu_custom_call" | custom-call | flops 2013265920 | bytes 8388608 | tf_op jit(solution)/shard_map/expert/pallas_call | solution.py:70
  136.1 1.6 collective-permute-done.1
  137.6 2.7 add_convert_fusion
  140.3 6.8 %all-to-all-start.2 = ((bf16[8,40,4096]{2,1,0:T(8,128)(2,1)}), bf16[8,40,4096]{2,1,0:T(8,128)(2,1)}, u32[]{:S(2)}, u32[]{:S(2)}) async-start(bf16[8,40,4096]{2,1,0:T(8,128)(2,1)} %bitcast.63), calls=%async_computation.2 | async-start | bytes 5242880 | tf_op jit(solution)/shard_map/combine/all_to_all | solution.py:193
  147.8 38.1 %all-to-all-done.2 = bf16[8,40,4096]{2,1,0:T(8,128)(2,1)} async-done(((bf16[8,40,4096]{2,1,0:T(8,128)(2,1)}), bf16[8,40,4096]{2,1,0:T(8,128)(2,1)}, u32[]{:S(2)}, u32[]{:S(2)}) %all-to-all-start.2) | async-done | bytes 2621472 | tf_op jit(solution)/shard_map/combine/all_to_all | solution.py:193
  186.0 3.5 %convolution_convert_fusion = bf16[128,4096]{1,0:T(8,128)(2,1)} fusion(bf16[128,320]{0,1:T(8,128)(2,1)S(1)} %bitcast.70, bf16[320,4096]{1,0:T(8,128)(2,1)} %bitcast.22), kind=kOutput, calls=%fused_computation.11 | convolution fusion | flops 336068608 | bytes 3751936 | tf_op jit(solution)/shard_map/combine/dot_general | solution.py:200
  189.5 8.0 %all-to-all-start.3 = ((bf16[8,16,4096]{2,1,0:T(8,128)(2,1)}), bf16[8,16,4096]{2,1,0:T(8,128)(2,1)}, u32[]{:S(2)}, u32[]{:S(2)}) async-start(bf16[8,16,4096]{2,1,0:T(8,128)(2,1)} %bitcast.64), calls=%async_computation.3 | async-start | bytes 2097152 | tf_op jit(solution)/shard_map/combine/all_to_all | solution.py:103
  198.2 0.7 mul.139
  198.9 19.2 %all-to-all-done.3 = bf16[8,16,4096]{2,1,0:T(8,128)(2,1)} async-done(((bf16[8,16,4096]{2,1,0:T(8,128)(2,1)}), bf16[8,16,4096]{2,1,0:T(8,128)(2,1)}, u32[]{:S(2)}, u32[]{:S(2)}) %all-to-all-start.3) | async-done | bytes 1048608 | tf_op jit(solution)/shard_map/combine/all_to_all | solution.py:103
  218.1 1.8 fusion.20
  219.9 1.0 fusion.11
  220.8 12.5 %all-to-all-start.4 = ((bf16[8,8,4096]{2,1,0:T(8,128)(2,1)}), bf16[8,8,4096]{2,1,0:T(8,128)(2,1)S(1)}, u32[]{:S(2)}, u32[]{:S(2)}) async-start(bf16[8,8,4096]{2,1,0:T(8,128)(2,1)} %fusion.11), calls=%async_computation.4 | async-start | bytes 1048576 | tf_op jit(solution)/shard_map/sum/all_to_all | solution.py:222
  233.3 0.8 fusion.41
  234.1 1.0 copy-done.2
  235.1 0.7 fusion.42
  235.8 1.0 fusion.10
  236.8 47.0 %all-to-all-done.4 = bf16[8,8,4096]{2,1,0:T(8,128)(2,1)S(1)} async-done(((bf16[8,8,4096]{2,1,0:T(8,128)(2,1)}), bf16[8,8,4096]{2,1,0:T(8,128)(2,1)S(1)}, u32[]{:S(2)}, u32[]{:S(2)}) %all-to-all-start.4) | async-done | bytes 524320 | tf_op jit(solution)/shard_map/sum/all_to_all | solution.py:222
  283.9 0.7 fusion.40
  (56 shorter events, 4.4 us)
Async XLA Ops:
  63.2 5.8 %copy-start.3 = (bf16[1,4096,96]{1,2,0:T(8,128)(2,1)S(1)}, bf16[1,4096,96]{1,2,0:T(8,128)(2,1)}, u32[]{:S(2)}) copy-start(bf16[1,4096,96]{1,2,0:T(8,128)(2,1)} %param.14) | copy-start | bytes 2359300
  63.2 5.8 %copy-start.4 = (bf16[1,4096,96]{1,2,0:T(8,128)(2,1)S(1)}, bf16[1,4096,96]{1,2,0:T(8,128)(2,1)}, u32[]{:S(2)}) copy-start(bf16[1,4096,96]{1,2,0:T(8,128)(2,1)} %param.13) | copy-start | bytes 2359300
  63.2 5.8 %copy-start.5 = (bf16[1,96,4096]{2,1,0:T(8,128)(2,1)S(1)}, bf16[1,96,4096]{2,1,0:T(8,128)(2,1)}, u32[]{:S(2)}) copy-start(bf16[1,96,4096]{2,1,0:T(8,128)(2,1)} %param.15) | copy-start | bytes 2359300
  64.8 24.3 %all-to-all-start = ((bf16[8,16,4224]{2,1,0:T(8,128)(2,1)}), bf16[8,16,4224]{2,1,0:T(8,128)(2,1)S(1)}, u32[]{:S(2)}, u32[]{:S(2)}) async-start(bf16[8,16,4224]{2,1,0:T(8,128)(2,1)} %bitcast.7), calls=%async_computation | async-start | bytes 2162688 | tf_op jit(solution)/shard_map/relay/all_to_all | solution.py:103
  90.6 37.1 %copy-start = (bf16[384,4096]{1,0:T(8,128)(2,1)S(1)}, bf16[384,4096]{1,0:T(8,128)(2,1)}, u32[]{:S(2)}) copy-start(bf16[384,4096]{1,0:T(8,128)(2,1)} %fusion.6.weights_ref) | copy-start | bytes 9437188
  120.9 6.8 %collective-permute-start = (bf16[8,40,4096]{2,1,0:T(8,128)(2,1)S(1)}, bf16[8,40,4096]{2,1,0:T(8,128)(2,1)S(1)}, u32[]{:S(2)}, u32[]{:S(2)}) collective-permute-start(bf16[8,40,4096]{2,1,0:T(8,128)(2,1)S(1)} %all_to_all.25), channel_id=1, source_target_pairs={{0,64},{64,0},{1,65},{65,1},{2,66},{66,2},{3,67},{67,3},{4,68},{68... | collective-permute-start | bytes 7864328 | tf_op jit(solution)/shard_map/dispatch/ppermute | solution.py:176
  127.7 3.2 %copy-start.1 = (bf16[8,40,4096]{2,1,0:T(8,128)(2,1)}, bf16[8,40,4096]{2,1,0:T(8,128)(2,1)S(1)}, u32[]{:S(2)}) copy-start(bf16[8,40,4096]{2,1,0:T(8,128)(2,1)S(1)} %collective-permute-done) | copy-start | bytes 7864324
  130.8 6.8 %collective-permute-start.1 = (bf16[320,4096]{1,0:T(8,128)(2,1)S(1)}, bf16[320,4096]{1,0:T(8,128)(2,1)S(1)}, u32[]{:S(2)}, u32[]{:S(2)}) collective-permute-start(bf16[320,4096]{1,0:T(8,128)(2,1)S(1)} %get-tuple-element.12), channel_id=1, source_target_pairs={{0,64},{64,0},{1,65},{65,1},{2,66},{66,2},{3,67},{67,3},{4,68},{68... | collective-permute-start | bytes 7864328 | tf_op jit(solution)/shard_map/expert/ppermute | solution.py:183
  140.3 45.7 %all-to-all-start.2 = ((bf16[8,40,4096]{2,1,0:T(8,128)(2,1)}), bf16[8,40,4096]{2,1,0:T(8,128)(2,1)}, u32[]{:S(2)}, u32[]{:S(2)}) async-start(bf16[8,40,4096]{2,1,0:T(8,128)(2,1)} %bitcast.63), calls=%async_computation.2 | async-start | bytes 5242880 | tf_op jit(solution)/shard_map/combine/all_to_all | solution.py:193
  189.5 28.6 %all-to-all-start.3 = ((bf16[8,16,4096]{2,1,0:T(8,128)(2,1)}), bf16[8,16,4096]{2,1,0:T(8,128)(2,1)}, u32[]{:S(2)}, u32[]{:S(2)}) async-start(bf16[8,16,4096]{2,1,0:T(8,128)(2,1)} %bitcast.64), calls=%async_computation.3 | async-start | bytes 2097152 | tf_op jit(solution)/shard_map/combine/all_to_all | solution.py:103
  220.8 63.0 %all-to-all-start.4 = ((bf16[8,8,4096]{2,1,0:T(8,128)(2,1)}), bf16[8,8,4096]{2,1,0:T(8,128)(2,1)S(1)}, u32[]{:S(2)}, u32[]{:S(2)}) async-start(bf16[8,8,4096]{2,1,0:T(8,128)(2,1)} %fusion.11), calls=%async_computation.4 | async-start | bytes 1048576 | tf_op jit(solution)/shard_map/sum/all_to_all | solution.py:222
  233.3 1.7 copy-start.2

commit v5 on v4

--- a/solution.py
+++ b/solution.py
@@ -40,48 +40,55 @@
     return groups
 
 
-def expert_kernel(capacity, rows_ref, weights_ref, out_ref, held_ref):
+def expert_kernel(capacity, rows_ref, mine_ref, other_ref, out_ref, held_mine_ref, held_other_ref):
     bf16, f32 = jnp.bfloat16, jnp.float32
     count, width = rows_ref.shape
-    pre = lax.dot_general(
-        rows_ref[...], weights_ref[...], (((1,), (1,)), ((), ())), preferred_element_type=f32
-    )
-    gate_pre, up_pre = pre[:, LANES : 2 * LANES], pre[:, 2 * LANES :]
-    grad_hidden = pltpu.roll(pre[:, :LANES], count - capacity, 0)
     row = lax.broadcasted_iota(jnp.int32, (count, LANES), 0)
     first = lax.rem(row, 2 * capacity) < capacity
-    sigma = 1.0 / (1.0 + jnp.exp(-gate_pre))
-    activ = gate_pre * sigma
-    hidden = jnp.where(first, activ * up_pre, 0.0)
-    dgate = grad_hidden * up_pre * sigma * (1.0 + gate_pre * (1.0 - sigma))
-    dgate = pltpu.roll(jnp.where(first, dgate, 0.0), capacity, 0)
-    dup = pltpu.roll(jnp.where(first, grad_hidden * activ, 0.0), capacity, 0)
-    held_ref[...] = pltpu.roll(hidden, capacity, 0).astype(bf16)
-    mixer = jnp.concatenate([hidden.astype(bf16), dgate.astype(bf16), dup.astype(bf16)], axis=1)
+    mixers = []
+    for weights_ref, held_ref in ((mine_ref, held_mine_ref), (other_ref, held_other_ref)):
+        pre = lax.dot_general(
+            rows_ref[...], weights_ref[...], (((1,), (1,)), ((), ())), preferred_element_type=f32
+        )
+        gate_pre, up_pre = pre[:, LANES : 2 * LANES], pre[:, 2 * LANES :]
+        grad_hidden = pltpu.roll(pre[:, :LANES], count - capacity, 0)
+        sigma = 1.0 / (1.0 + jnp.exp(-gate_pre))
+        activ = gate_pre * sigma
+        hidden = jnp.where(first, activ * up_pre, 0.0)
+        dgate = grad_hidden * up_pre * sigma * (1.0 + gate_pre * (1.0 - sigma))
+        dgate = pltpu.roll(jnp.where(first, dgate, 0.0), capacity, 0)
+        dup = pltpu.roll(jnp.where(first, grad_hidden * activ, 0.0), capacity, 0)
+        held_ref[...] = pltpu.roll(hidden, capacity, 0).astype(bf16)
+        mixers.append(
+            jnp.concatenate([hidden.astype(bf16), dgate.astype(bf16), dup.astype(bf16)], axis=1)
+        )
     step = min(width, 512)
     for at in range(0, width, step):
-        out_ref[:, at : at + step] = jnp.dot(
-            mixer, weights_ref[:, at : at + step], preferred_element_type=f32
-        ).astype(bf16)
-
-
-def expert_half(rows, weights, capacity):
+        cut = slice(at, at + step)
+        total = jnp.dot(mixers[0], mine_ref[:, cut], preferred_element_type=f32)
+        total += jnp.dot(mixers[1], other_ref[:, cut], preferred_element_type=f32)
+        out_ref[:, cut] = total.astype(bf16)
+
+
+def expert_pair(rows, mine, other, capacity):
     count, width = rows.shape
+    vmem = pl.BlockSpec(memory_space=pltpu.VMEM)
     return pl.pallas_call(
         functools.partial(expert_kernel, capacity),
         out_shape=(
             jax.ShapeDtypeStruct((count, width), jnp.bfloat16),
             jax.ShapeDtypeStruct((count, LANES), jnp.bfloat16),
+            jax.ShapeDtypeStruct((count, LANES), jnp.bfloat16),
         ),
-        in_specs=[pl.BlockSpec(memory_space=pltpu.VMEM)] * 2,
-        out_specs=(pl.BlockSpec(memory_space=pltpu.VMEM),) * 2,
-        compiler_params=pltpu.CompilerParams(vmem_limit_bytes=24 << 20),
+        in_specs=[vmem] * 3,
+        out_specs=(vmem,) * 3,
+        compiler_params=pltpu.CompilerParams(vmem_limit_bytes=32 << 20),
         cost_estimate=pl.CostEstimate(
-            flops=4 * count * width * 3 * LANES,
-            bytes_accessed=4 * count * width + 6 * LANES * width,
-            transcendentals=count * LANES,
+            flops=8 * count * width * 3 * LANES,
+            bytes_accessed=4 * count * width + 12 * LANES * width,
+            transcendentals=2 * count * LANES,
         ),
-    )(rows, weights)
+    )(rows, mine, other)
 
 
 def per_device(
@@ -153,7 +160,11 @@
         weights = jnp.concatenate(
             [jnp.pad(w, pad) for w in (down_weight[0], gate_weight[0].T, up_weight[0].T)], axis=0
         )
-        slot_part, weights = lax.optimization_barrier((got[:, :za, width:], weights))
+        swap = [(0, 1), (1, 0)]
+        weights_other = lax.ppermute(weights, "co", swap)
+        slot_part, weights, weights_other = lax.optimization_barrier(
+            (got[:, :za, width:], weights, weights_other)
+        )
 
     with jax.named_scope("dispatch"):
         got_slot = slot_part[:, :, 0].astype(jnp.int32)
@@ -172,22 +183,17 @@
         mine = lax.all_to_all(
             packed.reshape(chips, 2 * capacity, width), CHIPS, split_axis=0, concat_axis=0, tiled=True
         )
-        swap = [(0, 1), (1, 0)]
-        other = lax.ppermute(mine, "co", swap)
 
     with jax.named_scope("expert"):
-        flat_mine = mine.reshape(chips * 2 * capacity, width)
-        flat_other = other.reshape(chips * 2 * capacity, width)
-        part_mine, held_mine = expert_half(flat_mine, weights, capacity)
-        part_other, held_other = expert_half(flat_other, weights, capacity)
-        part_got = lax.ppermute(part_other, "co", swap)
-        part = (part_mine.astype(f32) + part_got.astype(f32)).astype(bf16)
-        grad_down = lax.dot_general(
-            held_mine, flat_mine, (((0,), (0,)), ((), ())), preferred_element_type=f32
-        ) + lax.dot_general(
-            held_other, flat_other, (((0,), (0,)), ((), ())), preferred_element_type=f32
-        )
-        grad_down = grad_down[:hid]
+        flat = mine.reshape(chips * 2 * capacity, width)
+        part, held_mine, held_other = expert_pair(flat, weights, weights_other, capacity)
+
+        def down_sum(held):
+            return lax.dot_general(
+                held, flat, (((0,), (0,)), ((), ())), preferred_element_type=f32
+            )[:hid]
+
+        grad_down = down_sum(held_mine) + lax.ppermute(down_sum(held_other), "co", swap)
 
     with jax.named_scope("combine"):
         parts = lax.all_to_all(

time: 285 us -> 277 us (0.972)
  the two profiles are of different devices: /device:TPU:14 before, /device:TPU:30 now
where the time goes in v5:
time: 277 us; the launch traced here: 276 us
  waiting for transfers between devices  96.9 us (35%)
  blocking collectives  91.9 us (33%)
  starting transfers between devices  55.4 us (20%)
  matrix products  8.37 us (3%)
  Pallas kernels  7.79 us (3%)
  other arithmetic  7.78 us (3%)
  local copies, waits for them, and re-layouts  6.99 us (3%)
    all_gather x1, blocking collectives, per_device(): lax.all_gather(jnp.concatenate([block, meta], axis=1), NAMES, axis=0, axi...  58.8 us
    all_to_all x1, waiting for transfers between devices, per_device(): lax.all_to_all(sums.reshape(za, 2 * tok_count, width), NAMES, split_axis=...  37.9 us
    all_to_all x1, blocking collectives, per_device(): lax.all_to_all(packed.reshape(chips, 2 * capacity, width), CHIPS, split_a...  33.2 us
    all_to_all x2, waiting for transfers between devices, exchange(): lax.all_to_all(rows_out, NAMES, split_axis=0, concat_axis=0, axis_index_g...  30.2 us
    all_to_all x1, waiting for transfers between devices, per_device(): lax.all_to_all(part.reshape(chips, 2 * capacity, width), CHIPS, split_axi...  25.8 us
    all_to_all x2, starting transfers between devices, exchange(): lax.all_to_all(rows_out, NAMES, split_axis=0, concat_axis=0, axis_index_g...  23.3 us
    all_to_all x1, starting transfers between devices, per_device(): lax.all_to_all(sums.reshape(za, 2 * tok_count, width), NAMES, split_axis=...  15.2 us
    ppermute x1, starting transfers between devices, per_device(): lax.ppermute(down_sum(held_other), 'co', swap)  8.03 us
  transfers between devices with their start and end apart: 6, of which 5 were waited for; matrix products, arithmetic and copies ran while one was open for 3% of the time, Pallas kernels for 0%

profile of v5, /device:TPU:30, one launch (start us, length us, event | category | flops | bytes accessed | tf_op | source)
XLA Modules:
  0.0 276.2 jit_solution(194361934619434237)
XLA Ops:
  0.7 0.8 pad_add_fusion
  1.5 0.8 fusion.22
  2.3 58.8 %all_gather.3 = bf16[64,4224]{1,0:T(8,128)(2,1)S(1)} all-gather(bf16[8,4224]{1,0:T(8,128)(2,1)S(1)} %fusion.22), channel_id=1, replica_groups={{0,4,8,12,17,21,25,29},{5,9,13,16,20,24,28,1},{10,14,19,23,27,31,2,6},{..., dimensions={0}, use_global_device_ids=true | all-gather | bytes 608256 | tf_op jit(solution)/shard_map/spread/all_gather | solution.py:119
  61.2 0.6 fusion.32
  63.2 0.5 fusion.4
  63.7 1.1 pad_maximum_fusion
  64.8 5.4 %all-to-all-start = ((bf16[8,16,4224]{2,1,0:T(8,128)(2,1)}), bf16[8,16,4224]{2,1,0:T(8,128)(2,1)}, u32[]{:S(2)}, u32[]{:S(2)}) async-start(bf16[8,16,4224]{2,1,0:T(8,128)(2,1)} %bitcast.7), calls=%async_computation | async-start | bytes 2162688 | tf_op jit(solution)/shard_map/relay/all_to_all | solution.py:110
  70.2 1.8 fusion.8.mine_ref
  72.0 1.9 collective-permute-start
  73.9 13.4 %all-to-all-done = bf16[8,16,4224]{2,1,0:T(8,128)(2,1)} async-done(((bf16[8,16,4224]{2,1,0:T(8,128)(2,1)}), bf16[8,16,4224]{2,1,0:T(8,128)(2,1)}, u32[]{:S(2)}, u32[]{:S(2)}) %all-to-all-start) | async-done | bytes 1081376 | tf_op jit(solution)/shard_map/relay/all_to_all | solution.py:110
  87.3 0.7 slice.75
  88.7 1.3 slice.76
  90.0 0.4 convolution_convert_fusion.1
  90.4 0.3 broadcast_in_dim.70
  90.7 33.2 %all_to_all.25 = bf16[8,40,4096]{2,1,0:T(8,128)(2,1)S(1)} all-to-all(bf16[8,40,4096]{2,1,0:T(8,128)(2,1)S(1)} %bitcast.59), channel_id=1, replica_groups=mesh['yl'=2,'x'=4,'co'=2,'yh'=2,'za'=8,'zd'=4] {'yl','x'}, dimensions={0} | all-to-all | bytes 5242880 | tf_op jit(solution)/shard_map/dispatch/all_to_all | solution.py:183
  123.8 7.8 %expert.1 = (bf16[320,4096]{1,0:T(8,128)(2,1)S(1)}, bf16[320,128]{1,0:T(8,128)(2,1)S(1)}, bf16[320,128]{1,0:T(8,128)(2,1)S(1)}) custom-call(bf16[320,4096]{1,0:T(8,128)(2,1)S(1)} %bitcast.55, bf16[384,4096]{1,0:T(8,128)(2,1)S(1)} %copy-done.1, bf16[384,4096]{1,0:T(8,128)(2,1)} %collective-permute-done.other_ref), custom_call_target="tpu_custom_call" | custom-call | flops 4026531840 | bytes 11534336 | tf_op jit(solution)/shard_map/expert/pallas_call | solution.py:76
  131.7 1.5 copy-done.2
  133.2 7.0 %all-to-all-start.2 = ((bf16[8,40,4096]{2,1,0:T(8,128)(2,1)}), bf16[8,40,4096]{2,1,0:T(8,128)(2,1)}, u32[]{:S(2)}, u32[]{:S(2)}) async-start(bf16[8,40,4096]{2,1,0:T(8,128)(2,1)} %bitcast.58), calls=%async_computation.2 | async-start | bytes 5242880 | tf_op jit(solution)/shard_map/combine/all_to_all | solution.py:199
  140.9 25.8 %all-to-all-done.2 = bf16[8,40,4096]{2,1,0:T(8,128)(2,1)} async-done(((bf16[8,40,4096]{2,1,0:T(8,128)(2,1)}), bf16[8,40,4096]{2,1,0:T(8,128)(2,1)}, u32[]{:S(2)}, u32[]{:S(2)}) %all-to-all-start.2) | async-done | bytes 2621472 | tf_op jit(solution)/shard_map/combine/all_to_all | solution.py:199
  166.7 3.5 %convolution_convert_fusion = bf16[128,4096]{1,0:T(8,128)(2,1)} fusion(bf16[128,320]{0,1:T(8,128)(2,1)S(1)} %bitcast.66, bf16[320,4096]{1,0:T(8,128)(2,1)} %bitcast.21), kind=kOutput, calls=%fused_computation.10 | convolution fusion | flops 336068608 | bytes 3751936 | tf_op jit(solution)/shard_map/combine/dot_general | solution.py:206
  170.2 17.9 %all-to-all-start.3 = ((bf16[8,16,4096]{2,1,0:T(8,128)(2,1)}), bf16[8,16,4096]{2,1,0:T(8,128)(2,1)}, u32[]{:S(2)}, u32[]{:S(2)}) async-start(bf16[8,16,4096]{2,1,0:T(8,128)(2,1)} %bitcast.60), calls=%async_computation.3 | async-start | bytes 2097152 | tf_op jit(solution)/shard_map/combine/all_to_all | solution.py:110
  188.8 0.7 mul.139
  189.5 16.8 %all-to-all-done.3 = bf16[8,16,4096]{2,1,0:T(8,128)(2,1)} async-done(((bf16[8,16,4096]{2,1,0:T(8,128)(2,1)}), bf16[8,16,4096]{2,1,0:T(8,128)(2,1)}, u32[]{:S(2)}, u32[]{:S(2)}) %all-to-all-start.3) | async-done | bytes 1048608 | tf_op jit(solution)/shard_map/combine/all_to_all | solution.py:110
  206.3 1.8 fusion.23
  208.1 0.9 fusion.11
  209.1 15.2 %all-to-all-start.4 = ((bf16[8,8,4096]{2,1,0:T(8,128)(2,1)}), bf16[8,8,4096]{2,1,0:T(8,128)(2,1)S(1)}, u32[]{:S(2)}, u32[]{:S(2)}) async-start(bf16[8,8,4096]{2,1,0:T(8,128)(2,1)} %fusion.11), calls=%async_computation.4 | async-start | bytes 1048576 | tf_op jit(solution)/shard_map/sum/all_to_all | solution.py:228
  224.2 0.7 fusion.19
  224.9 8.0 %collective-permute-start.1 = (f32[96,4096]{1,0:T(8,128)S(1)}, f32[96,4096]{1,0:T(8,128)S(1)}, u32[]{:S(2)}, u32[]{:S(2)}) collective-permute-start(f32[96,4096]{1,0:T(8,128)S(1)} %fusion.19), channel_id=1, source_target_pairs={{0,64},{64,0},{1,65},{65,1},{2,66},{66,2},{3,67},{67,3},{4,68},{68... | collective-permute-start | bytes 4718600 | tf_op jit(solution)/shard_map/expert/ppermute | solution.py:196
  233.0 3.0 %collective-permute-done.1 = f32[96,4096]{1,0:T(8,128)S(1)} collective-permute-done((f32[96,4096]{1,0:T(8,128)S(1)}, f32[96,4096]{1,0:T(8,128)S(1)}, u32[]{:S(2)}, u32[]{:S(2)}) %collective-permute-start.1) | collective-permute-done | bytes 1572896 | tf_op jit(solution)/shard_map/expert/ppermute | solution.py:196
  236.0 1.6 fusion.6
  237.6 37.9 %all-to-all-done.4 = bf16[8,8,4096]{2,1,0:T(8,128)(2,1)S(1)} async-done(((bf16[8,8,4096]{2,1,0:T(8,128)(2,1)}), bf16[8,8,4096]{2,1,0:T(8,128)(2,1)S(1)}, u32[]{:S(2)}, u32[]{:S(2)}) %all-to-all-start.4) | async-done | bytes 524320 | tf_op jit(solution)/shard_map/sum/all_to_all | solution.py:228
  275.6 0.7 fusion.43
  (47 shorter events, 3.6 us)
Async XLA Ops:
  64.8 22.5 %all-to-all-start = ((bf16[8,16,4224]{2,1,0:T(8,128)(2,1)}), bf16[8,16,4224]{2,1,0:T(8,128)(2,1)}, u32[]{:S(2)}, u32[]{:S(2)}) async-start(bf16[8,16,4224]{2,1,0:T(8,128)(2,1)} %bitcast.7), calls=%async_computation | async-start | bytes 2162688 | tf_op jit(solution)/shard_map/relay/all_to_all | solution.py:110
  72.0 18.7 %copy-start = (bf16[384,4096]{1,0:T(8,128)(2,1)}, bf16[384,4096]{1,0:T(8,128)(2,1)S(1)}, u32[]{:S(2)}) copy-start(bf16[384,4096]{1,0:T(8,128)(2,1)S(1)} %fusion.8.mine_ref) | copy-start | bytes 9437188
  72.0 16.3 %collective-permute-start = (bf16[384,4096]{1,0:T(8,128)(2,1)S(1)}, bf16[384,4096]{1,0:T(8,128)(2,1)}, u32[]{:S(2)}, u32[]{:S(2)}) collective-permute-start(bf16[384,4096]{1,0:T(8,128)(2,1)S(1)} %fusion.8.mine_ref), channel_id=1, source_target_pairs={{0,64},{64,0},{1,65},{65,1},{2,66},{66,2},{3,67},{67,3},{4,68},{68... | collective-permute-start | bytes 9437192 | tf_op jit(solution)/shard_map/relay/ppermute | solution.py:164
  90.7 33.2 %copy-start.1 = (bf16[384,4096]{1,0:T(8,128)(2,1)S(1)}, bf16[384,4096]{1,0:T(8,128)(2,1)}, u32[]{:S(2)}) copy-start(bf16[384,4096]{1,0:T(8,128)(2,1)} %copy-done) | copy-start | bytes 9437188
  131.6 1.5 copy-start.2
  133.2 33.5 %all-to-all-start.2 = ((bf16[8,40,4096]{2,1,0:T(8,128)(2,1)}), bf16[8,40,4096]{2,1,0:T(8,128)(2,1)}, u32[]{:S(2)}, u32[]{:S(2)}) async-start(bf16[8,40,4096]{2,1,0:T(8,128)(2,1)} %bitcast.58), calls=%async_computation.2 | async-start | bytes 5242880 | tf_op jit(solution)/shard_map/combine/all_to_all | solution.py:199
  170.2 36.2 %all-to-all-start.3 = ((bf16[8,16,4096]{2,1,0:T(8,128)(2,1)}), bf16[8,16,4096]{2,1,0:T(8,128)(2,1)}, u32[]{:S(2)}, u32[]{:S(2)}) async-start(bf16[8,16,4096]{2,1,0:T(8,128)(2,1)} %bitcast.60), calls=%async_computation.3 | async-start | bytes 2097152 | tf_op jit(solution)/shard_map/combine/all_to_all | solution.py:110
  209.1 66.4 %all-to-all-start.4 = ((bf16[8,8,4096]{2,1,0:T(8,128)(2,1)}), bf16[8,8,4096]{2,1,0:T(8,128)(2,1)S(1)}, u32[]{:S(2)}, u32[]{:S(2)}) async-start(bf16[8,8,4096]{2,1,0:T(8,128)(2,1)} %fusion.11), calls=%async_computation.4 | async-start | bytes 1048576 | tf_op jit(solution)/shard_map/sum/all_to_all | solution.py:228
  224.9 11.0 %collective-permute-start.1 = (f32[96,4096]{1,0:T(8,128)S(1)}, f32[96,4096]{1,0:T(8,128)S(1)}, u32[]{:S(2)}, u32[]{:S(2)}) collective-permute-start(f32[96,4096]{1,0:T(8,128)S(1)} %fusion.19), channel_id=1, source_target_pairs={{0,64},{64,0},{1,65},{65,1},{2,66},{66,2},{3,67},{67,3},{4,68},{68... | collective-permute-start | bytes 4718600 | tf_op jit(solution)/shard_map/expert/ppermute | solution.py:196

commit v6 on v4

--- a/solution.py
+++ b/solution.py
@@ -10,7 +10,6 @@
 
 EXP_COL = 2
 NAMES = ("yl", "x", "co", "yh", "za", "zd")
-CHIPS = ("yl", "x")
 LANES = 128
 
 
@@ -40,46 +39,73 @@
     return groups
 
 
-def expert_kernel(capacity, rows_ref, weights_ref, out_ref, held_ref):
+def expert_kernel(capacity, rows_ref, weights_ref, out_ref, held_ref, total_ref):
     bf16, f32 = jnp.bfloat16, jnp.float32
-    count, width = rows_ref.shape
+    width, hid = rows_ref.shape[1], held_ref.shape[0]
+    step_id = pl.program_id(0)
     pre = lax.dot_general(
-        rows_ref[...], weights_ref[...], (((1,), (1,)), ((), ())), preferred_element_type=f32
+        weights_ref[...], rows_ref[...], (((1,), (1,)), ((), ())), preferred_element_type=f32
     )
-    gate_pre, up_pre = pre[:, LANES : 2 * LANES], pre[:, 2 * LANES :]
-    grad_hidden = pltpu.roll(pre[:, :LANES], count - capacity, 0)
-    row = lax.broadcasted_iota(jnp.int32, (count, LANES), 0)
-    first = lax.rem(row, 2 * capacity) < capacity
+    lane = lax.broadcasted_iota(jnp.int32, (hid, LANES), 1)
+    first = lax.rem(lane, 2 * capacity) < capacity
+    grad_hidden = pltpu.roll(pre[:hid], LANES - capacity, 1)
+    gate_pre, up_pre = pre[hid : 2 * hid], pre[2 * hid :]
     sigma = 1.0 / (1.0 + jnp.exp(-gate_pre))
     activ = gate_pre * sigma
     hidden = jnp.where(first, activ * up_pre, 0.0)
     dgate = grad_hidden * up_pre * sigma * (1.0 + gate_pre * (1.0 - sigma))
-    dgate = pltpu.roll(jnp.where(first, dgate, 0.0), capacity, 0)
-    dup = pltpu.roll(jnp.where(first, grad_hidden * activ, 0.0), capacity, 0)
-    held_ref[...] = pltpu.roll(hidden, capacity, 0).astype(bf16)
-    mixer = jnp.concatenate([hidden.astype(bf16), dgate.astype(bf16), dup.astype(bf16)], axis=1)
+    dgate = pltpu.roll(jnp.where(first, dgate, 0.0), capacity, 1)
+    dup = pltpu.roll(jnp.where(first, grad_hidden * activ, 0.0), capacity, 1)
+    held_ref[...] = pltpu.roll(hidden, capacity, 1).astype(bf16)
+    mixer = jnp.concatenate([hidden.astype(bf16), dgate.astype(bf16), dup.astype(bf16)], axis=0)
     step = min(width, 512)
-    for at in range(0, width, step):
-        out_ref[:, at : at + step] = jnp.dot(
-            mixer, weights_ref[:, at : at + step], preferred_element_type=f32
-        ).astype(bf16)
-
-
-def expert_half(rows, weights, capacity):
-    count, width = rows.shape
+
+    def products():
+        for at in range(0, width, step):
+            cut = slice(at, at + step)
+            yield cut, lax.dot_general(
+                mixer, weights_ref[:, cut], (((0,), (0,)), ((), ())), preferred_element_type=f32
+            )
+
+    @pl.when(step_id == 0)
+    def _():
+        for cut, product in products():
+            total_ref[:, cut] = product
+
+    @pl.when(step_id > 0)
+    def _():
+        for cut, product in products():
+            total_ref[:, cut] += product
+
+    @pl.when(step_id == pl.num_programs(0) - 1)
+    def _():
+        out_ref[...] = total_ref[...].astype(bf16)
+
+
+def whole_expert(rows, weights, blocks, capacity):
+    width = rows.shape[1]
+    depth = weights.shape[0] // blocks
     return pl.pallas_call(
         functools.partial(expert_kernel, capacity),
+        grid=(blocks,),
         out_shape=(
-            jax.ShapeDtypeStruct((count, width), jnp.bfloat16),
-            jax.ShapeDtypeStruct((count, LANES), jnp.bfloat16),
+            jax.ShapeDtypeStruct((LANES, width), jnp.bfloat16),
+            jax.ShapeDtypeStruct((blocks * depth // 3, LANES), jnp.bfloat16),
         ),
-        in_specs=[pl.BlockSpec(memory_space=pltpu.VMEM)] * 2,
-        out_specs=(pl.BlockSpec(memory_space=pltpu.VMEM),) * 2,
-        compiler_params=pltpu.CompilerParams(vmem_limit_bytes=24 << 20),
+        in_specs=[
+            pl.BlockSpec((LANES, width), lambda b: (0, 0)),
+            pl.BlockSpec((depth, width), lambda b: (b, 0)),
+        ],
+        out_specs=(
+            pl.BlockSpec((LANES, width), lambda b: (0, 0)),
+            pl.BlockSpec((depth // 3, LANES), lambda b: (b, 0)),
+        ),
+        scratch_shapes=[pltpu.VMEM((LANES, width), jnp.float32)],
+        compiler_params=pltpu.CompilerParams(vmem_limit_bytes=56 << 20),
         cost_estimate=pl.CostEstimate(
-            flops=4 * count * width * 3 * LANES,
-            bytes_accessed=4 * count * width + 6 * LANES * width,
-            transcendentals=count * LANES,
+            flops=4 * LANES * width * blocks * depth,
+            bytes_accessed=2 * blocks * depth * width + 4 * LANES * width,
+            transcendentals=blocks * depth * LANES // 3,
         ),
     )(rows, weights)
 
@@ -94,7 +120,6 @@
     yl, xs = lax.axis_size("yl"), lax.axis_size("x")
     capacity = 5 * tok_count * top_count // 8
     dests = yh * zd
-    chips = yl * xs
     kinds = jnp.eye(2, dtype=f32)
     groups = block_groups(yl, xs, yh, za, zd)
     far_groups = spread_groups(yl, xs, yh, za, zd)
@@ -103,6 +128,10 @@
         return lax.all_to_all(
             rows_out, NAMES, split_axis=0, concat_axis=0, axis_index_groups=groups, tiled=True
         )
+
+    with jax.named_scope("weights"):
+        weights = jnp.concatenate([down_weight[0], gate_weight[0].T, up_weight[0].T], axis=0)
+        weights = lax.all_gather(weights, ("x", "co"), axis=0, tiled=True)
 
     with jax.named_scope("spread"):
         meta = jnp.concatenate([expert_ids, slot_ids, gate_units], axis=1)
@@ -148,16 +177,11 @@
         slot_rows = slot_rows.reshape(-1, LANES).astype(bf16)
         sending = jnp.concatenate([rows, slot_rows], axis=1).reshape(dests, 2 * za, -1)
         got = exchange(sending)
-        hid = down_weight.shape[1]
-        pad = ((0, LANES - hid), (0, 0))
-        weights = jnp.concatenate(
-            [jnp.pad(w, pad) for w in (down_weight[0], gate_weight[0].T, up_weight[0].T)], axis=0
-        )
-        slot_part, weights = lax.optimization_barrier((got[:, :za, width:], weights))
 
     with jax.named_scope("dispatch"):
-        got_slot = slot_part[:, :, 0].astype(jnp.int32)
-        position = jnp.arange(EXP_COL * capacity, dtype=jnp.int32).reshape(EXP_COL, capacity)
+        got_slot = got[:, :za, width].astype(jnp.int32)
+        parity = (lax.axis_index("yl") + jnp.arange(EXP_COL, dtype=jnp.int32)) % EXP_COL
+        position = parity[:, None] * capacity + jnp.arange(capacity, dtype=jnp.int32)
         placer = (got_slot[None, None] == position[:, :, None, None]).astype(f32)
         place = (
             placer[:, None, :, :, None, :] * kinds[None, :, None, None, :, None]
@@ -167,41 +191,23 @@
             got[:, :, :width].reshape(dests * 2 * za, width),
             preferred_element_type=f32,
         ).astype(bf16)
-        packed = packed.reshape(EXP_COL, 1, 2 * capacity, width)
-        packed = jnp.broadcast_to(packed, (EXP_COL, xs, 2 * capacity, width))
-        mine = lax.all_to_all(
-            packed.reshape(chips, 2 * capacity, width), CHIPS, split_axis=0, concat_axis=0, tiled=True
-        )
         swap = [(0, 1), (1, 0)]
-        other = lax.ppermute(mine, "co", swap)
+        half = 2 * capacity
+        theirs = lax.ppermute(packed[half:], "yl", swap)
 
     with jax.named_scope("expert"):
-        flat_mine = mine.reshape(chips * 2 * capacity, width)
-        flat_other = other.reshape(chips * 2 * capacity, width)
-        part_mine, held_mine = expert_half(flat_mine, weights, capacity)
-        part_other, held_other = expert_half(flat_other, weights, capacity)
-        part_got = lax.ppermute(part_other, "co", swap)
-        part = (part_mine.astype(f32) + part_got.astype(f32)).astype(bf16)
-        grad_down = lax.dot_general(
-            held_mine, flat_mine, (((0,), (0,)), ((), ())), preferred_element_type=f32
-        ) + lax.dot_general(
-            held_other, flat_other, (((0,), (0,)), ((), ())), preferred_element_type=f32
-        )
-        grad_down = grad_down[:hid]
+        spare = jnp.zeros((LANES - 2 * half, width), bf16)
+        rows_in = jnp.concatenate([packed[:half], theirs, spare], axis=0)
+        part, held = whole_expert(rows_in, weights, 2 * xs, capacity)
+        down_part = jnp.dot(held, rows_in, preferred_element_type=f32).astype(bf16)
+        grad_down = lax.psum_scatter(down_part, ("x", "co"), scatter_dimension=0, tiled=True)
 
     with jax.named_scope("combine"):
-        parts = lax.all_to_all(
-            part.reshape(chips, 2 * capacity, width), CHIPS, split_axis=0, concat_axis=0, tiled=True
-        )
-        gather = jnp.broadcast_to(
-            place[:, None], (EXP_COL, xs, 2 * capacity, dests * 2 * za)
-        ).reshape(chips * 2 * capacity, -1)
-        gather = lax.optimization_barrier(gather.T.astype(bf16))
-        back_rows = lax.dot_general(
-            gather,
-            parts.reshape(chips * 2 * capacity, width),
-            (((1,), (0,)), ((), ())),
-            preferred_element_type=f32,
+        back = lax.ppermute(part[half : 2 * half], "yl", swap)
+        parts = jnp.concatenate([part[:half], back], axis=0)
+        gather = place.reshape(EXP_COL * half, dests * 2 * za)
+        back_rows = jnp.dot(
+            gather.T.astype(bf16), parts, preferred_element_type=f32
         ).astype(bf16)
         home = exchange(back_rows.reshape(dests, 2 * za, width)).reshape(dests * 2 * za, width)
 

time: 285 us -> 263 us (0.923)
  the two profiles are of different devices: /device:TPU:14 before, /device:TPU:16 now
where the time goes in v6:
time: 263 us; the launch traced here: 262 us
  blocking collectives  126 us (48%)
  waiting for transfers between devices  66.4 us (25%)
  starting transfers between devices  19.6 us (7%)
  Pallas kernels  16.1 us (6%)
  between operations  14.3 us (5%)
  other arithmetic  8.26 us (3%)
  matrix products  7.29 us (3%)
  local copies, waits for them, and re-layouts  4.41 us (2%)
    all_to_all x1, blocking collectives, per_device(): lax.all_to_all(sums.reshape(za, 2 * tok_count, width), NAMES, split_axis=...  66.9 us
    all_gather x1, blocking collectives, per_device(): lax.all_gather(jnp.concatenate([block, meta], axis=1), NAMES, axis=0, axi...  58.8 us
    all_to_all x2, waiting for transfers between devices, exchange(): lax.all_to_all(rows_out, NAMES, split_axis=0, concat_axis=0, axis_index_g...  29.9 us
    all_gather x1, waiting for transfers between devices, per_device(): weights = lax.all_gather(weights, ('x', 'co'), axis=0, tiled=True)  22.1 us
    pallas_call x1, Pallas kernels, whole_expert(): pl.pallas_call(functools.partial(expert_kernel, capacity), grid=(blocks,)...  16.1 us
    all_to_all x2, starting transfers between devices, exchange(): lax.all_to_all(rows_out, NAMES, split_axis=0, concat_axis=0, axis_index_g...  13.1 us
    ppermute x1, waiting for transfers between devices, per_device(): back = lax.ppermute(part[half:2 * half], 'yl', swap)  8.66 us
    ppermute x1, waiting for transfers between devices, per_device(): theirs = lax.ppermute(packed[half:], 'yl', swap)  5.68 us
  transfers between devices with their start and end apart: 6, of which 5 were waited for; matrix products, arithmetic and copies ran while one was open for 5% of the time, Pallas kernels for 0%

profile of v6, /device:TPU:16, one launch (start us, length us, event | category | flops | bytes accessed | tf_op | source)
XLA Modules:
  0.0 262.1 jit_solution(13956141996009724179)
XLA Ops:
  7.2 3.3 %pad_maximum_fusion = bf16[288,4096]{1,0:T(8,128)(2,1)} fusion(bf16[96,4096]{1,0:T(8,128)(2,1)} %bitcast.42, bf16[96,4096]{1,0:T(8,128)(2,1)} %bitcast.43, bf16[96,4096]{1,0:T(8,128)(2,1)} %bitcast.44), kind=kLoop, calls=%fused_computation.5 | loop fusion | flops 7077888 | bytes 4718592 | tf_op jit(solution)/shard_map/weights/concatenate | solution.py:133
  10.6 0.6 copy-done.3
  11.3 58.8 %all_gather.6 = bf16[64,4224]{1,0:T(8,128)(2,1)S(1)} all-gather(bf16[8,4224]{1,0:T(8,128)(2,1)S(1)} %fusion.13), channel_id=1, replica_groups={{0,4,8,12,17,21,25,29},{5,9,13,16,20,24,28,1},{10,14,19,23,27,31,2,6},{..., dimensions={0}, use_global_device_ids=true | all-gather | bytes 608256 | tf_op jit(solution)/shard_map/spread/all_gather | solution.py:141
  70.2 0.6 fusion.23
  70.9 0.2 fusion.9
  71.2 0.3 multiply_convert_fusion
  71.5 0.2 convert_element_type.117
  71.8 0.3 fusion.12
  72.2 0.5 fusion
  72.8 1.1 pad_maximum_fusion.1
  73.9 5.4 %all-to-all-start = ((bf16[8,16,4224]{2,1,0:T(8,128)(2,1)}), bf16[8,16,4224]{2,1,0:T(8,128)(2,1)S(1)}, u32[]{:S(2)}, u32[]{:S(2)}) async-start(bf16[8,16,4224]{2,1,0:T(8,128)(2,1)} %bitcast.7), calls=%async_computation | async-start | bytes 2162688 | tf_op jit(solution)/shard_map/relay/all_to_all | solution.py:128
  79.3 17.0 %all-to-all-done = bf16[8,16,4224]{2,1,0:T(8,128)(2,1)S(1)} async-done(((bf16[8,16,4224]{2,1,0:T(8,128)(2,1)}), bf16[8,16,4224]{2,1,0:T(8,128)(2,1)S(1)}, u32[]{:S(2)}, u32[]{:S(2)}) %all-to-all-start) | async-done | bytes 1081376 | tf_op jit(solution)/shard_map/relay/all_to_all | solution.py:128
  96.6 0.2 multiply_convert_fusion.1
  97.0 0.4 convolution_convert_fusion.2
  97.4 3.2 %collective-permute-start = (bf16[40,4096]{1,0:T(8,128)(2,1)S(1)}, bf16[40,4096]{1,0:T(8,128)(2,1)S(1)}, u32[]{:S(2)}, u32[]{:S(2)}) collective-permute-start(bf16[40,4096]{1,0:T(8,128)(2,1)S(1)} %get-tuple-element.13), channel_id=1, source_target_pairs={{0,512},{512,0},{1,513},{513,1},{2,514},{514,2},{3,515},{515,3},{4... | collective-permute-start | bytes 983048 | tf_op jit(solution)/shard_map/dispatch/ppermute | solution.py:196
  100.7 5.7 %collective-permute-done = bf16[40,4096]{1,0:T(8,128)(2,1)S(1)} collective-permute-done((bf16[40,4096]{1,0:T(8,128)(2,1)S(1)}, bf16[40,4096]{1,0:T(8,128)(2,1)S(1)}, u32[]{:S(2)}, u32[]{:S(2)}) %collective-permute-start) | collective-permute-done | bytes 327712 | tf_op jit(solution)/shard_map/dispatch/ppermute | solution.py:196
  106.4 1.2 maximum_maximum_fusion.rows_ref
  107.5 22.1 %all-gather.2.cloned.1.call-done.weights_ref = bf16[2304,4096]{1,0:T(8,128)(2,1)} async-done(((bf16[288,4096]{1,0:T(8,128)(2,1)}), bf16[2304,4096]{1,0:T(8,128)(2,1)}) %all-gather.2.cloned.1.call-update) | async-done | bytes 18874384 | tf_op jit(solution)/shard_map/weights/all_gather | solution.py:134
  129.7 16.1 %expert.1 = (bf16[128,4096]{1,0:T(8,128)(2,1)}, bf16[768,128]{1,0:T(8,128)(2,1)}) custom-call(bf16[128,4096]{1,0:T(8,128)(2,1)} %maximum_maximum_fusion.rows_ref, bf16[2304,4096]{1,0:T(8,128)(2,1)} %all-gather.2.cloned.1.call-done.weights_ref), custom_call_target="tpu_custom_call" | custom-call | flops 4831838208 | bytes 20971520 | tf_op jit(solution)/shard_map/expert/pallas_call | solution.py:88
  145.8 1.1 fusion.37
  147.0 3.2 %collective-permute-start.1 = (bf16[40,4096]{1,0:T(8,128)(2,1)S(1)}, bf16[40,4096]{1,0:T(8,128)(2,1)S(1)}, u32[]{:S(2)}, u32[]{:S(2)}) collective-permute-start(bf16[40,4096]{1,0:T(8,128)(2,1)S(1)} %get-tuple-element.11), channel_id=1, source_target_pairs={{0,512},{512,0},{1,513},{513,1},{2,514},{514,2},{3,515},{515,3},{4... | collective-permute-start | bytes 983048 | tf_op jit(solution)/shard_map/combine/ppermute | solution.py:206
  150.2 8.7 %collective-permute-done.1 = bf16[40,4096]{1,0:T(8,128)(2,1)S(1)} collective-permute-done((bf16[40,4096]{1,0:T(8,128)(2,1)S(1)}, bf16[40,4096]{1,0:T(8,128)(2,1)S(1)}, u32[]{:S(2)}, u32[]{:S(2)}) %collective-permute-start.1) | collective-permute-done | bytes 327712 | tf_op jit(solution)/shard_map/combine/ppermute | solution.py:206
  158.9 1.4 convolution_convert_fusion.1
  160.3 7.8 %all-to-all-start.1 = ((bf16[8,16,4096]{2,1,0:T(8,128)(2,1)}), bf16[8,16,4096]{2,1,0:T(8,128)(2,1)S(1)}, u32[]{:S(2)}, u32[]{:S(2)}) async-start(bf16[8,16,4096]{2,1,0:T(8,128)(2,1)} %bitcast.15), calls=%async_computation.1 | async-start | bytes 2097152 | tf_op jit(solution)/shard_map/combine/all_to_all | solution.py:128
  168.1 4.5 %convolution_convert_fusion = bf16[768,4096]{1,0:T(8,128)(2,1)} fusion(bf16[768,128]{1,0:T(8,128)(2,1)S(1)} %copy-done, bf16[40,4096]{1,0:T(8,128)(2,1)S(1)} %collective-permute-done, bf16[40,4096]{1,0:T(8,128)(2,1)S(1)} %get-tuple-element.12, bf16[128]{0:T(256)(128)(2,1)S(1)} %pad.13.clone), kind=kOutput, calls=%fused_computation | convolution fusion | flops 811597824 | bytes 7143680 | tf_op jit(solution)/shard_map/expert/dot_general | solution.py:202
  173.0 0.3 broadcast_multiply_fusion
  173.3 0.7 mul.134
  174.0 13.0 %all-to-all-done.1 = bf16[8,16,4096]{2,1,0:T(8,128)(2,1)S(1)} async-done(((bf16[8,16,4096]{2,1,0:T(8,128)(2,1)}), bf16[8,16,4096]{2,1,0:T(8,128)(2,1)S(1)}, u32[]{:S(2)}, u32[]{:S(2)}) %all-to-all-start.1) | async-done | bytes 1048608 | tf_op jit(solution)/shard_map/combine/all_to_all | solution.py:128
  187.0 0.6 fusion.14
  187.5 0.1 fusion.6
  187.7 66.9 %all_to_all.15 = bf16[8,8,4096]{2,1,0:T(8,128)(2,1)S(1)} all-to-all(bf16[8,8,4096]{2,1,0:T(8,128)(2,1)S(1)} %fusion.6), channel_id=1, replica_groups={{0,4,8,12,17,21,25,29},{5,9,13,16,20,24,28,1},{10,14,19,23,27,31,2,6},{..., dimensions={0} | all-to-all | bytes 1048576 | tf_op jit(solution)/shard_map/sum/all_to_all | solution.py:228
  254.6 0.7 fusion.39
  (52 shorter events, 1.9 us)
Async XLA Ops:
  7.2 122.5 %all-gather.2.cloned.1.call-start = ((), (), s32[]{:S(2)}) async-start(), calls=%async_computation.4 | async-start | bytes 21233664 | tf_op jit(solution)/shard_map/weights/all_gather | solution.py:134
  10.5 0.7 copy-start.3
  10.5 0.7 copy-start.4
  10.5 0.7 copy-start.5
  10.5 0.8 copy-start.1
  10.5 0.8 copy-start.2
  73.9 22.4 %all-to-all-start = ((bf16[8,16,4224]{2,1,0:T(8,128)(2,1)}), bf16[8,16,4224]{2,1,0:T(8,128)(2,1)S(1)}, u32[]{:S(2)}, u32[]{:S(2)}) async-start(bf16[8,16,4224]{2,1,0:T(8,128)(2,1)} %bitcast.7), calls=%async_computation | async-start | bytes 2162688 | tf_op jit(solution)/shard_map/relay/all_to_all | solution.py:128
  97.4 9.0 %collective-permute-start = (bf16[40,4096]{1,0:T(8,128)(2,1)S(1)}, bf16[40,4096]{1,0:T(8,128)(2,1)S(1)}, u32[]{:S(2)}, u32[]{:S(2)}) collective-permute-start(bf16[40,4096]{1,0:T(8,128)(2,1)S(1)} %get-tuple-element.13), channel_id=1, source_target_pairs={{0,512},{512,0},{1,513},{513,1},{2,514},{514,2},{3,515},{515,3},{4... | collective-permute-start | bytes 983048 | tf_op jit(solution)/shard_map/dispatch/ppermute | solution.py:196
  147.0 21.1 %copy-start = (bf16[768,128]{1,0:T(8,128)(2,1)S(1)}, bf16[768,128]{1,0:T(8,128)(2,1)}, u32[]{:S(2)}) copy-start(bf16[768,128]{1,0:T(8,128)(2,1)} %get-tuple-element.6) | copy-start | bytes 589828
  147.0 11.9 %collective-permute-start.1 = (bf16[40,4096]{1,0:T(8,128)(2,1)S(1)}, bf16[40,4096]{1,0:T(8,128)(2,1)S(1)}, u32[]{:S(2)}, u32[]{:S(2)}) collective-permute-start(bf16[40,4096]{1,0:T(8,128)(2,1)S(1)} %get-tuple-element.11), channel_id=1, source_target_pairs={{0,512},{512,0},{1,513},{513,1},{2,514},{514,2},{3,515},{515,3},{4... | collective-permute-start | bytes 983048 | tf_op jit(solution)/shard_map/combine/ppermute | solution.py:206
  160.3 26.7 %all-to-all-start.1 = ((bf16[8,16,4096]{2,1,0:T(8,128)(2,1)}), bf16[8,16,4096]{2,1,0:T(8,128)(2,1)S(1)}, u32[]{:S(2)}, u32[]{:S(2)}) async-start(bf16[8,16,4096]{2,1,0:T(8,128)(2,1)} %bitcast.15), calls=%async_computation.1 | async-start | bytes 2097152 | tf_op jit(solution)/shard_map/combine/all_to_all | solution.py:128
  168.1 87.2 %reduce-scatter.2.cloned.1.call-start = ((), (), s32[]{:S(2)}) async-start(), calls=%async_computation.5 | async-start | bytes 7077888 | tf_op jit(solution)/shard_map/expert/reduce_scatter | solution.py:203
Sparse Core Ops, SparseCore 0:
  10.7 118.9 all-gather.1
  172.9 59.9 reduce-scatter.1

commit v7 on v6

--- a/solution.py
+++ b/solution.py
@@ -199,8 +199,6 @@
         spare = jnp.zeros((LANES - 2 * half, width), bf16)
         rows_in = jnp.concatenate([packed[:half], theirs, spare], axis=0)
         part, held = whole_expert(rows_in, weights, 2 * xs, capacity)
-        down_part = jnp.dot(held, rows_in, preferred_element_type=f32).astype(bf16)
-        grad_down = lax.psum_scatter(down_part, ("x", "co"), scatter_dimension=0, tiled=True)
 
     with jax.named_scope("combine"):
         back = lax.ppermute(part[half : 2 * half], "yl", swap)
@@ -209,13 +207,23 @@
         back_rows = jnp.dot(
             gather.T.astype(bf16), parts, preferred_element_type=f32
         ).astype(bf16)
+        back_rows, held = lax.optimization_barrier((back_rows, held))
         home = exchange(back_rows.reshape(dests, 2 * za, width)).reshape(dests * 2 * za, width)
 
+        down_part = jnp.dot(held, rows_in, preferred_element_type=f32).astype(bf16)
+        grad_down = lax.psum_scatter(down_part, ("x", "co"), scatter_dimension=0, tiled=True)
+
     with jax.named_scope("sum"):
+        own_kind = jnp.where(
+            lax.axis_index("za") < za // 2, lax.axis_index("zd"), lax.axis_index("zd") ^ 1
+        )
+        place_far = (lax.axis_index("za") + za - (lax.axis_index("co") * zd + own_kind) % za) % za
+        steps = jnp.arange(za, dtype=jnp.int32)
+        partner = ((place_far ^ steps)[:, None] == steps[None, :]).astype(f32)
         weigh = jnp.stack([pick_share, picks], axis=1)
         weigh = (
-            weigh.transpose(2, 1, 3, 0)[:, :, :, :, None, None]
-            * sources[:, None, None, None, None, :]
+            weigh.transpose(1, 3, 0, 2)[None, :, :, :, None, :]
+            * partner[:, None, None, None, None, :]
             * kinds[None, :, None, None, :, None]
         ).reshape(za * 2 * tok_count, dests * 2 * za)
         high = lax.reduce_precision(weigh, 8, 7)
@@ -225,15 +233,12 @@
         split = jnp.concatenate([high, middle, low], axis=0).astype(bf16)
         sums = jnp.dot(split, home, preferred_element_type=f32).reshape(3, -1, width)
         sums = (sums[0] + (sums[1] + sums[2])).astype(bf16)
-        blocks = lax.all_to_all(
-            sums.reshape(za, 2 * tok_count, width),
-            NAMES,
-            split_axis=0,
-            concat_axis=0,
-            axis_index_groups=far_groups,
-            tiled=True,
-        )
-        total = jnp.sum(blocks.astype(f32), axis=0).astype(bf16)
+        sums = sums.reshape(za, 2 * tok_count, width)
+        blocks = [sums[0]]
+        for step in range(1, za):
+            pairs = [(g[at], g[at ^ step]) for g in far_groups for at in range(za)]
+            blocks.append(lax.ppermute(sums[step], NAMES, pairs))
+        total = sum(b.astype(f32) for b in blocks).astype(bf16)
     return total[:tok_count], total[tok_count:], grad_down.astype(bf16)[None]
 
 

time: 263 us -> 284 us (1.080)
  the two profiles are of different devices: /device:TPU:16 before, /device:TPU:65 now
where the time goes in v7:
time: 284 us; the launch traced here: 283 us
  waiting for transfers between devices  101 us (36%)
  starting transfers between devices  80.8 us (28%)
  blocking collectives  51.1 us (18%)
  Pallas kernels  16.1 us (6%)
  between operations  14.5 us (5%)
  other arithmetic  8.29 us (3%)
  matrix products  7.31 us (3%)
  local copies, waits for them, and re-layouts  4.32 us (2%)
    ppermute x7, starting transfers between devices, per_device(): blocks.append(lax.ppermute(sums[step], NAMES, pairs))  60 us
    all_gather x1, blocking collectives, per_device(): lax.all_gather(jnp.concatenate([block, meta], axis=1), NAMES, axis=0, axi...  51.1 us
    all_to_all x2, waiting for transfers between devices, exchange(): lax.all_to_all(rows_out, NAMES, split_axis=0, concat_axis=0, axis_index_g...  49.4 us
    all_gather x1, waiting for transfers between devices, per_device(): weights = lax.all_gather(weights, ('x', 'co'), axis=0, tiled=True)  20 us
    ppermute x7, waiting for transfers between devices, per_device(): blocks.append(lax.ppermute(sums[step], NAMES, pairs))  17.4 us
    pallas_call x1, Pallas kernels, whole_expert(): pl.pallas_call(functools.partial(expert_kernel, capacity), grid=(blocks,)...  16.1 us
    all_to_all x2, starting transfers between devices, exchange(): lax.all_to_all(rows_out, NAMES, split_axis=0, concat_axis=0, axis_index_g...  15.3 us
    ppermute x1, waiting for transfers between devices, per_device(): back = lax.ppermute(part[half:2 * half], 'yl', swap)  7.83 us
  transfers between devices with their start and end apart: 13, of which 6 were waited for; matrix products, arithmetic and copies ran while one was open for 3% of the time, Pallas kernels for 0%

profile of v7, /device:TPU:65, one launch (start us, length us, event | category | flops | bytes accessed | tf_op | source)
XLA Modules:
  0.0 282.9 jit_solution(16187325121881637557)
XLA Ops:
  7.2 3.2 %pad_maximum_fusion = bf16[288,4096]{1,0:T(8,128)(2,1)} fusion(bf16[96,4096]{1,0:T(8,128)(2,1)} %bitcast.40, bf16[96,4096]{1,0:T(8,128)(2,1)} %bitcast.41, bf16[96,4096]{1,0:T(8,128)(2,1)} %bitcast.42), kind=kLoop, calls=%fused_computation.5 | loop fusion | flops 7077888 | bytes 4718592 | tf_op jit(solution)/shard_map/weights/concatenate | solution.py:133
  10.6 0.6 copy-done.3
  11.3 51.1 %all_gather.6 = bf16[64,4224]{1,0:T(8,128)(2,1)S(1)} all-gather(bf16[8,4224]{1,0:T(8,128)(2,1)S(1)} %fusion.12), channel_id=1, replica_groups={{0,4,8,12,17,21,25,29},{5,9,13,16,20,24,28,1},{10,14,19,23,27,31,2,6},{..., dimensions={0}, use_global_device_ids=true | all-gather | bytes 608256 | tf_op jit(solution)/shard_map/spread/all_gather | solution.py:141
  62.5 0.6 fusion.22
  64.6 0.5 fusion
  65.1 1.1 pad_maximum_fusion.1
  66.2 7.1 %all-to-all-start = ((bf16[8,16,4224]{2,1,0:T(8,128)(2,1)}), bf16[8,16,4224]{2,1,0:T(8,128)(2,1)S(1)}, u32[]{:S(2)}, u32[]{:S(2)}) async-start(bf16[8,16,4224]{2,1,0:T(8,128)(2,1)} %bitcast.7), calls=%async_computation | async-start | bytes 2162688 | tf_op jit(solution)/shard_map/relay/all_to_all | solution.py:128
  73.5 25.6 %all-to-all-done = bf16[8,16,4224]{2,1,0:T(8,128)(2,1)S(1)} async-done(((bf16[8,16,4224]{2,1,0:T(8,128)(2,1)}), bf16[8,16,4224]{2,1,0:T(8,128)(2,1)S(1)}, u32[]{:S(2)}, u32[]{:S(2)}) %all-to-all-start) | async-done | bytes 1081376 | tf_op jit(solution)/shard_map/relay/all_to_all | solution.py:128
  99.7 0.4 convolution_convert_fusion.2
  100.1 2.3 collective-permute-start
  102.5 5.8 %collective-permute-done = bf16[40,4096]{1,0:T(8,128)(2,1)S(1)} collective-permute-done((bf16[40,4096]{1,0:T(8,128)(2,1)S(1)}, bf16[40,4096]{1,0:T(8,128)(2,1)S(1)}, u32[]{:S(2)}, u32[]{:S(2)}) %collective-permute-start) | collective-permute-done | bytes 327712 | tf_op jit(solution)/shard_map/dispatch/ppermute | solution.py:196
  108.4 1.2 maximum_maximum_fusion.rows_ref
  109.6 20.0 %all-gather.2.cloned.1.call-done.weights_ref = bf16[2304,4096]{1,0:T(8,128)(2,1)} async-done(((bf16[288,4096]{1,0:T(8,128)(2,1)}), bf16[2304,4096]{1,0:T(8,128)(2,1)}) %all-gather.2.cloned.1.call-update) | async-done | bytes 18874384 | tf_op jit(solution)/shard_map/weights/all_gather | solution.py:134
  129.6 16.1 %expert.1 = (bf16[128,4096]{1,0:T(8,128)(2,1)}, bf16[768,128]{1,0:T(8,128)(2,1)}) custom-call(bf16[128,4096]{1,0:T(8,128)(2,1)} %maximum_maximum_fusion.rows_ref, bf16[2304,4096]{1,0:T(8,128)(2,1)} %all-gather.2.cloned.1.call-done.weights_ref), custom_call_target="tpu_custom_call" | custom-call | flops 4831838208 | bytes 20971520 | tf_op jit(solution)/shard_map/expert/pallas_call | solution.py:88
  145.7 1.2 fusion.37
  146.8 3.1 %collective-permute-start.1 = (bf16[40,4096]{1,0:T(8,128)(2,1)S(1)}, bf16[40,4096]{1,0:T(8,128)(2,1)S(1)}, u32[]{:S(2)}, u32[]{:S(2)}) collective-permute-start(bf16[40,4096]{1,0:T(8,128)(2,1)S(1)} %get-tuple-element.15), channel_id=1, source_target_pairs={{0,512},{512,0},{1,513},{513,1},{2,514},{514,2},{3,515},{515,3},{4... | collective-permute-start | bytes 983048 | tf_op jit(solution)/shard_map/combine/ppermute | solution.py:204
  150.0 7.8 %collective-permute-done.1 = bf16[40,4096]{1,0:T(8,128)(2,1)S(1)} collective-permute-done((bf16[40,4096]{1,0:T(8,128)(2,1)S(1)}, bf16[40,4096]{1,0:T(8,128)(2,1)S(1)}, u32[]{:S(2)}, u32[]{:S(2)}) %collective-permute-start.1) | collective-permute-done | bytes 327712 | tf_op jit(solution)/shard_map/combine/ppermute | solution.py:204
  157.8 1.4 convolution_convert_fusion.1
  159.2 4.5 %convolution_convert_fusion = bf16[768,4096]{1,0:T(8,128)(2,1)} fusion(bf16[768,128]{1,0:T(8,128)(2,1)S(1)} %copy-done, bf16[40,4096]{1,0:T(8,128)(2,1)S(1)} %collective-permute-done, bf16[40,4096]{1,0:T(8,128)(2,1)S(1)} %get-tuple-element.16, bf16[128]{0:T(256)(128)(2,1)S(1)} %pad.13.clone), kind=kOutput, calls=%fused_computation | convolution fusion | flops 811597824 | bytes 7143680 | tf_op jit(solution)/shard_map/combine/dot_general | solution.py:213
  163.8 8.2 %all-to-all-start.1 = ((bf16[8,16,4096]{2,1,0:T(8,128)(2,1)}), bf16[8,16,4096]{2,1,0:T(8,128)(2,1)S(1)}, u32[]{:S(2)}, u32[]{:S(2)}) async-start(bf16[8,16,4096]{2,1,0:T(8,128)(2,1)} %bitcast.15), calls=%async_computation.1 | async-start | bytes 2097152 | tf_op jit(solution)/shard_map/combine/all_to_all | solution.py:128
  172.5 0.7 mul.138
  173.2 23.9 %all-to-all-done.1 = bf16[8,16,4096]{2,1,0:T(8,128)(2,1)S(1)} async-done(((bf16[8,16,4096]{2,1,0:T(8,128)(2,1)}), bf16[8,16,4096]{2,1,0:T(8,128)(2,1)S(1)}, u32[]{:S(2)}, u32[]{:S(2)}) %all-to-all-start.1) | async-done | bytes 1048608 | tf_op jit(solution)/shard_map/combine/all_to_all | solution.py:128
  197.1 0.6 fusion.13
  197.8 7.4 %collective-permute-start.2 = (bf16[8,4096]{1,0:T(8,128)(2,1)S(1)}, bf16[8,4096]{1,0:T(8,128)(2,1)S(1)}, u32[]{:S(2)}, u32[]{:S(2)}) collective-permute-start(bf16[8,4096]{1,0:T(8,128)(2,1)S(1)} %get-tuple-element.18), channel_id=1, source_target_pairs={{0,4},{4,0},{8,12},{12,8},{17,21},{21,17},{25,29},{29,25},{5,9},{9... | collective-permute-start | bytes 196616 | tf_op jit(solution)/shard_map/sum/ppermute | solution.py:240
  205.2 1.9 collective-permute-start.3
  207.1 6.1 %collective-permute-start.4 = (bf16[8,4096]{1,0:T(8,128)(2,1)S(1)}, bf16[8,4096]{1,0:T(8,128)(2,1)S(1)}, u32[]{:S(2)}, u32[]{:S(2)}) collective-permute-start(bf16[8,4096]{1,0:T(8,128)(2,1)S(1)} %get-tuple-element.23), channel_id=1, source_target_pairs={{0,12},{4,8},{8,4},{12,0},{17,29},{21,25},{25,21},{29,17},{5,16},{... | collective-permute-start | bytes 196616 | tf_op jit(solution)/shard_map/sum/ppermute | solution.py:240
  213.2 16.4 %collective-permute-start.5 = (bf16[8,4096]{1,0:T(8,128)(2,1)S(1)}, bf16[8,4096]{1,0:T(8,128)(2,1)S(1)}, u32[]{:S(2)}, u32[]{:S(2)}) collective-permute-start(bf16[8,4096]{1,0:T(8,128)(2,1)S(1)} %get-tuple-element.22), channel_id=1, source_target_pairs={{0,17},{4,21},{8,25},{12,29},{17,0},{21,4},{25,8},{29,12},{5,20},{... | collective-permute-start | bytes 196616 | tf_op jit(solution)/shard_map/sum/ppermute | solution.py:240
  229.7 11.3 %collective-permute-start.6 = (bf16[8,4096]{1,0:T(8,128)(2,1)S(1)}, bf16[8,4096]{1,0:T(8,128)(2,1)S(1)}, u32[]{:S(2)}, u32[]{:S(2)}) collective-permute-start(bf16[8,4096]{1,0:T(8,128)(2,1)S(1)} %get-tuple-element.21), channel_id=1, source_target_pairs={{0,21},{4,17},{8,29},{12,25},{17,4},{21,0},{25,12},{29,8},{5,24},{... | collective-permute-start | bytes 196616 | tf_op jit(solution)/shard_map/sum/ppermute | solution.py:240
  241.1 7.7 %collective-permute-start.7 = (bf16[8,4096]{1,0:T(8,128)(2,1)S(1)}, bf16[8,4096]{1,0:T(8,128)(2,1)S(1)}, u32[]{:S(2)}, u32[]{:S(2)}) collective-permute-start(bf16[8,4096]{1,0:T(8,128)(2,1)S(1)} %get-tuple-element.20), channel_id=1, source_target_pairs={{0,25},{4,29},{8,17},{12,21},{17,8},{21,12},{25,0},{29,4},{5,28},{... | collective-permute-start | bytes 196616 | tf_op jit(solution)/shard_map/sum/ppermute | solution.py:240
  248.8 9.1 %collective-permute-start.8 = (bf16[8,4096]{1,0:T(8,128)(2,1)S(1)}, bf16[8,4096]{1,0:T(8,128)(2,1)S(1)}, u32[]{:S(2)}, u32[]{:S(2)}) collective-permute-start(bf16[8,4096]{1,0:T(8,128)(2,1)S(1)} %get-tuple-element.19), channel_id=1, source_target_pairs={{0,29},{4,25},{8,21},{12,17},{17,12},{21,8},{25,4},{29,0},{5,1},{9... | collective-permute-start | bytes 196616 | tf_op jit(solution)/shard_map/sum/ppermute | solution.py:240
  258.0 17.4 %collective-permute-done.8 = bf16[8,4096]{1,0:T(8,128)(2,1)S(1)} collective-permute-done((bf16[8,4096]{1,0:T(8,128)(2,1)S(1)}, bf16[8,4096]{1,0:T(8,128)(2,1)S(1)}, u32[]{:S(2)}, u32[]{:S(2)}) %collective-permute-start.8) | collective-permute-done | bytes 65568 | tf_op jit(solution)/shard_map/sum/ppermute | solution.py:240
  275.4 0.7 fusion.40
  (67 shorter events, 3.4 us)
Async XLA Ops:
  7.2 122.4 %all-gather.2.cloned.1.call-start = ((), (), s32[]{:S(2)}) async-start(), calls=%async_computation.3 | async-start | bytes 21233664 | tf_op jit(solution)/shard_map/weights/all_gather | solution.py:134
  10.5 0.7 copy-start.3
  10.5 0.7 copy-start.4
  10.5 0.7 copy-start.5
  10.5 0.8 copy-start.1
  10.5 0.8 copy-start.2
  66.2 32.8 %all-to-all-start = ((bf16[8,16,4224]{2,1,0:T(8,128)(2,1)}), bf16[8,16,4224]{2,1,0:T(8,128)(2,1)S(1)}, u32[]{:S(2)}, u32[]{:S(2)}) async-start(bf16[8,16,4224]{2,1,0:T(8,128)(2,1)} %bitcast.7), calls=%async_computation | async-start | bytes 2162688 | tf_op jit(solution)/shard_map/relay/all_to_all | solution.py:128
  73.3 202.8 %reduce-scatter.2.cloned.1.call-start = ((), (), s32[]{:S(2)}) async-start(), calls=%async_computation.4 | async-start | bytes 7077888 | tf_op jit(solution)/shard_map/combine/reduce_scatter | solution.py:214
  100.1 8.2 %collective-permute-start = (bf16[40,4096]{1,0:T(8,128)(2,1)S(1)}, bf16[40,4096]{1,0:T(8,128)(2,1)S(1)}, u32[]{:S(2)}, u32[]{:S(2)}) collective-permute-start(bf16[40,4096]{1,0:T(8,128)(2,1)S(1)} %get-tuple-element.17), channel_id=1, source_target_pairs={{0,512},{512,0},{1,513},{513,1},{2,514},{514,2},{3,515},{515,3},{4... | collective-permute-start | bytes 983048 | tf_op jit(solution)/shard_map/dispatch/ppermute | solution.py:196
  145.7 13.5 %copy-start = (bf16[768,128]{1,0:T(8,128)(2,1)S(1)}, bf16[768,128]{1,0:T(8,128)(2,1)}, u32[]{:S(2)}) copy-start(bf16[768,128]{1,0:T(8,128)(2,1)} %get-tuple-element.10) | copy-start | bytes 589828
  146.8 11.0 %collective-permute-start.1 = (bf16[40,4096]{1,0:T(8,128)(2,1)S(1)}, bf16[40,4096]{1,0:T(8,128)(2,1)S(1)}, u32[]{:S(2)}, u32[]{:S(2)}) collective-permute-start(bf16[40,4096]{1,0:T(8,128)(2,1)S(1)} %get-tuple-element.15), channel_id=1, source_target_pairs={{0,512},{512,0},{1,513},{513,1},{2,514},{514,2},{3,515},{515,3},{4... | collective-permute-start | bytes 983048 | tf_op jit(solution)/shard_map/combine/ppermute | solution.py:204
  163.8 33.3 %all-to-all-start.1 = ((bf16[8,16,4096]{2,1,0:T(8,128)(2,1)}), bf16[8,16,4096]{2,1,0:T(8,128)(2,1)S(1)}, u32[]{:S(2)}, u32[]{:S(2)}) async-start(bf16[8,16,4096]{2,1,0:T(8,128)(2,1)} %bitcast.15), calls=%async_computation.1 | async-start | bytes 2097152 | tf_op jit(solution)/shard_map/combine/all_to_all | solution.py:128
  197.8 43.2 %collective-permute-start.2 = (bf16[8,4096]{1,0:T(8,128)(2,1)S(1)}, bf16[8,4096]{1,0:T(8,128)(2,1)S(1)}, u32[]{:S(2)}, u32[]{:S(2)}) collective-permute-start(bf16[8,4096]{1,0:T(8,128)(2,1)S(1)} %get-tuple-element.18), channel_id=1, source_target_pairs={{0,4},{4,0},{8,12},{12,8},{17,21},{21,17},{25,29},{29,25},{5,9},{9... | collective-permute-start | bytes 196616 | tf_op jit(solution)/shard_map/sum/ppermute | solution.py:240
  205.2 43.6 %collective-permute-start.3 = (bf16[8,4096]{1,0:T(8,128)(2,1)S(1)}, bf16[8,4096]{1,0:T(8,128)(2,1)S(1)}, u32[]{:S(2)}, u32[]{:S(2)}) collective-permute-start(bf16[8,4096]{1,0:T(8,128)(2,1)S(1)} %get-tuple-element.24), channel_id=1, source_target_pairs={{0,8},{4,12},{8,0},{12,4},{17,25},{21,29},{25,17},{29,21},{5,13},{... | collective-permute-start | bytes 196616 | tf_op jit(solution)/shard_map/sum/ppermute | solution.py:240
  207.1 50.8 %collective-permute-start.4 = (bf16[8,4096]{1,0:T(8,128)(2,1)S(1)}, bf16[8,4096]{1,0:T(8,128)(2,1)S(1)}, u32[]{:S(2)}, u32[]{:S(2)}) collective-permute-start(bf16[8,4096]{1,0:T(8,128)(2,1)S(1)} %get-tuple-element.23), channel_id=1, source_target_pairs={{0,12},{4,8},{8,4},{12,0},{17,29},{21,25},{25,21},{29,17},{5,16},{... | collective-permute-start | bytes 196616 | tf_op jit(solution)/shard_map/sum/ppermute | solution.py:240
  213.2 44.7 %collective-permute-start.5 = (bf16[8,4096]{1,0:T(8,128)(2,1)S(1)}, bf16[8,4096]{1,0:T(8,128)(2,1)S(1)}, u32[]{:S(2)}, u32[]{:S(2)}) collective-permute-start(bf16[8,4096]{1,0:T(8,128)(2,1)S(1)} %get-tuple-element.22), channel_id=1, source_target_pairs={{0,17},{4,21},{8,25},{12,29},{17,0},{21,4},{25,8},{29,12},{5,20},{... | collective-permute-start | bytes 196616 | tf_op jit(solution)/shard_map/sum/ppermute | solution.py:240
  229.7 28.2 %collective-permute-start.6 = (bf16[8,4096]{1,0:T(8,128)(2,1)S(1)}, bf16[8,4096]{1,0:T(8,128)(2,1)S(1)}, u32[]{:S(2)}, u32[]{:S(2)}) collective-permute-start(bf16[8,4096]{1,0:T(8,128)(2,1)S(1)} %get-tuple-element.21), channel_id=1, source_target_pairs={{0,21},{4,17},{8,29},{12,25},{17,4},{21,0},{25,12},{29,8},{5,24},{... | collective-permute-start | bytes 196616 | tf_op jit(solution)/shard_map/sum/ppermute | solution.py:240
  241.1 16.9 %collective-permute-start.7 = (bf16[8,4096]{1,0:T(8,128)(2,1)S(1)}, bf16[8,4096]{1,0:T(8,128)(2,1)S(1)}, u32[]{:S(2)}, u32[]{:S(2)}) collective-permute-start(bf16[8,4096]{1,0:T(8,128)(2,1)S(1)} %get-tuple-element.20), channel_id=1, source_target_pairs={{0,25},{4,29},{8,17},{12,21},{17,8},{21,12},{25,0},{29,4},{5,28},{... | collective-permute-start | bytes 196616 | tf_op jit(solution)/shard_map/sum/ppermute | solution.py:240
  248.8 26.6 %collective-permute-start.8 = (bf16[8,4096]{1,0:T(8,128)(2,1)S(1)}, bf16[8,4096]{1,0:T(8,128)(2,1)S(1)}, u32[]{:S(2)}, u32[]{:S(2)}) collective-permute-start(bf16[8,4096]{1,0:T(8,128)(2,1)S(1)} %get-tuple-element.19), channel_id=1, source_target_pairs={{0,29},{4,25},{8,21},{12,17},{17,12},{21,8},{25,4},{29,0},{5,1},{9... | collective-permute-start | bytes 196616 | tf_op jit(solution)/shard_map/sum/ppermute | solution.py:240
Sparse Core Ops, SparseCore 0:
  10.7 118.8 all-gather.1
  163.9 61.0 reduce-scatter.1

commit v8 on v6

--- a/solution.py
+++ b/solution.py
@@ -11,6 +11,7 @@
 EXP_COL = 2
 NAMES = ("yl", "x", "co", "yh", "za", "zd")
 LANES = 128
+PAIR = 2
 
 
 def block_groups(yl, xs, yh, za, zd):
@@ -41,23 +42,27 @@
 
 def expert_kernel(capacity, rows_ref, weights_ref, out_ref, held_ref, total_ref):
     bf16, f32 = jnp.bfloat16, jnp.float32
-    width, hid = rows_ref.shape[1], held_ref.shape[0]
+    width, hid = rows_ref.shape[1], held_ref.shape[0] // PAIR
     step_id = pl.program_id(0)
-    pre = lax.dot_general(
+    products_in = lax.dot_general(
         weights_ref[...], rows_ref[...], (((1,), (1,)), ((), ())), preferred_element_type=f32
     )
     lane = lax.broadcasted_iota(jnp.int32, (hid, LANES), 1)
     first = lax.rem(lane, 2 * capacity) < capacity
-    grad_hidden = pltpu.roll(pre[:hid], LANES - capacity, 1)
-    gate_pre, up_pre = pre[hid : 2 * hid], pre[2 * hid :]
-    sigma = 1.0 / (1.0 + jnp.exp(-gate_pre))
-    activ = gate_pre * sigma
-    hidden = jnp.where(first, activ * up_pre, 0.0)
-    dgate = grad_hidden * up_pre * sigma * (1.0 + gate_pre * (1.0 - sigma))
-    dgate = pltpu.roll(jnp.where(first, dgate, 0.0), capacity, 1)
-    dup = pltpu.roll(jnp.where(first, grad_hidden * activ, 0.0), capacity, 1)
-    held_ref[...] = pltpu.roll(hidden, capacity, 1).astype(bf16)
-    mixer = jnp.concatenate([hidden.astype(bf16), dgate.astype(bf16), dup.astype(bf16)], axis=0)
+    mixer = []
+    for block in range(PAIR):
+        pre = products_in[block * 3 * hid : (block + 1) * 3 * hid]
+        grad_hidden = pltpu.roll(pre[:hid], LANES - capacity, 1)
+        gate_pre, up_pre = pre[hid : 2 * hid], pre[2 * hid :]
+        sigma = 1.0 / (1.0 + jnp.exp(-gate_pre))
+        activ = gate_pre * sigma
+        hidden = jnp.where(first, activ * up_pre, 0.0)
+        dgate = grad_hidden * up_pre * sigma * (1.0 + gate_pre * (1.0 - sigma))
+        dgate = pltpu.roll(jnp.where(first, dgate, 0.0), capacity, 1)
+        dup = pltpu.roll(jnp.where(first, grad_hidden * activ, 0.0), capacity, 1)
+        held_ref[block * hid : (block + 1) * hid, :] = pltpu.roll(hidden, capacity, 1).astype(bf16)
+        mixer += [hidden.astype(bf16), dgate.astype(bf16), dup.astype(bf16)]
+    mixer = jnp.concatenate(mixer, axis=0)
     step = min(width, 512)
 
     def products():
@@ -87,18 +92,18 @@
     depth = weights.shape[0] // blocks
     return pl.pallas_call(
         functools.partial(expert_kernel, capacity),
-        grid=(blocks,),
+        grid=(blocks // PAIR,),
         out_shape=(
             jax.ShapeDtypeStruct((LANES, width), jnp.bfloat16),
             jax.ShapeDtypeStruct((blocks * depth // 3, LANES), jnp.bfloat16),
         ),
         in_specs=[
             pl.BlockSpec((LANES, width), lambda b: (0, 0)),
-            pl.BlockSpec((depth, width), lambda b: (b, 0)),
+            pl.BlockSpec((PAIR * depth, width), lambda b: (b, 0)),
         ],
         out_specs=(
             pl.BlockSpec((LANES, width), lambda b: (0, 0)),
-            pl.BlockSpec((depth // 3, LANES), lambda b: (b, 0)),
+            pl.BlockSpec((PAIR * depth // 3, LANES), lambda b: (b, 0)),
         ),
         scratch_shapes=[pltpu.VMEM((LANES, width), jnp.float32)],
         compiler_params=pltpu.CompilerParams(vmem_limit_bytes=56 << 20),

time: 263 us -> 260 us (0.989)
  no operation moved by 1% of the time
where the time goes in v8:
time: 260 us
  blocking collectives  126 us (48%)
  waiting for transfers between devices  66.4 us (26%)
  starting transfers between devices  19.6 us (8%)
  between operations  14.3 us (6%)
  Pallas kernels  13.8 us (5%)
  other arithmetic  8.26 us (3%)
  matrix products  7.3 us (3%)
  local copies, waits for them, and re-layouts  4.41 us (2%)
    all_to_all x1, blocking collectives, per_device(): lax.all_to_all(sums.reshape(za, 2 * tok_count, width), NAMES, split_axis=...  66.9 us
    all_gather x1, blocking collectives, per_device(): lax.all_gather(jnp.concatenate([block, meta], axis=1), NAMES, axis=0, axi...  58.8 us
    all_to_all x2, waiting for transfers between devices, exchange(): lax.all_to_all(rows_out, NAMES, split_axis=0, concat_axis=0, axis_index_g...  29.9 us
    all_gather x1, waiting for transfers between devices, per_device(): weights = lax.all_gather(weights, ('x', 'co'), axis=0, tiled=True)  22.1 us
    pallas_call x1, Pallas kernels, whole_expert(): pl.pallas_call(functools.partial(expert_kernel, capacity), grid=(blocks /...  13.8 us
    all_to_all x2, starting transfers between devices, exchange(): lax.all_to_all(rows_out, NAMES, split_axis=0, concat_axis=0, axis_index_g...  13.1 us
    ppermute x1, waiting for transfers between devices, per_device(): back = lax.ppermute(part[half:2 * half], 'yl', swap)  8.66 us
    ppermute x1, waiting for transfers between devices, per_device(): theirs = lax.ppermute(packed[half:], 'yl', swap)  5.68 us
  transfers between devices with their start and end apart: 6, of which 5 were waited for; matrix products, arithmetic and copies ran while one was open for 5% of the time, Pallas kernels for 0%

profile of v8, /device:TPU:16, one launch (start us, length us, event | category | flops | bytes accessed | tf_op | source)
XLA Modules:
  0.0 259.7 jit_solution(2366052998693836767)
XLA Ops:
  7.2 3.3 %pad_maximum_fusion = bf16[288,4096]{1,0:T(8,128)(2,1)} fusion(bf16[96,4096]{1,0:T(8,128)(2,1)} %bitcast.42, bf16[96,4096]{1,0:T(8,128)(2,1)} %bitcast.43, bf16[96,4096]{1,0:T(8,128)(2,1)} %bitcast.44), kind=kLoop, calls=%fused_computation.5 | loop fusion | flops 7077888 | bytes 4718592 | tf_op jit(solution)/shard_map/weights/concatenate | solution.py:138
  10.6 0.6 copy-done.3
  11.3 58.8 %all_gather.6 = bf16[64,4224]{1,0:T(8,128)(2,1)S(1)} all-gather(bf16[8,4224]{1,0:T(8,128)(2,1)S(1)} %fusion.13), channel_id=1, replica_groups={{0,4,8,12,17,21,25,29},{5,9,13,16,20,24,28,1},{10,14,19,23,27,31,2,6},{..., dimensions={0}, use_global_device_ids=true | all-gather | bytes 608256 | tf_op jit(solution)/shard_map/spread/all_gather | solution.py:146
  70.2 0.6 fusion.23
  70.9 0.2 fusion.9
  71.2 0.3 multiply_convert_fusion
  71.5 0.2 convert_element_type.117
  71.8 0.3 fusion.12
  72.2 0.5 fusion
  72.8 1.1 pad_maximum_fusion.1
  73.9 5.4 %all-to-all-start = ((bf16[8,16,4224]{2,1,0:T(8,128)(2,1)}), bf16[8,16,4224]{2,1,0:T(8,128)(2,1)S(1)}, u32[]{:S(2)}, u32[]{:S(2)}) async-start(bf16[8,16,4224]{2,1,0:T(8,128)(2,1)} %bitcast.7), calls=%async_computation | async-start | bytes 2162688 | tf_op jit(solution)/shard_map/relay/all_to_all | solution.py:133
  79.3 17.0 %all-to-all-done = bf16[8,16,4224]{2,1,0:T(8,128)(2,1)S(1)} async-done(((bf16[8,16,4224]{2,1,0:T(8,128)(2,1)}), bf16[8,16,4224]{2,1,0:T(8,128)(2,1)S(1)}, u32[]{:S(2)}, u32[]{:S(2)}) %all-to-all-start) | async-done | bytes 1081376 | tf_op jit(solution)/shard_map/relay/all_to_all | solution.py:133
  96.6 0.2 multiply_convert_fusion.1
  97.0 0.4 convolution_convert_fusion.2
  97.4 3.2 %collective-permute-start = (bf16[40,4096]{1,0:T(8,128)(2,1)S(1)}, bf16[40,4096]{1,0:T(8,128)(2,1)S(1)}, u32[]{:S(2)}, u32[]{:S(2)}) collective-permute-start(bf16[40,4096]{1,0:T(8,128)(2,1)S(1)} %get-tuple-element.13), channel_id=1, source_target_pairs={{0,512},{512,0},{1,513},{513,1},{2,514},{514,2},{3,515},{515,3},{4... | collective-permute-start | bytes 983048 | tf_op jit(solution)/shard_map/dispatch/ppermute | solution.py:201
  100.7 5.7 %collective-permute-done = bf16[40,4096]{1,0:T(8,128)(2,1)S(1)} collective-permute-done((bf16[40,4096]{1,0:T(8,128)(2,1)S(1)}, bf16[40,4096]{1,0:T(8,128)(2,1)S(1)}, u32[]{:S(2)}, u32[]{:S(2)}) %collective-permute-start) | collective-permute-done | bytes 327712 | tf_op jit(solution)/shard_map/dispatch/ppermute | solution.py:201
  106.4 1.2 maximum_maximum_fusion.rows_ref
  107.5 22.1 %all-gather.2.cloned.1.call-done.weights_ref = bf16[2304,4096]{1,0:T(8,128)(2,1)} async-done(((bf16[288,4096]{1,0:T(8,128)(2,1)}), bf16[2304,4096]{1,0:T(8,128)(2,1)}) %all-gather.2.cloned.1.call-update) | async-done | bytes 18874384 | tf_op jit(solution)/shard_map/weights/all_gather | solution.py:139
  129.7 13.8 %expert.1 = (bf16[128,4096]{1,0:T(8,128)(2,1)}, bf16[768,128]{1,0:T(8,128)(2,1)}) custom-call(bf16[128,4096]{1,0:T(8,128)(2,1)} %maximum_maximum_fusion.rows_ref, bf16[2304,4096]{1,0:T(8,128)(2,1)} %all-gather.2.cloned.1.call-done.weights_ref), custom_call_target="tpu_custom_call" | custom-call | flops 4831838208 | bytes 20971520 | tf_op jit(solution)/shard_map/expert/pallas_call | solution.py:93
  143.4 1.1 fusion.37
  144.6 3.2 %collective-permute-start.1 = (bf16[40,4096]{1,0:T(8,128)(2,1)S(1)}, bf16[40,4096]{1,0:T(8,128)(2,1)S(1)}, u32[]{:S(2)}, u32[]{:S(2)}) collective-permute-start(bf16[40,4096]{1,0:T(8,128)(2,1)S(1)} %get-tuple-element.11), channel_id=1, source_target_pairs={{0,512},{512,0},{1,513},{513,1},{2,514},{514,2},{3,515},{515,3},{4... | collective-permute-start | bytes 983048 | tf_op jit(solution)/shard_map/combine/ppermute | solution.py:211
  147.8 8.7 %collective-permute-done.1 = bf16[40,4096]{1,0:T(8,128)(2,1)S(1)} collective-permute-done((bf16[40,4096]{1,0:T(8,128)(2,1)S(1)}, bf16[40,4096]{1,0:T(8,128)(2,1)S(1)}, u32[]{:S(2)}, u32[]{:S(2)}) %collective-permute-start.1) | collective-permute-done | bytes 327712 | tf_op jit(solution)/shard_map/combine/ppermute | solution.py:211
  156.5 1.4 convolution_convert_fusion.1
  157.9 7.8 %all-to-all-start.1 = ((bf16[8,16,4096]{2,1,0:T(8,128)(2,1)}), bf16[8,16,4096]{2,1,0:T(8,128)(2,1)S(1)}, u32[]{:S(2)}, u32[]{:S(2)}) async-start(bf16[8,16,4096]{2,1,0:T(8,128)(2,1)} %bitcast.15), calls=%async_computation.1 | async-start | bytes 2097152 | tf_op jit(solution)/shard_map/combine/all_to_all | solution.py:133
  165.7 4.5 %convolution_convert_fusion = bf16[768,4096]{1,0:T(8,128)(2,1)} fusion(bf16[768,128]{1,0:T(8,128)(2,1)S(1)} %copy-done, bf16[40,4096]{1,0:T(8,128)(2,1)S(1)} %collective-permute-done, bf16[40,4096]{1,0:T(8,128)(2,1)S(1)} %get-tuple-element.12, bf16[128]{0:T(256)(128)(2,1)S(1)} %pad.13.clone), kind=kOutput, calls=%fused_computation | convolution fusion | flops 811597824 | bytes 7143680 | tf_op jit(solution)/shard_map/expert/dot_general | solution.py:207
  170.6 0.3 broadcast_multiply_fusion
  170.9 0.7 mul.134
  171.6 13.0 %all-to-all-done.1 = bf16[8,16,4096]{2,1,0:T(8,128)(2,1)S(1)} async-done(((bf16[8,16,4096]{2,1,0:T(8,128)(2,1)}), bf16[8,16,4096]{2,1,0:T(8,128)(2,1)S(1)}, u32[]{:S(2)}, u32[]{:S(2)}) %all-to-all-start.1) | async-done | bytes 1048608 | tf_op jit(solution)/shard_map/combine/all_to_all | solution.py:133
  184.6 0.6 fusion.14
  185.2 0.1 fusion.6
  185.3 66.9 %all_to_all.15 = bf16[8,8,4096]{2,1,0:T(8,128)(2,1)S(1)} all-to-all(bf16[8,8,4096]{2,1,0:T(8,128)(2,1)S(1)} %fusion.6), channel_id=1, replica_groups={{0,4,8,12,17,21,25,29},{5,9,13,16,20,24,28,1},{10,14,19,23,27,31,2,6},{..., dimensions={0} | all-to-all | bytes 1048576 | tf_op jit(solution)/shard_map/sum/all_to_all | solution.py:233
  252.3 0.7 fusion.39
  (52 shorter events, 1.9 us)
Async XLA Ops:
  7.2 122.5 %all-gather.2.cloned.1.call-start = ((), (), s32[]{:S(2)}) async-start(), calls=%async_computation.4 | async-start | bytes 21233664 | tf_op jit(solution)/shard_map/weights/all_gather | solution.py:139
  10.5 0.7 copy-start.3
  10.5 0.7 copy-start.4
  10.5 0.7 copy-start.5
  10.5 0.8 copy-start.1
  10.5 0.8 copy-start.2
  73.9 22.4 %all-to-all-start = ((bf16[8,16,4224]{2,1,0:T(8,128)(2,1)}), bf16[8,16,4224]{2,1,0:T(8,128)(2,1)S(1)}, u32[]{:S(2)}, u32[]{:S(2)}) async-start(bf16[8,16,4224]{2,1,0:T(8,128)(2,1)} %bitcast.7), calls=%async_computation | async-start | bytes 2162688 | tf_op jit(solution)/shard_map/relay/all_to_all | solution.py:133
  97.4 9.0 %collective-permute-start = (bf16[40,4096]{1,0:T(8,128)(2,1)S(1)}, bf16[40,4096]{1,0:T(8,128)(2,1)S(1)}, u32[]{:S(2)}, u32[]{:S(2)}) collective-permute-start(bf16[40,4096]{1,0:T(8,128)(2,1)S(1)} %get-tuple-element.13), channel_id=1, source_target_pairs={{0,512},{512,0},{1,513},{513,1},{2,514},{514,2},{3,515},{515,3},{4... | collective-permute-start | bytes 983048 | tf_op jit(solution)/shard_map/dispatch/ppermute | solution.py:201
  144.6 21.1 %copy-start = (bf16[768,128]{1,0:T(8,128)(2,1)S(1)}, bf16[768,128]{1,0:T(8,128)(2,1)}, u32[]{:S(2)}) copy-start(bf16[768,128]{1,0:T(8,128)(2,1)} %get-tuple-element.6) | copy-start | bytes 589828
  144.6 11.9 %collective-permute-start.1 = (bf16[40,4096]{1,0:T(8,128)(2,1)S(1)}, bf16[40,4096]{1,0:T(8,128)(2,1)S(1)}, u32[]{:S(2)}, u32[]{:S(2)}) collective-permute-start(bf16[40,4096]{1,0:T(8,128)(2,1)S(1)} %get-tuple-element.11), channel_id=1, source_target_pairs={{0,512},{512,0},{1,513},{513,1},{2,514},{514,2},{3,515},{515,3},{4... | collective-permute-start | bytes 983048 | tf_op jit(solution)/shard_map/combine/ppermute | solution.py:211
  157.9 26.7 %all-to-all-start.1 = ((bf16[8,16,4096]{2,1,0:T(8,128)(2,1)}), bf16[8,16,4096]{2,1,0:T(8,128)(2,1)S(1)}, u32[]{:S(2)}, u32[]{:S(2)}) async-start(bf16[8,16,4096]{2,1,0:T(8,128)(2,1)} %bitcast.15), calls=%async_computation.1 | async-start | bytes 2097152 | tf_op jit(solution)/shard_map/combine/all_to_all | solution.py:133
  165.7 87.2 %reduce-scatter.2.cloned.1.call-start = ((), (), s32[]{:S(2)}) async-start(), calls=%async_computation.5 | async-start | bytes 7077888 | tf_op jit(solution)/shard_map/expert/reduce_scatter | solution.py:208
Sparse Core Ops, SparseCore 0:
  10.7 118.9 all-gather.1
  170.5 60.0 reduce-scatter.1
